TPU v7x, 128 devices: a whole 4x4x4 slice. The times are simulated.
128 devices in a mesh: seq: 8 (over x, core), node: 16 (over y, z).
Axes of the slice: x: 4, y: 4, z: 4, core: 2. Of those that a mesh axis runs over, the one named last changes fastest.
Arguments:
- queries: float32 [131072, 1024], P(('seq', 'node')), may hold values from -9 to 9
- keys: float32 [131072, 1024], P(('seq', 'node')), may hold values from -9 to 9
- values: float32 [131072, 1024], P(('seq', 'node')), may hold values from -6 to 6
Outputs:
- attended: float32 [131072, 1024], P(('seq', 'node'))
All inputs are finite; a program needn't handle non-finite values.
Results may differ from a plain program's by a relative error of at most 0.0003.
Values sent between devices are 32-bit elements; how exact they have to be, the bound alone decides.
No kernel may reach another device: no remote copies, remote signals or barrier semaphores. Data moves between devices by JAX's collectives and lax.ppermute only.
A program may use at most 192 MiB of HBM per device.

v0:
```python
import math

import jax
import jax.numpy as jnp
from jax import lax
from jax.sharding import PartitionSpec as P

HEADS = 8
CHANNEL_WIDTH = 128
SEGMENT_LENGTH = 128


NATURAL_LN_DUO = math.log(2.0)


def swapped(shard, axis, distance):
    return lax.ppermute(shard, axis, [(i, i ^ 1 << distance) for i in range(lax.axis_size(axis))])


def head_major(matrix):
    row_count = matrix.shape[0]
    return jnp.transpose(matrix.reshape(row_count, HEADS, CHANNEL_WIDTH), (1, 0, 2))


def pool_pairs(tensor):
    paired = tensor.reshape(tensor.shape[0], tensor.shape[1] // 2, 2, tensor.shape[2])
    return 0.5 * (paired[:, :, 0] + paired[:, :, 1])


def batched_attend(probe_blocks, lookup_blocks, payload_blocks, logit_offset):
    block_count = probe_blocks.shape[1]
    row_count = probe_blocks.shape[2]
    logit_grid = jnp.einsum(
        "hbrd,hbcd->hbrc", probe_blocks, lookup_blocks, precision=lax.Precision.HIGHEST
    )
    logit_grid = logit_grid * CHANNEL_WIDTH ** (-0.5) + logit_offset
    peak = jnp.max(logit_grid, axis=3)
    weights = jnp.exp(logit_grid - peak[:, :, :, None])
    weight_sum = jnp.sum(weights, axis=3)
    numerator = jnp.einsum(
        "hbrc,hbcd->hbrd", weights, payload_blocks, precision=lax.Precision.HIGHEST
    )
    total_rows = block_count * row_count
    return (
        peak.reshape(HEADS, total_rows),
        weight_sum.reshape(HEADS, total_rows),
        numerator.reshape(HEADS, total_rows, CHANNEL_WIDTH),
    )


def mix_sibling_segments(probe_entries, lookup_entries, payload_entries, logit_offset):
    return batched_attend(
        probe_entries[:, None], lookup_entries[:, None], payload_entries[:, None], logit_offset
    )


def level_rows(level_q, level_k, level_v, hierarchy_depth):
    row_count = level_q.shape[1]
    if hierarchy_depth == 0:
        shape = (HEADS, row_count // (2 * SEGMENT_LENGTH), 2 * SEGMENT_LENGTH, CHANNEL_WIDTH)
        return batched_attend(
            level_q.reshape(shape), level_k.reshape(shape), level_v.reshape(shape), 0.0
        )
    block_count = row_count // SEGMENT_LENGTH
    shape = (HEADS, block_count, SEGMENT_LENGTH, CHANNEL_WIDTH)
    pair_shape = (HEADS, block_count // 2, 2, SEGMENT_LENGTH, CHANNEL_WIDTH)
    sibling_k = jnp.flip(level_k.reshape(pair_shape), axis=2).reshape(shape)
    sibling_v = jnp.flip(level_v.reshape(pair_shape), axis=2).reshape(shape)
    return batched_attend(
        level_q.reshape(shape), sibling_k, sibling_v, hierarchy_depth * NATURAL_LN_DUO
    )


def combine_coarse(finer, coarse):
    fine_peak, fine_sum, fine_num = finer
    coarse_peak, coarse_sum, coarse_num = coarse
    fine_rows = fine_peak.shape[1]
    coarse_rows = coarse_peak.shape[1]
    factor = fine_rows // coarse_rows
    fine_peak = fine_peak.reshape(HEADS, coarse_rows, factor)
    fine_sum = fine_sum.reshape(HEADS, coarse_rows, factor)
    fine_num = fine_num.reshape(HEADS, coarse_rows, factor, CHANNEL_WIDTH)
    coarse_peak = coarse_peak[:, :, None]
    peak = jnp.maximum(fine_peak, coarse_peak)
    scale_fine = jnp.exp(fine_peak - peak)
    scale_coarse = jnp.exp(coarse_peak - peak)
    weight_sum = fine_sum * scale_fine + coarse_sum[:, :, None] * scale_coarse
    numerator = (
        fine_num * scale_fine[:, :, :, None]
        + coarse_num[:, :, None, :] * scale_coarse[:, :, :, None]
    )
    return (
        peak.reshape(HEADS, fine_rows),
        weight_sum.reshape(HEADS, fine_rows),
        numerator.reshape(HEADS, fine_rows, CHANNEL_WIDTH),
    )


def ascend_pair(own_rows, partner_rows, bit_value):
    joined = jnp.where(
        bit_value == 1,
        jnp.concatenate([partner_rows, own_rows], axis=1),
        jnp.concatenate([own_rows, partner_rows], axis=1),
    )
    return pool_pairs(joined)


def on_device(queries, keys, values):
    row_count = queries.shape[0]
    local_count = (row_count // SEGMENT_LENGTH).bit_length() - 1
    level_q = head_major(queries)
    level_k = head_major(keys)
    level_v = head_major(values)
    collected = [level_rows(level_q, level_k, level_v, 0)]
    for hierarchy_depth in range(1, local_count):
        level_q = pool_pairs(level_q)
        level_k = pool_pairs(level_k)
        level_v = pool_pairs(level_v)
        collected.append(level_rows(level_q, level_k, level_v, hierarchy_depth))
    own_q = pool_pairs(level_q)
    group_k = pool_pairs(level_k)
    group_v = pool_pairs(level_v)
    hierarchy_depth = local_count
    node_bits = lax.axis_size("node").bit_length() - 1
    seq_bits = lax.axis_size("seq").bit_length() - 1
    node_place = lax.axis_index("node")
    for bit_index in range(node_bits):
        partner_k, partner_v = swapped((group_k, group_v), "node", bit_index)
        collected.append(
            mix_sibling_segments(own_q, partner_k, partner_v, hierarchy_depth * NATURAL_LN_DUO)
        )
        bit_value = jnp.bitwise_and(jnp.right_shift(node_place, bit_index), 1)
        group_k = ascend_pair(group_k, partner_k, bit_value)
        group_v = ascend_pair(group_v, partner_v, bit_value)
        own_q = pool_pairs(own_q)
        hierarchy_depth = hierarchy_depth + 1
    seq_place = lax.axis_index("seq")
    for bit_index in range(seq_bits):
        partner_k, partner_v = swapped((group_k, group_v), "seq", bit_index)
        collected.append(
            mix_sibling_segments(own_q, partner_k, partner_v, hierarchy_depth * NATURAL_LN_DUO)
        )
        bit_value = jnp.bitwise_and(jnp.right_shift(seq_place, bit_index), 1)
        group_k = ascend_pair(group_k, partner_k, bit_value)
        group_v = ascend_pair(group_v, partner_v, bit_value)
        own_q = pool_pairs(own_q)
        hierarchy_depth = hierarchy_depth + 1
    running = collected[-1]
    for finer in reversed(collected[:-1]):
        running = combine_coarse(finer, running)
    peak, weight_sum, numerator = running
    result = numerator / weight_sum[:, :, None]
    return jnp.transpose(result, (1, 0, 2)).reshape(row_count, HEADS * CHANNEL_WIDTH)


def solution(mesh):
    return jax.shard_map(
        on_device,
        mesh=mesh,
        in_specs=(P(("seq", "node"), None), P(("seq", "node"), None), P(("seq", "node"), None)),
        out_specs=P(("seq", "node"), None),
        check_vma=False,
    )
```

profile of v0, /device:TPU:0, one launch (start us, length us, event | category | flops | bytes accessed | tf_op | source)
XLA Modules:
  0.0 249.8 jit_solution(6835307924463165445)
XLA Ops:
  0.0 3.2 %copy.581 = f32[128,8,8,128]{3,2,1,0:T(8,128)S(1)} copy(f32[128,8,8,128]{3,1,2,0:T(8,128)} %bitcast.238) | data formatting | bytes 8388608
  8.1 2.0 collective-permute-start.7
  16.7 3.2 %copy.579 = f32[128,8,8,128]{3,2,1,0:T(8,128)S(1)} copy(f32[128,8,8,128]{3,1,2,0:T(8,128)} %bitcast.240) | data formatting | bytes 8388608
  31.7 2.3 reverse.15
  38.7 2.3 reverse.13
  41.0 12.4 %multiply_reduce_fusion = (f32[8,4,256]{2,1,0:T(4,128)S(1)}, f32[8,4,256,256]{2,3,1,0:T(8,128)S(1)}) fusion(f32[8,4,256,128]{3,0,2,1:T(8,128)} %bitcast.219, f32[8,4,256,128]{3,0,2,1:T(8,128)} %bitcast.221), kind=kOutput, calls=%fused_computation.1 | convolution fusion | flops 3225411584 | bytes 16809984 | tf_op jit(solution)/shard_map/hbrd,hbcd->hbrc/dot_general | solution.py:33
  55.6 16.2 %fusion.1 = f32[8,4,256,128]{3,2,1,0:T(8,128)} fusion(f32[8,4,256,256]{2,3,1,0:T(8,128)S(1)} %get-tuple-element.81, f32[8,4,256,128]{3,0,2,1:T(8,128)S(1)} %bitcast.217, f32[8,4,256]{2,1,0:T(4,128)S(1)} %get-tuple-element.80), kind=kOutput, calls=%fused_computation.3 | convolution fusion | flops 3225419776 | bytes 16809984 | tf_op jit(solution)/shard_map/hbrc,hbcd->hbrd/dot_general | solution.py:40
  73.0 4.6 %fusion.14 = (f32[8,4,128]{2,1,0:T(4,128)S(1)}, f32[8,4,128,128]{2,3,1,0:T(8,128)S(1)}) fusion(f32[8,4,128,128]{3,2,1,0:T(8,128)S(1)} %bitcast.228, f32[8,4,128,128]{3,0,2,1:T(8,128)S(1)} %bitcast.223), kind=kOutput, calls=%fused_computation.26 | convolution fusion | flops 806875136 | bytes 6307840 | tf_op jit(solution)/shard_map/hbrd,hbcd->hbrc/dot_general | solution.py:33
  78.8 2.4 fusion.131
  81.2 2.9 %fusion.33 = f32[8,2,128,128]{3,2,1,0:T(8,128)} fusion(f32[8,1,2,128,128]{4,3,2,0,1:T(8,128)S(1)} %copy-done.10, f32[8,2,128,128]{2,3,1,0:T(8,128)S(1)} %get-tuple-element.85, f32[8,2,128]{2,1,0:T(2,128)S(1)} %get-tuple-element.84), kind=kOutput, calls=%fused_computation.75 | convolution fusion | flops 403177472 | bytes 3153920 | tf_op jit(solution)/shard_map/hbrc,hbcd->hbrd/dot_general | solution.py:40
  84.9 3.8 %fusion.16 = f32[8,4,128,128]{3,2,1,0:T(8,128)S(1)} fusion(f32[8,4,128,128]{3,2,1,0:T(8,128)S(1)} %bitcast.227, f32[8,4,128,128]{2,3,1,0:T(8,128)S(1)} %get-tuple-element.83, f32[8,4,128]{2,1,0:T(4,128)S(1)} %get-tuple-element.82), kind=kOutput, calls=%fused_computation.28 | convolution fusion | flops 806879232 | bytes 6307840 | tf_op jit(solution)/shard_map/hbrc,hbcd->hbrd/dot_general | solution.py:40
  88.7 2.5 %maximum_select_fusion = (f32[8,256,128]{2,1,0:T(8,128)S(1)}, f32[8,256,128]{2,1,0:T(8,128)S(1)}) fusion(f32[8,128,128]{2,1,0:T(8,128)} %fusion.66, f32[8,128,128]{2,1,0:T(8,128)} %collective-permute-done, pred[]{:T(512)S(6)} %eq.24, f32[8,128,128]{2,1,0:T(8,128)} %collective-permute-done.7, f32[8,128,128]{2,1,0:T(8,128)} %fusion.56), kind=kLoop, calls=%fused_computation.61 | loop fusion | flops 1572864 | bytes 4194305 | tf_op jit(solution)/shard_map/jit(_where)/select_n | solution.py:100
  92.5 3.7 %collective-permute-start.1 = (f32[8,128,128]{2,1,0:T(8,128)S(1)}, f32[8,128,128]{2,1,0:T(8,128)S(1)}, u32[]{:S(2)}, u32[]{:S(2)}) collective-permute-start(f32[8,128,128]{2,1,0:T(8,128)S(1)} %multiply_bitcast_fusion.1), channel_id=1, source_target_pairs={{0,2},{1,3},{2,0},{3,1},{4,6},{5,7},{6,4},{7,5},{8,10},{9,11},{10,... | collective-permute-start | bytes 1572872 | tf_op jit(solution)/shard_map/ppermute | solution.py:17
  97.8 2.3 fusion.138
  100.8 8.2 %collective-permute-done.1 = f32[8,128,128]{2,1,0:T(8,128)S(1)} collective-permute-done((f32[8,128,128]{2,1,0:T(8,128)S(1)}, f32[8,128,128]{2,1,0:T(8,128)S(1)}, u32[]{:S(2)}, u32[]{:S(2)}) %collective-permute-start.1) | collective-permute-done | bytes 524320 | tf_op jit(solution)/shard_map/ppermute | solution.py:17
  111.7 7.4 %collective-permute-done.8 = f32[8,128,128]{2,1,0:T(8,128)S(1)} collective-permute-done((f32[8,128,128]{2,1,0:T(8,128)S(1)}, f32[8,128,128]{2,1,0:T(8,128)S(1)}, u32[]{:S(2)}, u32[]{:S(2)}) %collective-permute-start.8) | collective-permute-done | bytes 524320 | tf_op jit(solution)/shard_map/ppermute | solution.py:17
  124.9 3.0 %collective-permute-start.3 = (f32[8,128,128]{2,1,0:T(8,128)S(1)}, f32[8,128,128]{2,1,0:T(8,128)S(1)}, u32[]{:S(2)}, u32[]{:S(2)}) collective-permute-start(f32[8,128,128]{2,1,0:T(8,128)S(1)} %fusion.62), channel_id=1, source_target_pairs={{0,8},{1,9},{2,10},{3,11},{4,12},{5,13},{6,14},{7,15},{8,0},{9,1},... | collective-permute-start | bytes 1572872 | tf_op jit(solution)/shard_map/ppermute | solution.py:17
  127.9 7.1 %collective-permute-done.9 = f32[8,128,128]{2,1,0:T(8,128)S(1)} collective-permute-done((f32[8,128,128]{2,1,0:T(8,128)S(1)}, f32[8,128,128]{2,1,0:T(8,128)S(1)}, u32[]{:S(2)}, u32[]{:S(2)}) %collective-permute-start.9) | collective-permute-done | bytes 524320 | tf_op jit(solution)/shard_map/ppermute | solution.py:17
  136.1 3.3 %collective-permute-start.10 = (f32[8,128,128]{2,1,0:T(8,128)S(1)}, f32[8,128,128]{2,1,0:T(8,128)S(1)}, u32[]{:S(2)}, u32[]{:S(2)}) collective-permute-start(f32[8,128,128]{2,1,0:T(8,128)S(1)} %fusion.50), channel_id=1, source_target_pairs={{0,8},{1,9},{2,10},{3,11},{4,12},{5,13},{6,14},{7,15},{8,0},{9,1},... | collective-permute-start | bytes 1572872 | tf_op jit(solution)/shard_map/ppermute | solution.py:17
  141.2 7.5 %collective-permute-done.3 = f32[8,128,128]{2,1,0:T(8,128)S(1)} collective-permute-done((f32[8,128,128]{2,1,0:T(8,128)S(1)}, f32[8,128,128]{2,1,0:T(8,128)S(1)}, u32[]{:S(2)}, u32[]{:S(2)}) %collective-permute-start.3) | collective-permute-done | bytes 524320 | tf_op jit(solution)/shard_map/ppermute | solution.py:17
  150.1 7.8 %collective-permute-done.10 = f32[8,128,128]{2,1,0:T(8,128)S(1)} collective-permute-done((f32[8,128,128]{2,1,0:T(8,128)S(1)}, f32[8,128,128]{2,1,0:T(8,128)S(1)}, u32[]{:S(2)}, u32[]{:S(2)}) %collective-permute-start.10) | collective-permute-done | bytes 524320 | tf_op jit(solution)/shard_map/ppermute | solution.py:17
  167.5 9.8 %collective-permute-done.5 = f32[8,128,128]{2,1,0:T(8,128)S(1)} collective-permute-done((f32[8,128,128]{2,1,0:T(8,128)S(1)}, f32[8,128,128]{2,1,0:T(8,128)S(1)}, u32[]{:S(2)}, u32[]{:S(2)}) %collective-permute-start.5) | collective-permute-done | bytes 524320 | tf_op jit(solution)/shard_map/ppermute | solution.py:17
  178.5 3.1 %collective-permute-start.6 = (f32[8,128,128]{2,1,0:T(8,128)S(1)}, f32[8,128,128]{2,1,0:T(8,128)S(1)}, u32[]{:S(2)}, u32[]{:S(2)}) collective-permute-start(f32[8,128,128]{2,1,0:T(8,128)S(1)} %multiply_bitcast_fusion), channel_id=1, source_target_pairs={{0,64},{16,80},{32,96},{48,112},{64,0},{80,16},{96,32},{112,48},{1... | collective-permute-start | bytes 1572872 | tf_op jit(solution)/shard_map/ppermute | solution.py:17
  181.6 6.9 %collective-permute-done.12 = f32[8,128,128]{2,1,0:T(8,128)S(1)} collective-permute-done((f32[8,128,128]{2,1,0:T(8,128)S(1)}, f32[8,128,128]{2,1,0:T(8,128)S(1)}, u32[]{:S(2)}, u32[]{:S(2)}) %collective-permute-start.12) | collective-permute-done | bytes 524320 | tf_op jit(solution)/shard_map/ppermute | solution.py:17
  190.4 3.2 %collective-permute-start.13 = (f32[8,128,128]{2,1,0:T(8,128)}, f32[8,128,128]{2,1,0:T(8,128)}, u32[]{:S(2)}, u32[]{:S(2)}) collective-permute-start(f32[8,128,128]{2,1,0:T(8,128)} %fusion.44), channel_id=1, source_target_pairs={{0,64},{16,80},{32,96},{48,112},{64,0},{80,16},{96,32},{112,48},{1... | collective-permute-start | bytes 1572872 | tf_op jit(solution)/shard_map/ppermute | solution.py:17
  195.4 6.5 %collective-permute-done.6 = f32[8,128,128]{2,1,0:T(8,128)S(1)} collective-permute-done((f32[8,128,128]{2,1,0:T(8,128)S(1)}, f32[8,128,128]{2,1,0:T(8,128)S(1)}, u32[]{:S(2)}, u32[]{:S(2)}) %collective-permute-start.6) | collective-permute-done | bytes 524320 | tf_op jit(solution)/shard_map/ppermute | solution.py:17
  220.2 2.0 max.237
  232.5 2.3 fusion.18
  236.6 2.6 %fusion.11 = f32[8,512,128]{2,1,0:T(8,128)} fusion(f32[8,4,128,128]{3,2,1,0:T(8,128)S(1)} %fusion.16, f32[8,512,128]{2,1,0:T(8,128)S(1)} %bitcast.229, f32[8,512]{1,0:T(8,128)S(1)} %copy-done.49, f32[8,512]{1,0:T(8,128)S(1)} %copy-done.48), kind=kLoop, calls=%fused_computation.19 | loop fusion | flops 1572864 | bytes 6324224 | tf_op jit(solution)/shard_map/add | solution.py:89
  239.3 3.2 %mul.879 = f32[8,512,2,128]{3,2,1,0:T(2,128)S(1)} broadcast(f32[8,512,128]{2,1,0:T(8,128)} %fusion.11), dimensions={0,1,3} | broadcast | bytes 6291456 | tf_op jit(solution)/shard_map/mul | solution.py:90
  242.5 4.2 %fusion.3 = f32[8,1024,128]{2,1,0:T(8,128)S(1)} fusion(f32[8,4,256,128]{3,2,1,0:T(8,128)S(1)} %copy-done.4, f32[8,1024,128]{2,1,0:T(8,128)S(1)} %bitcast.224, f32[8,1024]{1,0:T(8,128)S(1)} %get-tuple-element.5, f32[8,1024]{1,0:T(8,128)S(1)} %get-tuple-element.7, f32[8,1024]{1,0:T(8,128)S(1)} %get-tuple-element.6), kind=kLoop, calls=%fused_computation.7 | loop fusion | flops 4194304 | bytes 12681216 | tf_op jit(solution)/shard_map/div | solution.py:152
  246.7 2.6 %copy_bitcast_fusion = f32[1024,1024]{1,0:T(8,128)} fusion(f32[8,1024,128]{2,1,0:T(8,128)S(1)} %fusion.3), kind=kLoop, calls=%fused_computation.4 | loop fusion | bytes 8388608 | tf_op jit(solution)/shard_map/reshape | solution.py:153
  (305 shorter events, 93.7 us)
Async XLA Ops:
  8.1 80.7 %collective-permute-start.7 = (f32[8,128,128]{2,1,0:T(8,128)}, f32[8,128,128]{2,1,0:T(8,128)}, u32[]{:S(2)}, u32[]{:S(2)}) collective-permute-start(f32[8,128,128]{2,1,0:T(8,128)} %fusion.56), channel_id=1, source_target_pairs={{0,1},{1,0},{2,3},{3,2},{4,5},{5,4},{6,7},{7,6},{8,9},{9,8},{10,11... | collective-permute-start | bytes 1572872 | tf_op jit(solution)/shard_map/ppermute | solution.py:17
  15.9 72.8 %collective-permute-start = (f32[8,128,128]{2,1,0:T(8,128)}, f32[8,128,128]{2,1,0:T(8,128)}, u32[]{:S(2)}, u32[]{:S(2)}) collective-permute-start(f32[8,128,128]{2,1,0:T(8,128)} %fusion.66), channel_id=1, source_target_pairs={{0,1},{1,0},{2,3},{3,2},{4,5},{5,4},{6,7},{7,6},{8,9},{9,8},{10,11... | collective-permute-start | bytes 1572872 | tf_op jit(solution)/shard_map/ppermute | solution.py:17
  55.6 17.4 %copy-start.6 = (f32[8,2,2,128,128]{4,3,2,1,0:T(8,128)S(1)}, f32[8,2,2,128,128]{4,3,2,1,0:T(8,128)}, u32[]{:S(2)}) copy-start(f32[8,2,2,128,128]{4,3,2,1,0:T(8,128)} %copy.439) | copy-start | bytes 6291460
  92.5 16.5 %collective-permute-start.1 = (f32[8,128,128]{2,1,0:T(8,128)S(1)}, f32[8,128,128]{2,1,0:T(8,128)S(1)}, u32[]{:S(2)}, u32[]{:S(2)}) collective-permute-start(f32[8,128,128]{2,1,0:T(8,128)S(1)} %multiply_bitcast_fusion.1), channel_id=1, source_target_pairs={{0,2},{1,3},{2,0},{3,1},{4,6},{5,7},{6,4},{7,5},{8,10},{9,11},{10,... | collective-permute-start | bytes 1572872 | tf_op jit(solution)/shard_map/ppermute | solution.py:17
  97.1 22.0 %collective-permute-start.8 = (f32[8,128,128]{2,1,0:T(8,128)S(1)}, f32[8,128,128]{2,1,0:T(8,128)S(1)}, u32[]{:S(2)}, u32[]{:S(2)}) collective-permute-start(f32[8,128,128]{2,1,0:T(8,128)S(1)} %fusion.54), channel_id=1, source_target_pairs={{0,2},{1,3},{2,0},{3,1},{4,6},{5,7},{6,4},{7,5},{8,10},{9,11},{10,... | collective-permute-start | bytes 1572872 | tf_op jit(solution)/shard_map/ppermute | solution.py:17
  100.1 9.6 %copy-start.35 = (f32[8,128]{1,0:T(8,128)}, f32[8,128]{1,0:T(8,128)S(1)}, u32[]{:S(2)}) copy-start(f32[8,128]{1,0:T(8,128)S(1)} %get-tuple-element.98) | copy-start | bytes 12292
  110.0 13.9 %collective-permute-start.2 = (f32[8,128,128]{2,1,0:T(8,128)S(1)}, f32[8,128,128]{2,1,0:T(8,128)S(1)}, u32[]{:S(2)}, u32[]{:S(2)}) collective-permute-start(f32[8,128,128]{2,1,0:T(8,128)S(1)} %fusion.64), channel_id=1, source_target_pairs={{0,4},{1,5},{2,6},{3,7},{4,0},{5,1},{6,2},{7,3},{8,12},{9,13},{10,... | collective-permute-start | bytes 1572872 | tf_op jit(solution)/shard_map/ppermute | solution.py:17
  120.1 14.9 %collective-permute-start.9 = (f32[8,128,128]{2,1,0:T(8,128)S(1)}, f32[8,128,128]{2,1,0:T(8,128)S(1)}, u32[]{:S(2)}, u32[]{:S(2)}) collective-permute-start(f32[8,128,128]{2,1,0:T(8,128)S(1)} %fusion.52), channel_id=1, source_target_pairs={{0,4},{1,5},{2,6},{3,7},{4,0},{5,1},{6,2},{7,3},{8,12},{9,13},{10,... | collective-permute-start | bytes 1572872 | tf_op jit(solution)/shard_map/ppermute | solution.py:17
  124.9 23.8 %collective-permute-start.3 = (f32[8,128,128]{2,1,0:T(8,128)S(1)}, f32[8,128,128]{2,1,0:T(8,128)S(1)}, u32[]{:S(2)}, u32[]{:S(2)}) collective-permute-start(f32[8,128,128]{2,1,0:T(8,128)S(1)} %fusion.62), channel_id=1, source_target_pairs={{0,8},{1,9},{2,10},{3,11},{4,12},{5,13},{6,14},{7,15},{8,0},{9,1},... | collective-permute-start | bytes 1572872 | tf_op jit(solution)/shard_map/ppermute | solution.py:17
  136.1 21.8 %collective-permute-start.10 = (f32[8,128,128]{2,1,0:T(8,128)S(1)}, f32[8,128,128]{2,1,0:T(8,128)S(1)}, u32[]{:S(2)}, u32[]{:S(2)}) collective-permute-start(f32[8,128,128]{2,1,0:T(8,128)S(1)} %fusion.50), channel_id=1, source_target_pairs={{0,8},{1,9},{2,10},{3,11},{4,12},{5,13},{6,14},{7,15},{8,0},{9,1},... | collective-permute-start | bytes 1572872 | tf_op jit(solution)/shard_map/ppermute | solution.py:17
  140.4 9.1 %copy-start.40 = (f32[8,32]{1,0:T(8,128)}, f32[8,32]{1,0:T(8,128)S(1)}, u32[]{:S(2)}) copy-start(f32[8,32]{1,0:T(8,128)S(1)} %get-tuple-element.94) | copy-start | bytes 3076
  149.8 11.5 %collective-permute-start.4 = (f32[8,128,128]{2,1,0:T(8,128)S(1)}, f32[8,128,128]{2,1,0:T(8,128)S(1)}, u32[]{:S(2)}, u32[]{:S(2)}) collective-permute-start(f32[8,128,128]{2,1,0:T(8,128)S(1)} %fusion.60), channel_id=1, source_target_pairs={{0,16},{16,0},{32,48},{48,32},{64,80},{80,64},{96,112},{112,96},{1... | collective-permute-start | bytes 1572872 | tf_op jit(solution)/shard_map/ppermute | solution.py:17
  159.0 5.0 %collective-permute-start.11 = (f32[8,128,128]{2,1,0:T(8,128)S(1)}, f32[8,128,128]{2,1,0:T(8,128)S(1)}, u32[]{:S(2)}, u32[]{:S(2)}) collective-permute-start(f32[8,128,128]{2,1,0:T(8,128)S(1)} %fusion.48), channel_id=1, source_target_pairs={{0,16},{16,0},{32,48},{48,32},{64,80},{80,64},{96,112},{112,96},{1... | collective-permute-start | bytes 1572872 | tf_op jit(solution)/shard_map/ppermute | solution.py:17
  162.4 14.9 %collective-permute-start.5 = (f32[8,128,128]{2,1,0:T(8,128)S(1)}, f32[8,128,128]{2,1,0:T(8,128)S(1)}, u32[]{:S(2)}, u32[]{:S(2)}) collective-permute-start(f32[8,128,128]{2,1,0:T(8,128)S(1)} %fusion.58), channel_id=1, source_target_pairs={{0,32},{16,48},{32,0},{48,16},{64,96},{80,112},{96,64},{112,80},{1... | collective-permute-start | bytes 1572872 | tf_op jit(solution)/shard_map/ppermute | solution.py:17
  165.1 23.5 %collective-permute-start.12 = (f32[8,128,128]{2,1,0:T(8,128)S(1)}, f32[8,128,128]{2,1,0:T(8,128)S(1)}, u32[]{:S(2)}, u32[]{:S(2)}) collective-permute-start(f32[8,128,128]{2,1,0:T(8,128)S(1)} %fusion.46), channel_id=1, source_target_pairs={{0,32},{16,48},{32,0},{48,16},{64,96},{80,112},{96,64},{112,80},{1... | collective-permute-start | bytes 1572872 | tf_op jit(solution)/shard_map/ppermute | solution.py:17
  166.7 11.8 %copy-start.25 = (f32[8,8,128]{2,1,0:T(8,128)}, f32[8,8,128]{2,1,0:T(8,128)S(1)}, u32[]{:S(2)}) copy-start(f32[8,8,128]{2,1,0:T(8,128)S(1)} %get-tuple-element.91) | copy-start | bytes 98308
  166.7 11.8 %copy-start.44 = (f32[8,8]{1,0:T(8,128)}, f32[8,8]{1,0:T(8,128)S(1)}, u32[]{:S(2)}) copy-start(f32[8,8]{1,0:T(8,128)S(1)} %get-tuple-element.90) | copy-start | bytes 772
  178.5 23.4 %collective-permute-start.6 = (f32[8,128,128]{2,1,0:T(8,128)S(1)}, f32[8,128,128]{2,1,0:T(8,128)S(1)}, u32[]{:S(2)}, u32[]{:S(2)}) collective-permute-start(f32[8,128,128]{2,1,0:T(8,128)S(1)} %multiply_bitcast_fusion), channel_id=1, source_target_pairs={{0,64},{16,80},{32,96},{48,112},{64,0},{80,16},{96,32},{112,48},{1... | collective-permute-start | bytes 1572872 | tf_op jit(solution)/shard_map/ppermute | solution.py:17
  189.3 12.6 %copy-start.51 = (f32[8,2,128]{2,0,1:T(8,128)S(1)}, f32[8,2,128]{2,0,1:T(8,128)}, u32[]{:S(2)}) copy-start(f32[8,2,128]{2,0,1:T(8,128)} %fusion.100) | copy-start | bytes 24580
  190.4 33.7 %collective-permute-start.13 = (f32[8,128,128]{2,1,0:T(8,128)}, f32[8,128,128]{2,1,0:T(8,128)}, u32[]{:S(2)}, u32[]{:S(2)}) collective-permute-start(f32[8,128,128]{2,1,0:T(8,128)} %fusion.44), channel_id=1, source_target_pairs={{0,64},{16,80},{32,96},{48,112},{64,0},{80,16},{96,32},{112,48},{1... | collective-permute-start | bytes 1572872 | tf_op jit(solution)/shard_map/ppermute | solution.py:17
  194.6 8.3 %copy-start.27 = (f32[8,4,128]{2,1,0:T(4,128)}, f32[8,4,128]{2,1,0:T(4,128)S(1)}, u32[]{:S(2)}) copy-start(f32[8,4,128]{2,1,0:T(4,128)S(1)} %get-tuple-element.89) | copy-start | bytes 49156
  194.6 8.3 %copy-start.46 = (f32[8,4]{1,0:T(8,128)}, f32[8,4]{1,0:T(8,128)S(1)}, u32[]{:S(2)}) copy-start(f32[8,4]{1,0:T(8,128)S(1)} %get-tuple-element.88) | copy-start | bytes 388
  201.9 13.4 %copy-start.47 = (f32[8,4,128]{2,1,0:T(4,128)S(1)}, f32[8,4,128]{2,1,0:T(4,128)}, u32[]{:S(2)}) copy-start(f32[8,4,128]{2,1,0:T(4,128)} %fusion.15) | copy-start | bytes 49156
  216.8 10.7 %copy-start.45 = (f32[8,8]{1,0:T(8,128)S(1)}, f32[8,8]{1,0:T(8,128)}, u32[]{:S(2)}) copy-start(f32[8,8]{1,0:T(8,128)} %copy-done.44) | copy-start | bytes 772
  216.8 10.7 %copy-start.54 = (f32[8,8]{1,0:T(8,128)S(1)}, f32[8,8]{1,0:T(8,128)}, u32[]{:S(2)}) copy-start(f32[8,8]{1,0:T(8,128)} %get-tuple-element.31) | copy-start | bytes 772
  217.9 11.3 %copy-start.43 = (f32[8,16]{1,0:T(8,128)S(1)}, f32[8,16]{1,0:T(8,128)}, u32[]{:S(2)}) copy-start(f32[8,16]{1,0:T(8,128)} %copy-done.42) | copy-start | bytes 1540
  220.2 10.5 %copy-start.16 = (f32[8,128,128]{2,1,0:T(8,128)S(1)}, f32[8,128,128]{2,1,0:T(8,128)}, u32[]{:S(2)}) copy-start(f32[8,128,128]{2,1,0:T(8,128)} %copy-done.15) | copy-start | bytes 1572868
  220.2 10.5 %copy-start.41 = (f32[8,32]{1,0:T(8,128)S(1)}, f32[8,32]{1,0:T(8,128)}, u32[]{:S(2)}) copy-start(f32[8,32]{1,0:T(8,128)} %copy-done.40) | copy-start | bytes 3076
  224.0 7.5 %copy-start.18 = (f32[8,128,128]{2,1,0:T(8,128)S(1)}, f32[8,128,128]{2,1,0:T(8,128)}, u32[]{:S(2)}) copy-start(f32[8,128,128]{2,1,0:T(8,128)} %copy-done.17) | copy-start | bytes 1572868
  224.0 7.5 %copy-start.38 = (f32[8,64]{1,0:T(8,128)S(1)}, f32[8,64]{1,0:T(8,128)}, u32[]{:S(2)}) copy-start(f32[8,64]{1,0:T(8,128)} %copy-done.37) | copy-start | bytes 6148
  224.1 7.5 %copy-start.57 = (f32[8,64]{1,0:T(8,128)S(1)}, f32[8,64]{1,0:T(8,128)}, u32[]{:S(2)}) copy-start(f32[8,64]{1,0:T(8,128)} %get-tuple-element.19) | copy-start | bytes 6148
  224.1 7.5 %copy-start.58 = (f32[8,64]{1,0:T(8,128)S(1)}, f32[8,64]{1,0:T(8,128)}, u32[]{:S(2)}) copy-start(f32[8,64]{1,0:T(8,128)} %get-tuple-element.20) | copy-start | bytes 6148
  (43 other events, 114.5 us)
where the time goes:
time: 254 us; the launch traced here: 250 us
  waiting for transfers between devices  61.3 us (24%)
  matrix products  60.7 us (24%)
  local copies, waits for them, and re-layouts  53.5 us (21%)
  other arithmetic  47.6 us (19%)
  starting transfers between devices  25 us (10%)
    ppermute x14, waiting for transfers between devices, swapped(): lax.ppermute(shard, axis, [(i, i ^ 1 << distance) for i in range(lax.axis...  61.3 us
    dot_general x10, matrix products, batched_attend(): jnp.einsum('hbrc,hbcd->hbrd', weights, payload_blocks, precision=lax.Prec...  33 us
    dot_general x10, matrix products, batched_attend(): jnp.einsum('hbrd,hbcd->hbrc', probe_blocks, lookup_blocks, precision=lax....  27.8 us
    ppermute x14, starting transfers between devices, swapped(): lax.ppermute(shard, axis, [(i, i ^ 1 << distance) for i in range(lax.axis...  25 us
    unnamed x127, local copies, waits for them, and re-layouts  15.1 us
    mul x31, other arithmetic, pool_pairs(): return 0.5 * (paired[:, :, 0] + paired[:, :, 1])  14.6 us
    add x9, other arithmetic, combine_coarse(): weight_sum = fine_sum * scale_fine + coarse_sum[:, :, None] * scale_coarse  9.8 us
    reduce_sum x10, other arithmetic, batched_attend(): weight_sum = jnp.sum(weights, axis=3)  8.24 us
  transfers between devices with their start and end apart: 14, of which 8 were waited for; matrix products, arithmetic and copies ran while one was open for 48% of the time, Pallas kernels for 0%

commit v1 on v0

v1 whole, which is shorter than its diff:
```python
import functools
import math

import jax
import jax.numpy as jnp
from jax import lax
from jax.experimental import pallas as pl
from jax.experimental.pallas import tpu as pltpu
from jax.sharding import PartitionSpec as P

HEADS = 8
WIDTH = 128
ROWS = 1024
F32 = jnp.float32
BF16 = jnp.bfloat16
SCALE = WIDTH ** (-0.5) / math.log(2.0)
VMEM_LIMIT = 48 * 1024 * 1024

GROUPS = [list(range(8)), [12, 13, 14, 15, 8, 9, 10, 11]]


def params():
    return pltpu.CompilerParams(vmem_limit_bytes=VMEM_LIMIT)


def split(x):
    hi = x.astype(BF16)
    lo = (x - hi.astype(F32)).astype(BF16)
    return hi, lo


def dot_nt(a, b):
    return lax.dot_general(a, b, (((1,), (1,)), ((), ())), preferred_element_type=F32)


def dot_nn(a, b):
    return lax.dot_general(a, b, (((1,), (0,)), ((), ())), preferred_element_type=F32)


def key_side(k):
    hi, lo = split(k)
    return jnp.concatenate([hi, hi], axis=1), jnp.concatenate([lo, jnp.zeros_like(lo)], axis=1)


def scores(q, sides):
    hi, lo = split(q)
    both = jnp.concatenate([hi, lo], axis=1)
    first, second = sides
    n = first.shape[0]
    if n == 128:
        s = dot_nt(both, jnp.concatenate([first, second], axis=0))
        return s[:, :n] + s[:, n:]
    return dot_nt(both, first) + dot_nt(both, second)


def value_side(v):
    hi, lo = split(v)
    return hi, lo


def weigh(p, side):
    hi, lo = side
    p_hi, p_lo = split(p)
    if hi.shape[0] == 128:
        left = jnp.concatenate([p_hi, p_lo], axis=1)
        right = jnp.concatenate(
            [jnp.concatenate([hi, lo], axis=1), jnp.concatenate([hi, jnp.zeros_like(lo)], axis=1)], axis=0
        )
        r = dot_nn(left, right)
        return r[:, :WIDTH] + r[:, WIDTH:]
    r = dot_nn(p_hi, jnp.concatenate([hi, lo], axis=1))
    return r[:, :WIDTH] + r[:, WIDTH:] + dot_nn(p_lo, hi)


def attend(q, k_side, v_side, level):
    s = scores(q, k_side)
    peak = jnp.max(s, axis=1, keepdims=True)
    p = jnp.exp2(s - peak)
    total = jnp.sum(p, axis=1, keepdims=True)
    return peak + float(level), total, weigh(p, v_side)


def merge(a, b):
    ma, sa, na = a
    mb, sb, nb = b
    gap = ma - mb
    small = jnp.exp2(-jnp.abs(gap))
    fa = jnp.where(gap >= 0, 1.0, small)
    fb = jnp.where(gap >= 0, small, 1.0)
    return jnp.maximum(ma, mb), sa * fa + sb * fb, na * fa + nb * fb


def pool_body(q_ref, k_ref, v_ref, q3_ref, kv3_ref, kv4_ref, pay_ref, scratch):
    def level3(ref):
        total = ref[pl.ds(0, 128, stride=8), :]
        for k in range(1, 8):
            total = total + ref[pl.ds(k, 128, stride=8), :]
        return total * 0.125

    def halve(ref, n):
        return 0.5 * (ref[pl.ds(0, n, stride=2), :] + ref[pl.ds(1, n, stride=2), :])

    q3 = level3(q_ref) * SCALE
    k3 = level3(k_ref)
    v3 = level3(v_ref)
    q3_ref[...] = q3
    kv3_ref[0] = k3
    kv3_ref[1] = v3
    for i, x in enumerate((q3, k3, v3)):
        scratch[i, 0:128, :] = x
        x4 = halve(scratch.at[i, 0:128], 64)
        scratch[i, 128:192, :] = x4
        if i > 0:
            kv4_ref[i - 1] = x4
        pay_ref[0, 32 * i : 32 * i + 32, :] = halve(scratch.at[i, 128:192], 32)


def pool_call(q, k, v):
    block = pl.BlockSpec((ROWS, WIDTH), lambda h: (0, h))
    return pl.pallas_call(
        pool_body,
        name="pool_rows",
        grid=(HEADS,),
        in_specs=[block] * 3,
        out_specs=[
            pl.BlockSpec((128, WIDTH), lambda h: (0, h)),
            pl.BlockSpec((2, 128, WIDTH), lambda h: (0, 0, h)),
            pl.BlockSpec((2, 64, WIDTH), lambda h: (0, 0, h)),
            pl.BlockSpec((1, 96, WIDTH), lambda h: (h, 0, 0)),
        ],
        out_shape=[
            jax.ShapeDtypeStruct((128, HEADS * WIDTH), F32),
            jax.ShapeDtypeStruct((2, 128, HEADS * WIDTH), F32),
            jax.ShapeDtypeStruct((2, 64, HEADS * WIDTH), F32),
            jax.ShapeDtypeStruct((HEADS, 96, WIDTH), F32),
        ],
        scratch_shapes=[pltpu.VMEM((3, 192, WIDTH), F32)],
        compiler_params=params(),
        cost_estimate=pl.CostEstimate(flops=3 << 20, bytes_accessed=14 << 20, transcendentals=0),
    )(q, k, v)


def local_body(q_ref, k_ref, v_ref, o_ref, lse_ref):
    head = pl.program_id(0)

    def load(ref):
        return [ref[pl.ds(k, 128, stride=8), :] for k in range(8)]

    def pool(parts):
        return [0.5 * (parts[2 * i] + parts[2 * i + 1]) for i in range(len(parts) // 2)]

    def rows(parts, first, count):
        return jnp.concatenate([x[first : first + count] for x in parts], axis=0)

    q0 = [x * SCALE for x in load(q_ref)]
    k0, v0 = load(k_ref), load(v_ref)
    q1, k1, v1 = pool(q0), pool(k0), pool(v0)
    q2, k2, v2 = pool(q1), pool(k1), pool(v1)

    at2 = []
    for b in range(2):
        c = b ^ 1
        at2.append(attend(rows(q2, 64 * b, 64), key_side(rows(k2, 64 * c, 64)), value_side(rows(v2, 64 * c, 64)), 2))

    lane = lax.broadcasted_iota(jnp.int32, (128, WIDTH), 1)
    lses = [[None] * 4 for _ in range(8)]
    for p in range(4):
        c = p ^ 1
        m1, s1, n1 = attend(
            rows(q1, 32 * p, 32), key_side(rows(k1, 32 * c, 32)), value_side(rows(v1, 32 * c, 32)), 1
        )
        m0, s0, n0 = attend(
            rows(q0, 32 * p, 32), key_side(rows(k0, 32 * p, 32)), value_side(rows(v0, 32 * p, 32)), 0
        )
        off = 32 * (p % 2)
        for j in range(4):
            i = j // 2
            one = tuple(x[32 * j : 32 * j + 32] for x in (m1, s1, n1))
            two = tuple(x[64 * i + off : 64 * i + off + 32] for x in at2[p // 2])
            coarse = merge(one, two)
            for k in (2 * j, 2 * j + 1):
                zero = tuple(x[32 * k : 32 * k + 32] for x in (m0, s0, n0))
                m, s, n = merge(zero, coarse)
                o_ref[128 * k + 32 * p : 128 * k + 32 * p + 32, :] = n / s
                lses[k][p] = m + jnp.log2(s)
    for k in range(8):
        old = lse_ref[128 * k : 128 * k + 128, :]
        lse_ref[128 * k : 128 * k + 128, :] = jnp.where(lane == head, jnp.concatenate(lses[k], axis=0), old)


def local_call(q, k, v):
    block = pl.BlockSpec((ROWS, WIDTH), lambda h: (0, h))
    return pl.pallas_call(
        local_body,
        name="local_levels",
        grid=(HEADS,),
        in_specs=[block] * 3,
        out_specs=[block, pl.BlockSpec((ROWS, WIDTH), lambda h: (0, 0))],
        out_shape=[
            jax.ShapeDtypeStruct((ROWS, HEADS * WIDTH), F32),
            jax.ShapeDtypeStruct((ROWS, WIDTH), F32),
        ],
        compiler_params=params(),
        cost_estimate=pl.CostEstimate(flops=4 << 30, bytes_accessed=16 << 20, transcendentals=3 << 20),
    )(q, k, v)


def near_body(q3_ref, kv3_ref, kv4a_ref, kv4b_ref, o_ref, lse_ref, scratch, *, step):
    group = pl.program_id(0)
    lane = lax.broadcasted_iota(jnp.int32, (128, WIDTH), 1)
    packed = lse_ref[...]
    for h in range(step):
        cols = slice(WIDTH * h, WIDTH * h + WIDTH)
        scratch[h, 0, :, :] = q3_ref[:, cols]
        q4 = 0.5 * (scratch[h, 0, pl.ds(0, 64, stride=2), :] + scratch[h, 0, pl.ds(1, 64, stride=2), :])
        k4 = jnp.concatenate([kv4a_ref[0, :, cols], kv4b_ref[0, :, cols]], axis=0)
        v4 = jnp.concatenate([kv4a_ref[1, :, cols], kv4b_ref[1, :, cols]], axis=0)
        m4, s4, n4 = attend(q4, key_side(k4), value_side(v4), 4)
        for i, x in enumerate((m4, s4, n4)):
            x = jnp.broadcast_to(x, (64, WIDTH))
            scratch[h, i + 1, pl.ds(0, 64, stride=2), :] = x
            scratch[h, i + 1, pl.ds(1, 64, stride=2), :] = x
        three = attend(q3_ref[:, cols], key_side(kv3_ref[0, :, cols]), value_side(kv3_ref[1, :, cols]), 3)
        m, s, n = merge(three, (scratch[h, 1], scratch[h, 2], scratch[h, 3]))
        o_ref[:, cols] = n / s
        packed = jnp.where(lane == group * step + h, m + jnp.log2(s), packed)
    lse_ref[...] = packed


def near_call(q3, kv3, kv4a, kv4b):
    step = 4
    wide = step * WIDTH
    return pl.pallas_call(
        functools.partial(near_body, step=step),
        name="near_levels",
        grid=(HEADS // step,),
        in_specs=[
            pl.BlockSpec((128, wide), lambda h: (0, h)),
            pl.BlockSpec((2, 128, wide), lambda h: (0, 0, h)),
            pl.BlockSpec((2, 64, wide), lambda h: (0, 0, h)),
            pl.BlockSpec((2, 64, wide), lambda h: (0, 0, h)),
        ],
        out_specs=[pl.BlockSpec((128, wide), lambda h: (0, h)), pl.BlockSpec((128, WIDTH), lambda h: (0, 0))],
        out_shape=[
            jax.ShapeDtypeStruct((128, HEADS * WIDTH), F32),
            jax.ShapeDtypeStruct((128, WIDTH), F32),
        ],
        scratch_shapes=[pltpu.VMEM((step, 4, 128, WIDTH), F32)],
        compiler_params=params(),
        cost_estimate=pl.CostEstimate(flops=400 << 20, bytes_accessed=4 << 20, transcendentals=1 << 18),
    )(q3, kv3, kv4a, kv4b)


def rise_body(got_ref, a6_ref, a7_ref, a8_ref, a9_ref, scratch):
    outs = (a6_ref, a7_ref, a8_ref, a9_ref)
    for i in range(2):
        for s in range(8):
            scratch[32 * s : 32 * s + 32, :] = got_ref[s, 32 * (i + 1) : 32 * (i + 2), :]
        count, base = 128, 0
        for ref in outs:
            x = 0.5 * (
                scratch[pl.ds(base, count, stride=2), :] + scratch[pl.ds(base + 1, count, stride=2), :]
            )
            ref[i] = x
            base = base + 2 * count
            if count > 16:
                scratch[base : base + count, :] = x
            count = count // 2


def rise_call(got):
    return pl.pallas_call(
        rise_body,
        name="rise_rows",
        out_shape=[jax.ShapeDtypeStruct((2, n, WIDTH), F32) for n in (128, 64, 32, 16)],
        scratch_shapes=[pltpu.VMEM((512, WIDTH), F32)],
        compiler_params=params(),
        cost_estimate=pl.CostEstimate(flops=1 << 18, bytes_accessed=1 << 19, transcendentals=0),
    )(got)


def far_body(got_ref, kv6_ref, near_ref, across_ref, out_ref, qs, es):
    q5 = jnp.concatenate([got_ref[s, 0:32, :] for s in range(8)], axis=0)
    qs[0:256, :] = q5
    base, count = 0, 128
    queries = [q5]
    while count >= 16:
        x = 0.5 * (qs[pl.ds(base, count, stride=2), :] + qs[pl.ds(base + 1, count, stride=2), :])
        queries.append(x)
        base = base + 2 * count
        if count > 16:
            qs[base : base + count, :] = x
        count = count // 2

    def keys(i, first, count):
        return jnp.concatenate([near_ref[i, first : first + count], across_ref[i, first : first + count]], axis=0)

    results = []
    for g in range(2):
        other = range(4) if g == 1 else range(4, 8)
        k5 = jnp.concatenate([got_ref[s, 32:64, :] for s in other], axis=0)
        v5 = jnp.concatenate([got_ref[s, 64:96, :] for s in other], axis=0)
        results.append(attend(q5[128 * g : 128 * g + 128], key_side(k5), value_side(v5), 5))
    five = tuple(jnp.concatenate([a, b], axis=0) for a, b in zip(*results))
    levels = [five, attend(queries[1], key_side(kv6_ref[0]), value_side(kv6_ref[1]), 6)]
    for i in range(3):
        levels.append(
            attend(queries[2 + i], key_side(keys(0, 64 * i, 64)), value_side(keys(1, 64 * i, 64)), 7 + i)
        )
    running = levels[-1]
    base = 0
    for finer in reversed(levels[:-1]):
        n = running[0].shape[0]
        wide = []
        for i, x in enumerate(running):
            x = jnp.broadcast_to(x, (n, WIDTH))
            es[i, pl.ds(base, n, stride=2), :] = x
            es[i, pl.ds(base + 1, n, stride=2), :] = x
            wide.append(es[i, base : base + 2 * n, :])
        base = base + 2 * n
        running = merge(finer, tuple(wide))
    m, s, n = running
    o = n / s
    lse = jnp.broadcast_to(m + jnp.log2(s), (256, WIDTH))
    for d in range(8):
        out_ref[d, 0:32, :] = o[32 * d : 32 * d + 32]
        out_ref[d, 32:64, :] = lse[32 * d : 32 * d + 32]


def far_call(got, kv6, near, across):
    return pl.pallas_call(
        far_body,
        name="far_levels",
        out_shape=jax.ShapeDtypeStruct((HEADS, 64, WIDTH), F32),
        scratch_shapes=[pltpu.VMEM((512, WIDTH), F32), pltpu.VMEM((3, 512, WIDTH), F32)],
        compiler_params=params(),
        cost_estimate=pl.CostEstimate(flops=100 << 20, bytes_accessed=1 << 20, transcendentals=1 << 17),
    )(got, kv6, near, across)


def join_body(o_ref, lse_ref, o34_ref, lse34_ref, far_ref, out_ref, scratch):
    head = pl.program_id(0)
    lane = lax.broadcasted_iota(jnp.int32, (128, WIDTH), 1)

    def pick(x):
        return jnp.sum(jnp.where(lane == head, x, 0.0), axis=1, keepdims=True)

    for i in range(2):
        x = far_ref[0, 32 * i : 32 * i + 32, :]
        for c in range(4):
            scratch[i, pl.ds(c, 32, stride=4), :] = x
    m, s, n = merge((pick(lse34_ref[...]), 1.0, o34_ref[...]), (scratch[1], 1.0, scratch[0]))
    for k in range(8):
        own = (pick(lse_ref[128 * k : 128 * k + 128, :]), 1.0, o_ref[128 * k : 128 * k + 128, :])
        _, den, num = merge(own, (m, s, n))
        out_ref[pl.ds(k, 128, stride=8), :] = num / den


def join_call(o, lse, o34, lse34, far):
    block = pl.BlockSpec((ROWS, WIDTH), lambda h: (0, h))
    return pl.pallas_call(
        join_body,
        name="join_levels",
        grid=(HEADS,),
        in_specs=[
            block,
            pl.BlockSpec((ROWS, WIDTH), lambda h: (0, 0)),
            pl.BlockSpec((128, WIDTH), lambda h: (0, h)),
            pl.BlockSpec((128, WIDTH), lambda h: (0, 0)),
            pl.BlockSpec((1, 64, WIDTH), lambda h: (h, 0, 0)),
        ],
        out_specs=block,
        out_shape=jax.ShapeDtypeStruct((ROWS, HEADS * WIDTH), F32),
        scratch_shapes=[pltpu.VMEM((2, 128, WIDTH), F32)],
        compiler_params=params(),
        cost_estimate=pl.CostEstimate(flops=16 << 20, bytes_accessed=9 << 20, transcendentals=1 << 20),
    )(o, lse, o34, lse34, far)


def hop(x, axis, flip):
    return lax.ppermute(x, axis, [(i, i ^ flip) for i in range(lax.axis_size(axis))])


def transpose_heads(x):
    return lax.all_to_all(x, "node", 0, 0, axis_index_groups=GROUPS, tiled=True)


def on_device(queries, keys, values):
    q3, kv3, kv4, pay = pool_call(queries, keys, values)
    got = transpose_heads(pay)
    got, kv3, kv4 = lax.optimization_barrier((got, kv3, kv4))
    o, lse = local_call(queries, keys, values)
    a6, a7, a8, a9 = rise_call(got)

    r8 = hop(a8, "seq", 2)
    r9a = hop(a9, "seq", 4)
    r9b = hop(a9, "seq", 6)
    kv6 = hop(a6, "node", 12)
    c7 = hop(a7, "seq", 1)
    fetched = jnp.concatenate([r8, r9a, r9b], axis=1)
    passed = hop(fetched, "seq", 1)
    near = jnp.concatenate([c7, fetched[:, :32], passed[:, :32], fetched[:, 32:], passed[:, 32:]], axis=1)
    across = hop(near, "node", 12)

    sib3 = hop(kv3, "node", 1)
    sib4a = hop(kv4, "node", 3)
    sib4b = hop(kv4, "node", 2)

    far = far_call(got, kv6, near, across)
    back = transpose_heads(far)
    o34, lse34 = near_call(q3, sib3, sib4a, sib4b)
    return join_call(o, lse, o34, lse34, back)


def solution(mesh):
    spec = P(("seq", "node"), None)
    return jax.shard_map(on_device, mesh=mesh, in_specs=(spec, spec, spec), out_specs=spec, check_vma=False)
```

time: 254 us -> 93.9 us (0.37); the launches traced: 250 us -> 93.2 us
  matrix products: 60.7 us -> 0 us
  waiting for transfers between devices: 61.3 us -> 9.88 us
  other arithmetic: 47.6 us -> 0.01 us
  Pallas kernels: 0 us -> 47.5 us
  local copies, waits for them, and re-layouts: 53.5 us -> 6.05 us
  blocking collectives: 0 us -> 14.9 us
  starting transfers between devices: 25 us -> 14.8 us
    dot_general x20 -> x0, matrix products: 60.7 us -> none  [the longest x10 33 us: batched_attend(): jnp.einsum('hbrc,hbcd->hbrd', weights, payload_blocks, precision=lax.Prec...]
    ppermute x14 -> x10, waiting for transfers between devices: 61.3 us -> 9.88 us  [hop(): lax.ppermute(x, axis, [(i, i ^ flip) for i in range(lax.axis_size(axis))])]
    pallas_call x0 -> x6, Pallas kernels: none -> 47.5 us  [the longest x1 26 us: local_call(): pl.pallas_call(local_body, name='local_levels', grid=(HEADS,), in_specs=[...]
    all_to_all x0 -> x1, blocking collectives: none -> 14.9 us  [transpose_heads(): return lax.all_to_all(x, 'node', 0, 0, axis_index_groups=GROUPS, tiled=True)]
    mul x31 -> x0, other arithmetic: 14.6 us -> none  [pool_pairs(): return 0.5 * (paired[:, :, 0] + paired[:, :, 1])]
    ppermute x14 -> x10, starting transfers between devices: 25 us -> 11.4 us  [hop(): lax.ppermute(x, axis, [(i, i ^ flip) for i in range(lax.axis_size(axis))])]
    add x11 -> x0, other arithmetic: 13.1 us -> none  [the longest x9 9.8 us: combine_coarse(): weight_sum = fine_sum * scale_fine + coarse_sum[:, :, None] * scale_coarse]
    unnamed x127 -> x13, local copies, waits for them, and re-layouts: 15.1 us -> 6.05 us
  transfers between devices with their start and end apart: 14 -> 11, of which waited for: 8 -> 4; matrix products, arithmetic and copies ran while one was open for 48% -> 0% of each run, Pallas kernels for 0% -> 36%
where the time goes in v1:
time: 93.9 us; the launch traced here: 93.2 us
  Pallas kernels  47.5 us (51%)
  blocking collectives  14.9 us (16%)
  starting transfers between devices  14.8 us (16%)
  waiting for transfers between devices  9.88 us (11%)
  local copies, waits for them, and re-layouts  6.05 us (6%)
    pallas_call x1, Pallas kernels, local_call(): pl.pallas_call(local_body, name='local_levels', grid=(HEADS,), in_specs=[...  26 us
    all_to_all x1, blocking collectives, transpose_heads(): return lax.all_to_all(x, 'node', 0, 0, axis_index_groups=GROUPS, tiled=True)  14.9 us
    ppermute x10, starting transfers between devices, hop(): lax.ppermute(x, axis, [(i, i ^ flip) for i in range(lax.axis_size(axis))])  11.4 us
    ppermute x10, waiting for transfers between devices, hop(): lax.ppermute(x, axis, [(i, i ^ flip) for i in range(lax.axis_size(axis))])  9.88 us
    pallas_call x1, Pallas kernels, pool_call(): pl.pallas_call(pool_body, name='pool_rows', grid=(HEADS,), in_specs=[bloc...  8.45 us
    unnamed x13, local copies, waits for them, and re-layouts  6.05 us
    pallas_call x1, Pallas kernels, join_call(): pl.pallas_call(join_body, name='join_levels', grid=(HEADS,), in_specs=[bl...  5.44 us
    pallas_call x1, Pallas kernels, near_call(): pl.pallas_call(functools.partial(near_body, step=step), name='near_levels...  4.97 us
  transfers between devices with their start and end apart: 11, of which 4 were waited for; matrix products, arithmetic and copies ran while one was open for 0% of the time, Pallas kernels for 36%

profile of v1, /device:TPU:0, one launch (start us, length us, event | category | flops | bytes accessed | tf_op | source)
XLA Modules:
  0.0 93.2 jit_solution(632530116997576606)
XLA Ops:
  0.0 8.5 %pool_rows.1 = (f32[128,1024]{1,0:T(8,128)S(1)}, f32[2,128,1024]{2,1,0:T(8,128)}, f32[2,64,1024]{2,1,0:T(8,128)}, f32[8,96,128]{2,1,0:T(8,128)S(1)}) custom-call(f32[1024,1024]{1,0:T(8,128)} %q_ref.3, f32[1024,1024]{1,0:T(8,128)} %k_ref.3, f32[1024,1024]{1,0:T(8,128)} %v_ref.3), custom_call_target="tpu_custom_call" | custom-call | flops 3145728 | bytes 14680064 | tf_op jit(solution)/shard_map/pool_rows/pallas_call | solution.py:120
  8.5 14.9 %all_to_all.10.got_ref = f32[8,96,128]{2,1,0:T(8,128)S(1)} all-to-all(f32[8,96,128]{2,1,0:T(8,128)S(1)} %get-tuple-element.23), channel_id=1, replica_groups={{0,1,2,3,4,5,6,7},{12,13,14,15,8,9,10,11},{16,17,18,19,20,21,22,23},{28..., dimensions={0} | all-to-all | bytes 786432 | tf_op jit(solution)/shard_map/all_to_all | solution.py:385
  23.3 0.1 rise_rows.1
  23.4 1.6 %collective-permute-start.5 = (f32[2,32,128]{2,1,0:T(8,128)S(1)}, f32[2,32,128]{2,1,0:T(8,128)S(1)}, u32[]{:S(2)}, u32[]{:S(2)}) collective-permute-start(f32[2,32,128]{2,1,0:T(8,128)S(1)} %get-tuple-element.33), channel_id=1, source_target_pairs={{0,32},{16,48},{32,0},{48,16},{64,96},{80,112},{96,64},{112,80},{1... | collective-permute-start | bytes 98312 | tf_op jit(solution)/shard_map/ppermute | solution.py:381
  25.0 2.1 %collective-permute-start.7 = (f32[2,16,128]{2,1,0:T(8,128)S(1)}, f32[2,16,128]{2,1,0:T(8,128)S(1)}, u32[]{:S(2)}, u32[]{:S(2)}) collective-permute-start(f32[2,16,128]{2,1,0:T(8,128)S(1)} %get-tuple-element.34), channel_id=1, source_target_pairs={{0,96},{16,112},{32,64},{48,80},{64,32},{80,48},{96,0},{112,16},{1... | collective-permute-start | bytes 49160 | tf_op jit(solution)/shard_map/ppermute | solution.py:381
  27.1 0.6 collective-permute-start.6
  27.7 0.0 collective-permute-start.4
  27.7 0.5 collective-permute-start
  28.2 1.7 %collective-permute-done.7 = f32[2,16,128]{2,1,0:T(8,128)S(1)} collective-permute-done((f32[2,16,128]{2,1,0:T(8,128)S(1)}, f32[2,16,128]{2,1,0:T(8,128)S(1)}, u32[]{:S(2)}, u32[]{:S(2)}) %collective-permute-start.7) | collective-permute-done | bytes 16416 | tf_op jit(solution)/shard_map/ppermute | solution.py:381
  29.9 2.4 %collective-permute-done.6 = f32[2,16,128]{2,1,0:T(8,128)S(1)} collective-permute-done((f32[2,16,128]{2,1,0:T(8,128)S(1)}, f32[2,16,128]{2,1,0:T(8,128)S(1)}, u32[]{:S(2)}, u32[]{:S(2)}) %collective-permute-start.6) | collective-permute-done | bytes 16416 | tf_op jit(solution)/shard_map/ppermute | solution.py:381
  32.3 0.0 collective-permute-done.5
  32.3 0.1 collective-permute-start.8
  32.4 0.0 collective-permute-done.4
  32.5 1.2 %collective-permute-done.8 = f32[2,64,128]{2,1,0:T(8,128)S(1)} collective-permute-done((f32[2,64,128]{2,1,0:T(8,128)S(1)}, f32[2,64,128]{2,1,0:T(8,128)S(1)}, u32[]{:S(2)}, u32[]{:S(2)}) %collective-permute-start.8) | collective-permute-done | bytes 65568 | tf_op jit(solution)/shard_map/ppermute | solution.py:381
  33.7 2.3 %collective-permute-start.9 = (f32[2,192,128]{2,1,0:T(8,128)S(1)}, f32[2,192,128]{2,1,0:T(8,128)S(1)}, u32[]{:S(2)}, u32[]{:S(2)}) collective-permute-start(f32[2,192,128]{2,1,0:T(8,128)S(1)} %slice_dynamic-update-slice_fusion.near_ref), channel_id=1, source_target_pairs={{0,12},{1,13},{2,14},{3,15},{4,8},{5,9},{6,10},{7,11},{8,4},{9,5},... | collective-permute-start | bytes 589832 | tf_op jit(solution)/shard_map/ppermute | solution.py:381
  36.0 1.1 %collective-permute-start.3 = (f32[2,128,128]{2,1,0:T(8,128)S(1)}, f32[2,128,128]{2,1,0:T(8,128)S(1)}, u32[]{:S(2)}, u32[]{:S(2)}) collective-permute-start(f32[2,128,128]{2,1,0:T(8,128)S(1)} %get-tuple-element.31), channel_id=1, source_target_pairs={{0,12},{1,13},{2,14},{3,15},{4,8},{5,9},{6,10},{7,11},{8,4},{9,5},... | collective-permute-start | bytes 393224 | tf_op jit(solution)/shard_map/ppermute | solution.py:381
  37.0 0.9 %collective-permute-start.2 = (f32[2,64,1024]{2,1,0:T(8,128)}, f32[2,64,1024]{2,1,0:T(8,128)S(1)}, u32[]{:S(2)}, u32[]{:S(2)}) collective-permute-start(f32[2,64,1024]{2,1,0:T(8,128)} %get-tuple-element.27), channel_id=1, source_target_pairs={{0,2},{1,3},{2,0},{3,1},{4,6},{5,7},{6,4},{7,5},{8,10},{9,11},{10,... | collective-permute-start | bytes 1572872 | tf_op jit(solution)/shard_map/ppermute | solution.py:381
  38.0 2.2 %collective-permute-start.1 = (f32[2,64,1024]{2,1,0:T(8,128)}, f32[2,64,1024]{2,1,0:T(8,128)S(1)}, u32[]{:S(2)}, u32[]{:S(2)}) collective-permute-start(f32[2,64,1024]{2,1,0:T(8,128)} %get-tuple-element.27), channel_id=1, source_target_pairs={{0,3},{1,2},{2,1},{3,0},{4,7},{5,6},{6,5},{7,4},{8,11},{9,10},{10,... | collective-permute-start | bytes 1572872 | tf_op jit(solution)/shard_map/ppermute | solution.py:381
  40.2 4.6 %collective-permute-done.3.kv6_ref = f32[2,128,128]{2,1,0:T(8,128)S(1)} collective-permute-done((f32[2,128,128]{2,1,0:T(8,128)S(1)}, f32[2,128,128]{2,1,0:T(8,128)S(1)}, u32[]{:S(2)}, u32[]{:S(2)}) %collective-permute-start.3) | collective-permute-done | bytes 131104 | tf_op jit(solution)/shard_map/ppermute | solution.py:381
  44.8 0.0 collective-permute-done.9.across_ref
  44.8 2.6 %far_levels.1 = f32[8,64,128]{2,1,0:T(8,128)} custom-call(f32[8,96,128]{2,1,0:T(8,128)S(1)} %all_to_all.10.got_ref, f32[2,128,128]{2,1,0:T(8,128)S(1)} %collective-permute-done.3.kv6_ref, f32[2,192,128]{2,1,0:T(8,128)S(1)} %slice_dynamic-update-slice_fusion.near_ref, f32[2,192,128]{2,1,0:T(8,128)S(1)} %collective-permute-done.9.across_ref), custom_call_target="tpu_custom_call" | custom-call | flops 104857600 | bytes 1048576 | tf_op jit(solution)/shard_map/far_levels/pallas_call | solution.py:331
  47.3 3.4 %all-to-all-start.1 = ((f32[8,64,128]{2,1,0:T(8,128)}), f32[8,64,128]{2,1,0:T(8,128)S(1)}, u32[]{:S(2)}, u32[]{:S(2)}) async-start(f32[8,64,128]{2,1,0:T(8,128)} %far_levels.1), calls=%async_computation.1 | async-start | bytes 524288 | tf_op jit(solution)/shard_map/all_to_all | solution.py:385
  50.8 26.0 %local_levels.1 = (f32[1024,1024]{1,0:T(8,128)S(1)}, f32[1024,128]{1,0:T(8,128)S(1)}) custom-call(f32[1024,1024]{1,0:T(8,128)} %q_ref.3, f32[1024,1024]{1,0:T(8,128)} %k_ref.3, f32[1024,1024]{1,0:T(8,128)} %v_ref.3), custom_call_target="tpu_custom_call" | custom-call | flops 4294967296 | bytes 16777216 | tf_op jit(solution)/shard_map/local_levels/pallas_call | solution.py:193
  76.7 0.0 copy-start
  76.8 2.0 %copy-done = f32[1024,1024]{1,0:T(8,128)} copy-done((f32[1024,1024]{1,0:T(8,128)}, f32[1024,1024]{1,0:T(8,128)S(1)}, u32[]{:S(2)}) %copy-start) | copy-done | bytes 4194328
  78.8 0.0 collective-permute-done.2.kv4b_ref
  78.8 5.0 %near_levels.1 = (f32[128,1024]{1,0:T(8,128)S(1)}, f32[128,128]{1,0:T(8,128)S(1)}) custom-call(f32[128,1024]{1,0:T(8,128)S(1)} %get-tuple-element.22.q3_ref, f32[2,128,1024]{2,1,0:T(8,128)S(1)} %collective-permute-done.kv3_ref, f32[2,64,1024]{2,1,0:T(8,128)S(1)} %collective-permute-done.1.kv4a_ref, f32[2,64,1024]{2,1,0:T(8,128)S(1)} %collective-permute-done.2.kv4b_ref), custom_call_target="tpu_custom_call" | custom-call | flops 419430400 | bytes 4194304 | tf_op jit(solution)/shard_map/near_levels/pallas_call | solution.py:233
  83.8 0.8 copy-done.2
  84.5 0.0 all-to-all-done.1.far_ref
  84.6 2.2 %copy-done.1 = f32[1024,1024]{1,0:T(8,128)S(1)} copy-done((f32[1024,1024]{1,0:T(8,128)S(1)}, f32[1024,1024]{1,0:T(8,128)}, u32[]{:S(2)}) %copy-start.1) | copy-done | bytes 4194328
  86.7 1.0 %copy-done.3 = f32[128,1024]{1,0:T(8,128)S(1)} copy-done((f32[128,1024]{1,0:T(8,128)S(1)}, f32[128,1024]{1,0:T(8,128)}, u32[]{:S(2)}) %copy-start.3) | copy-done | bytes 524312
  87.8 5.4 %join_levels.1 = f32[1024,1024]{1,0:T(8,128)} custom-call(f32[1024,1024]{1,0:T(8,128)S(1)} %copy-done.1, f32[1024,128]{1,0:T(8,128)S(1)} %get-tuple-element.21.lse_ref, f32[128,1024]{1,0:T(8,128)S(1)} %copy-done.3, f32[128,128]{1,0:T(8,128)S(1)} %get-tuple-element.29.lse34_ref, f32[8,64,128]{2,1,0:T(8,128)S(1)} %all-to-all-done.1.far_ref), custom_call_target="tpu_custom_call" | custom-call | flops 16777216 | bytes 9437184 | tf_op jit(solution)/shard_map/join_levels/pallas_call | solution.py:361
  (12 shorter events, 0.0 us)
Async XLA Ops:
  23.4 8.9 %collective-permute-start.5 = (f32[2,32,128]{2,1,0:T(8,128)S(1)}, f32[2,32,128]{2,1,0:T(8,128)S(1)}, u32[]{:S(2)}, u32[]{:S(2)}) collective-permute-start(f32[2,32,128]{2,1,0:T(8,128)S(1)} %get-tuple-element.33), channel_id=1, source_target_pairs={{0,32},{16,48},{32,0},{48,16},{64,96},{80,112},{96,64},{112,80},{1... | collective-permute-start | bytes 98312 | tf_op jit(solution)/shard_map/ppermute | solution.py:381
  25.0 4.9 %collective-permute-start.7 = (f32[2,16,128]{2,1,0:T(8,128)S(1)}, f32[2,16,128]{2,1,0:T(8,128)S(1)}, u32[]{:S(2)}, u32[]{:S(2)}) collective-permute-start(f32[2,16,128]{2,1,0:T(8,128)S(1)} %get-tuple-element.34), channel_id=1, source_target_pairs={{0,96},{16,112},{32,64},{48,80},{64,32},{80,48},{96,0},{112,16},{1... | collective-permute-start | bytes 49160 | tf_op jit(solution)/shard_map/ppermute | solution.py:381
  27.1 5.2 %collective-permute-start.6 = (f32[2,16,128]{2,1,0:T(8,128)S(1)}, f32[2,16,128]{2,1,0:T(8,128)S(1)}, u32[]{:S(2)}, u32[]{:S(2)}) collective-permute-start(f32[2,16,128]{2,1,0:T(8,128)S(1)} %get-tuple-element.34), channel_id=1, source_target_pairs={{0,64},{16,80},{32,96},{48,112},{64,0},{80,16},{96,32},{112,48},{1... | collective-permute-start | bytes 49160 | tf_op jit(solution)/shard_map/ppermute | solution.py:381
  27.7 4.7 %collective-permute-start.4 = (f32[2,64,128]{2,1,0:T(8,128)S(1)}, f32[2,64,128]{2,1,0:T(8,128)S(1)}, u32[]{:S(2)}, u32[]{:S(2)}) collective-permute-start(f32[2,64,128]{2,1,0:T(8,128)S(1)} %get-tuple-element.32), channel_id=1, source_target_pairs={{0,16},{16,0},{32,48},{48,32},{64,80},{80,64},{96,112},{112,96},{1... | collective-permute-start | bytes 196616 | tf_op jit(solution)/shard_map/ppermute | solution.py:381
  27.7 51.1 %collective-permute-start = (f32[2,128,1024]{2,1,0:T(8,128)}, f32[2,128,1024]{2,1,0:T(8,128)S(1)}, u32[]{:S(2)}, u32[]{:S(2)}) collective-permute-start(f32[2,128,1024]{2,1,0:T(8,128)} %get-tuple-element.26), channel_id=1, source_target_pairs={{0,1},{1,0},{2,3},{3,2},{4,5},{5,4},{6,7},{7,6},{8,9},{9,8},{10,11... | collective-permute-start | bytes 3145736 | tf_op jit(solution)/shard_map/ppermute | solution.py:381
  32.3 1.3 %collective-permute-start.8 = (f32[2,64,128]{2,1,0:T(8,128)S(1)}, f32[2,64,128]{2,1,0:T(8,128)S(1)}, u32[]{:S(2)}, u32[]{:S(2)}) collective-permute-start(f32[2,64,128]{2,1,0:T(8,128)S(1)} %pad_maximum_fusion), channel_id=1, source_target_pairs={{0,16},{16,0},{32,48},{48,32},{64,80},{80,64},{96,112},{112,96},{1... | collective-permute-start | bytes 196616 | tf_op jit(solution)/shard_map/ppermute | solution.py:381
  33.7 11.1 %collective-permute-start.9 = (f32[2,192,128]{2,1,0:T(8,128)S(1)}, f32[2,192,128]{2,1,0:T(8,128)S(1)}, u32[]{:S(2)}, u32[]{:S(2)}) collective-permute-start(f32[2,192,128]{2,1,0:T(8,128)S(1)} %slice_dynamic-update-slice_fusion.near_ref), channel_id=1, source_target_pairs={{0,12},{1,13},{2,14},{3,15},{4,8},{5,9},{6,10},{7,11},{8,4},{9,5},... | collective-permute-start | bytes 589832 | tf_op jit(solution)/shard_map/ppermute | solution.py:381
  36.0 8.8 %collective-permute-start.3 = (f32[2,128,128]{2,1,0:T(8,128)S(1)}, f32[2,128,128]{2,1,0:T(8,128)S(1)}, u32[]{:S(2)}, u32[]{:S(2)}) collective-permute-start(f32[2,128,128]{2,1,0:T(8,128)S(1)} %get-tuple-element.31), channel_id=1, source_target_pairs={{0,12},{1,13},{2,14},{3,15},{4,8},{5,9},{6,10},{7,11},{8,4},{9,5},... | collective-permute-start | bytes 393224 | tf_op jit(solution)/shard_map/ppermute | solution.py:381
  37.0 41.8 %collective-permute-start.2 = (f32[2,64,1024]{2,1,0:T(8,128)}, f32[2,64,1024]{2,1,0:T(8,128)S(1)}, u32[]{:S(2)}, u32[]{:S(2)}) collective-permute-start(f32[2,64,1024]{2,1,0:T(8,128)} %get-tuple-element.27), channel_id=1, source_target_pairs={{0,2},{1,3},{2,0},{3,1},{4,6},{5,7},{6,4},{7,5},{8,10},{9,11},{10,... | collective-permute-start | bytes 1572872 | tf_op jit(solution)/shard_map/ppermute | solution.py:381
  38.0 40.8 %collective-permute-start.1 = (f32[2,64,1024]{2,1,0:T(8,128)}, f32[2,64,1024]{2,1,0:T(8,128)S(1)}, u32[]{:S(2)}, u32[]{:S(2)}) collective-permute-start(f32[2,64,1024]{2,1,0:T(8,128)} %get-tuple-element.27), channel_id=1, source_target_pairs={{0,3},{1,2},{2,1},{3,0},{4,7},{5,6},{6,5},{7,4},{8,11},{9,10},{10,... | collective-permute-start | bytes 1572872 | tf_op jit(solution)/shard_map/ppermute | solution.py:381
  47.3 37.2 %all-to-all-start.1 = ((f32[8,64,128]{2,1,0:T(8,128)}), f32[8,64,128]{2,1,0:T(8,128)S(1)}, u32[]{:S(2)}, u32[]{:S(2)}) async-start(f32[8,64,128]{2,1,0:T(8,128)} %far_levels.1), calls=%async_computation.1 | async-start | bytes 524288 | tf_op jit(solution)/shard_map/all_to_all | solution.py:385
  76.7 2.0 %copy-start = (f32[1024,1024]{1,0:T(8,128)}, f32[1024,1024]{1,0:T(8,128)S(1)}, u32[]{:S(2)}) copy-start(f32[1024,1024]{1,0:T(8,128)S(1)} %get-tuple-element.20.o_ref) | copy-start | bytes 12582916
  83.7 0.8 copy-start.2
  84.6 2.2 %copy-start.1 = (f32[1024,1024]{1,0:T(8,128)S(1)}, f32[1024,1024]{1,0:T(8,128)}, u32[]{:S(2)}) copy-start(f32[1024,1024]{1,0:T(8,128)} %copy-done) | copy-start | bytes 12582916
  86.7 1.0 %copy-start.3 = (f32[128,1024]{1,0:T(8,128)S(1)}, f32[128,1024]{1,0:T(8,128)}, u32[]{:S(2)}) copy-start(f32[128,1024]{1,0:T(8,128)} %copy-done.2) | copy-start | bytes 1572868

commit v2 on v1

v2 whole, which is shorter than its diff:
```python
import functools
import math

import jax
import jax.numpy as jnp
from jax import lax
from jax.experimental import pallas as pl
from jax.experimental.pallas import tpu as pltpu
from jax.sharding import PartitionSpec as P

HEADS = 8
CALLS = (2, 1, 5)
WIDTH = 128
ROWS = 1024
F32 = jnp.float32
BF16 = jnp.bfloat16
SCALE = WIDTH ** (-0.5) / math.log(2.0)
MIB = 1024 * 1024

GROUPS = [list(range(8)), [12, 13, 14, 15, 8, 9, 10, 11]]


def params(mib=12):
    return pltpu.CompilerParams(vmem_limit_bytes=mib * MIB)


def in_hbm(x):
    return pltpu.with_memory_space_constraint(x, pltpu.HBM)


def split(x):
    hi = x.astype(BF16)
    lo = (x - hi.astype(F32)).astype(BF16)
    return hi, lo


def dot_nt(a, b):
    return lax.dot_general(a, b, (((1,), (1,)), ((), ())), preferred_element_type=F32)


def dot_nn(a, b):
    return lax.dot_general(a, b, (((1,), (0,)), ((), ())), preferred_element_type=F32)


def key_side(k):
    hi, lo = split(k)
    return jnp.concatenate([hi, hi], axis=1), jnp.concatenate([lo, jnp.zeros_like(lo)], axis=1)


def scores(q, sides):
    hi, lo = split(q)
    both = jnp.concatenate([hi, lo], axis=1)
    first, second = sides
    n = first.shape[0]
    if n == 128:
        s = dot_nt(both, jnp.concatenate([first, second], axis=0))
        return s[:, :n] + s[:, n:]
    return dot_nt(both, first) + dot_nt(both, second)


def weigh(p, side):
    hi, lo = side
    p_hi, p_lo = split(p)
    if hi.shape[0] == 128:
        left = jnp.concatenate([p_hi, p_lo], axis=1)
        right = jnp.concatenate(
            [jnp.concatenate([hi, lo], axis=1), jnp.concatenate([hi, jnp.zeros_like(lo)], axis=1)], axis=0
        )
        r = dot_nn(left, right)
        return r[:, :WIDTH] + r[:, WIDTH:]
    r = dot_nn(p_hi, jnp.concatenate([hi, lo], axis=1))
    return r[:, :WIDTH] + r[:, WIDTH:] + dot_nn(p_lo, hi)


def attend_all(tasks):
    grids = [scores(q, key_side(k)) for q, k, _, _ in tasks]
    peaks = [jnp.max(s, axis=1, keepdims=True) for s in grids]
    weights = [jnp.exp2(s - peak) for s, peak in zip(grids, peaks)]
    totals = [jnp.sum(p, axis=1, keepdims=True) for p in weights]
    numerators = [weigh(p, split(task[2])) for p, task in zip(weights, tasks)]
    return [(peak + float(task[3]), t, n) for peak, t, n, task in zip(peaks, totals, numerators, tasks)]


def merge(a, b):
    ma, sa, na = a
    mb, sb, nb = b
    gap = ma - mb
    small = jnp.exp2(-jnp.abs(gap))
    fa = jnp.where(gap >= 0, 1.0, small)
    fb = jnp.where(gap >= 0, small, 1.0)
    return jnp.maximum(ma, mb), sa * fa + sb * fb, na * fa + nb * fb


def pool_body(q_hbm, k_hbm, v_hbm, q3_ref, mean_ref, half_ref, pay_ref, rows, scratch, sems):
    arrays = (q_hbm, k_hbm, v_hbm)

    def fetch(i, h):
        return pltpu.make_async_copy(
            arrays[i].at[:, WIDTH * h : WIDTH * h + WIDTH], rows.at[i, h], sems.at[i, h]
        )

    for h in range(HEADS):
        for i in range(3):
            fetch(i, h).start()

    def pairs(ref, n):
        return 0.5 * ref[pl.ds(0, n, stride=2), :], 0.5 * ref[pl.ds(1, n, stride=2), :]

    for h in range(HEADS):
        cols = slice(WIDTH * h, WIDTH * h + WIDTH)
        for i in range(3):
            fetch(i, h).wait()
            ref = rows.at[i, h]
            total = ref[pl.ds(0, 128, stride=8), :]
            for k in range(1, 8):
                total = total + ref[pl.ds(k, 128, stride=8), :]
            x = total * (0.125 * SCALE if i == 0 else 0.125)
            scratch[i, 0:128, :] = x
            even, odd = pairs(scratch.at[i, 0:128], 64)
            scratch[i, 128:192, :] = even + odd
            pay_ref[h, 32 * i : 32 * i + 32, :] = sum(pairs(scratch.at[i, 128:192], 32))
            if i == 0:
                q3_ref[:, cols] = x
            else:
                mean_ref[i - 1, :, cols] = even + odd
                half_ref[i - 1, :, cols] = even - odd


def pool_call(q, k, v):
    return pl.pallas_call(
        pool_body,
        name="pool_rows",
        in_specs=[pl.BlockSpec(memory_space=pl.ANY)] * 3,
        out_shape=[
            pltpu.HBM((128, HEADS * WIDTH), F32),
            pltpu.HBM((2, 64, HEADS * WIDTH), F32),
            pltpu.HBM((2, 64, HEADS * WIDTH), F32),
            pltpu.HBM((HEADS, 96, WIDTH), F32),
        ],
        scratch_shapes=[
            pltpu.VMEM((3, HEADS, ROWS, WIDTH), F32),
            pltpu.VMEM((3, 192, WIDTH), F32),
            pltpu.SemaphoreType.DMA((3, HEADS)),
        ],
        compiler_params=params(24),
        cost_estimate=pl.CostEstimate(flops=3 << 20, bytes_accessed=14 << 20, transcendentals=0),
    )(in_hbm(q), in_hbm(k), in_hbm(v))


def local_body(first, q_ref, k_ref, v_ref, o_ref, lse_ref):
    head = pl.program_id(0) + first

    def load(ref):
        return [ref[pl.ds(k, 128, stride=8), :] for k in range(8)]

    def pool(parts):
        return [0.5 * (parts[2 * i] + parts[2 * i + 1]) for i in range(len(parts) // 2)]

    def rows(parts, begin, count):
        return jnp.concatenate([x[begin : begin + count] for x in parts], axis=0)

    q0 = [x * SCALE for x in load(q_ref)]
    k0, v0 = load(k_ref), load(v_ref)
    q1, k1, v1 = pool(q0), pool(k0), pool(v0)
    q2, k2, v2 = pool(q1), pool(k1), pool(v1)
    tasks = []
    for b in range(2):
        c = 64 * (b ^ 1)
        tasks.append((rows(q2, 64 * b, 64), rows(k2, c, 64), rows(v2, c, 64), 2))
    for p in range(4):
        c = 32 * (p ^ 1)
        tasks.append((rows(q1, 32 * p, 32), rows(k1, c, 32), rows(v1, c, 32), 1))
    for p in range(4):
        c = 32 * p
        tasks.append((rows(q0, c, 32), rows(k0, c, 32), rows(v0, c, 32), 0))
    done = attend_all(tasks)
    at2, at1, at0 = done[:2], done[2:6], done[6:]

    lane = lax.broadcasted_iota(jnp.int32, (128, WIDTH), 1)
    lses = [[None] * 4 for _ in range(8)]
    for p in range(4):
        off = 32 * (p % 2)
        for j in range(4):
            i = j // 2
            one = tuple(x[32 * j : 32 * j + 32] for x in at1[p])
            two = tuple(x[64 * i + off : 64 * i + off + 32] for x in at2[p // 2])
            coarse = merge(one, two)
            for k in (2 * j, 2 * j + 1):
                m, s, n = merge(tuple(x[32 * k : 32 * k + 32] for x in at0[p]), coarse)
                o_ref[128 * k + 32 * p : 128 * k + 32 * p + 32, :] = n / s
                lses[k][p] = m + jnp.log2(s)
    for k in range(8):
        old = lse_ref[128 * k : 128 * k + 128, :]
        lse_ref[128 * k : 128 * k + 128, :] = jnp.where(lane == head, jnp.concatenate(lses[k], axis=0), old)


def local_call(q, k, v, first, count):
    block = pl.BlockSpec((ROWS, WIDTH), lambda h: (0, h + first))
    return pl.pallas_call(
        functools.partial(local_body, first),
        name="local_levels",
        grid=(count,),
        in_specs=[block] * 3,
        out_specs=[pl.BlockSpec((ROWS, WIDTH), lambda h: (0, h)), pl.BlockSpec((ROWS, WIDTH), lambda h: (0, 0))],
        out_shape=[
            pltpu.HBM((ROWS, count * WIDTH), F32),
            pltpu.HBM((ROWS, WIDTH), F32),
        ],
        compiler_params=params(16),
        cost_estimate=pl.CostEstimate(
            flops=(count << 30), bytes_accessed=count << 21, transcendentals=count << 19
        ),
    )(in_hbm(q), in_hbm(k), in_hbm(v))


def near_body(q3_ref, mean_ref, half_ref, kv4a_ref, kv4b_ref, o_ref, lse_ref, scratch, *, step):
    group = pl.program_id(0)
    lane = lax.broadcasted_iota(jnp.int32, (128, WIDTH), 1)
    tasks = []
    for h in range(step):
        cols = slice(WIDTH * h, WIDTH * h + WIDTH)
        scratch[h, 0, :, :] = q3_ref[:, cols]
        q4 = 0.5 * (scratch[h, 0, pl.ds(0, 64, stride=2), :] + scratch[h, 0, pl.ds(1, 64, stride=2), :])
        k4 = jnp.concatenate([kv4a_ref[0, :, cols], kv4b_ref[0, :, cols]], axis=0)
        v4 = jnp.concatenate([kv4a_ref[1, :, cols], kv4b_ref[1, :, cols]], axis=0)
        tasks.append((q4, k4, v4, 4))
        k3, v3 = (
            jnp.concatenate(
                [mean_ref[i, :, cols] + half_ref[i, :, cols], mean_ref[i, :, cols] - half_ref[i, :, cols]], axis=0
            )
            for i in range(2)
        )
        tasks.append((q3_ref[:, cols], k3, v3, 3))
    done = attend_all(tasks)
    packed = lse_ref[...]
    for h in range(step):
        cols = slice(WIDTH * h, WIDTH * h + WIDTH)
        for i, x in enumerate(done[2 * h]):
            x = jnp.broadcast_to(x, (64, WIDTH))
            scratch[h, i + 1, pl.ds(0, 64, stride=2), :] = x
            scratch[h, i + 1, pl.ds(1, 64, stride=2), :] = x
        m, s, n = merge(done[2 * h + 1], (scratch[h, 1], scratch[h, 2], scratch[h, 3]))
        o_ref[:, cols] = n / s
        packed = jnp.where(lane == group * step + h, m + jnp.log2(s), packed)
    lse_ref[...] = packed


def near_call(q3, mean, half, kv4a, kv4b):
    step = 8
    wide = step * WIDTH
    return pl.pallas_call(
        functools.partial(near_body, step=step),
        name="near_levels",
        grid=(HEADS // step,),
        in_specs=[
            pl.BlockSpec((128, wide), lambda h: (0, h)),
        ]
        + [pl.BlockSpec((2, 64, wide), lambda h: (0, 0, h))] * 4,
        out_specs=[pl.BlockSpec((128, wide), lambda h: (0, h)), pl.BlockSpec((128, WIDTH), lambda h: (0, 0))],
        out_shape=[
            pltpu.HBM((128, HEADS * WIDTH), F32),
            pltpu.HBM((128, WIDTH), F32),
        ],
        scratch_shapes=[pltpu.VMEM((step, 4, 128, WIDTH), F32)],
        compiler_params=params(),
        cost_estimate=pl.CostEstimate(flops=400 << 20, bytes_accessed=4 << 20, transcendentals=1 << 18),
    )(in_hbm(q3), mean, half, kv4a, kv4b)


def rise_body(got_ref, a6_ref, a7_ref, a8_ref, a9_ref, scratch):
    outs = (a6_ref, a7_ref, a8_ref, a9_ref)
    for i in range(2):
        for s in range(8):
            scratch[32 * s : 32 * s + 32, :] = got_ref[s, 32 * (i + 1) : 32 * (i + 2), :]
        count, base = 128, 0
        for ref in outs:
            x = 0.5 * (
                scratch[pl.ds(base, count, stride=2), :] + scratch[pl.ds(base + 1, count, stride=2), :]
            )
            ref[i] = x
            base = base + 2 * count
            if count > 16:
                scratch[base : base + count, :] = x
            count = count // 2


def rise_call(got):
    return pl.pallas_call(
        rise_body,
        name="rise_rows",
        out_shape=[jax.ShapeDtypeStruct((2, n, WIDTH), F32) for n in (128, 64, 32, 16)],
        scratch_shapes=[pltpu.VMEM((512, WIDTH), F32)],
        compiler_params=params(),
        cost_estimate=pl.CostEstimate(flops=1 << 18, bytes_accessed=1 << 19, transcendentals=0),
    )(got)


def far_body(got_ref, kv6_ref, near_ref, across_ref, out_ref, qs, es):
    q5 = jnp.concatenate([got_ref[s, 0:32, :] for s in range(8)], axis=0)
    qs[0:256, :] = q5
    base, count = 0, 128
    queries = [q5]
    while count >= 16:
        x = 0.5 * (qs[pl.ds(base, count, stride=2), :] + qs[pl.ds(base + 1, count, stride=2), :])
        queries.append(x)
        base = base + 2 * count
        if count > 16:
            qs[base : base + count, :] = x
        count = count // 2

    def keys(i, first, count):
        return jnp.concatenate([near_ref[i, first : first + count], across_ref[i, first : first + count]], axis=0)

    tasks = []
    for g in range(2):
        other = range(4) if g == 1 else range(4, 8)
        k5 = jnp.concatenate([got_ref[s, 32:64, :] for s in other], axis=0)
        v5 = jnp.concatenate([got_ref[s, 64:96, :] for s in other], axis=0)
        tasks.append((q5[128 * g : 128 * g + 128], k5, v5, 5))
    tasks.append((queries[1], kv6_ref[0], kv6_ref[1], 6))
    for i in range(3):
        tasks.append((queries[2 + i], keys(0, 64 * i, 64), keys(1, 64 * i, 64), 7 + i))
    done = attend_all(tasks)
    five = tuple(jnp.concatenate([a, b], axis=0) for a, b in zip(done[0], done[1]))
    levels = [five] + done[2:]
    running = levels[-1]
    base = 0
    for finer in reversed(levels[:-1]):
        n = running[0].shape[0]
        wide = []
        for i, x in enumerate(running):
            x = jnp.broadcast_to(x, (n, WIDTH))
            es[i, pl.ds(base, n, stride=2), :] = x
            es[i, pl.ds(base + 1, n, stride=2), :] = x
            wide.append(es[i, base : base + 2 * n, :])
        base = base + 2 * n
        running = merge(finer, tuple(wide))
    m, s, n = running
    o = n / s
    lse = jnp.broadcast_to(m + jnp.log2(s), (256, WIDTH))
    for d in range(8):
        out_ref[d, 0:32, :] = o[32 * d : 32 * d + 32]
        out_ref[d, 32:64, :] = lse[32 * d : 32 * d + 32]


def far_call(got, kv6, near, across):
    return pl.pallas_call(
        far_body,
        name="far_levels",
        out_shape=pltpu.HBM((HEADS, 64, WIDTH), F32),
        scratch_shapes=[pltpu.VMEM((512, WIDTH), F32), pltpu.VMEM((3, 512, WIDTH), F32)],
        compiler_params=params(),
        cost_estimate=pl.CostEstimate(flops=100 << 20, bytes_accessed=1 << 20, transcendentals=1 << 17),
    )(got, kv6, near, across)


def join_body(*refs):
    n = len(CALLS)
    own_hbm, own_lse_hbm = refs[:n], refs[n : 2 * n]
    o34_hbm, lse34_hbm, far_ref, out_hbm = refs[2 * n : 2 * n + 4]
    own, own_lse, o34, lse34, wide, stage, own_sems, sems, out_sems = refs[2 * n + 4 :]
    place = [(c, i) for c, count in enumerate(CALLS) for i in range(count)]

    def columns(h):
        return slice(WIDTH * h, WIDTH * h + WIDTH)

    def fetch(h):
        c, i = place[h]
        return pltpu.make_async_copy(own_hbm[c].at[:, columns(i)], own.at[h], own_sems.at[h])

    def send(h):
        return pltpu.make_async_copy(stage.at[h % 4], out_hbm.at[:, columns(h)], out_sems.at[h % 4])

    others = [
        pltpu.make_async_copy(source, target, sems.at[i])
        for i, (source, target) in enumerate(
            [(lse34_hbm, lse34), (o34_hbm, o34)] + [(own_lse_hbm[c], own_lse.at[c]) for c in range(n)]
        )
    ]
    for copy in others[:3]:
        copy.start()
    for h in range(HEADS):
        fetch(h).start()
        if h == 0:
            for copy in others[3:]:
                copy.start()
    for copy in others:
        copy.wait()

    def column(x, h):
        return jnp.broadcast_to(x[:, h : h + 1], (128, WIDTH))

    for h in range(HEADS):
        if h >= 4:
            send(h - 4).wait()
        for i in range(2):
            x = far_ref[h, 32 * i : 32 * i + 32, :]
            for c in range(4):
                wide[h % 2, i, pl.ds(c, 32, stride=4), :] = x
        coarse = merge((column(lse34[...], h), 1.0, o34[:, columns(h)]), (wide[h % 2, 1], 1.0, wide[h % 2, 0]))
        fetch(h).wait()
        for k in range(8):
            part = slice(128 * k, 128 * k + 128)
            lse = column(own_lse[place[h][0], part, :], h)
            _, den, num = merge((lse, 1.0, own[h, part, :]), coarse)
            stage[h % 4, pl.ds(k, 128, stride=8), :] = num / den
        send(h).start()
    for h in range(HEADS - 4, HEADS):
        send(h).wait()


def join_call(own, o34, lse34, far):
    n = len(CALLS)
    anywhere = pl.BlockSpec(memory_space=pl.ANY)
    return pl.pallas_call(
        join_body,
        name="join_levels",
        in_specs=[anywhere] * (2 * n + 2) + [pl.BlockSpec(memory_space=pltpu.VMEM)],
        out_specs=anywhere,
        out_shape=pltpu.HBM((ROWS, HEADS * WIDTH), F32),
        scratch_shapes=[
            pltpu.VMEM((HEADS, ROWS, WIDTH), F32),
            pltpu.VMEM((n, ROWS, WIDTH), F32),
            pltpu.VMEM((128, HEADS * WIDTH), F32),
            pltpu.VMEM((128, WIDTH), F32),
            pltpu.VMEM((2, 2, 128, WIDTH), F32),
            pltpu.VMEM((4, ROWS, WIDTH), F32),
            pltpu.SemaphoreType.DMA((HEADS,)),
            pltpu.SemaphoreType.DMA((n + 2,)),
            pltpu.SemaphoreType.DMA((4,)),
        ],
        compiler_params=params(16),
        cost_estimate=pl.CostEstimate(flops=16 << 20, bytes_accessed=9 << 20, transcendentals=1 << 20),
    )(*[in_hbm(o) for o, _ in own], *[in_hbm(lse) for _, lse in own], in_hbm(o34), in_hbm(lse34), far)


def hop(x, axis, flip):
    return lax.ppermute(x, axis, [(i, i ^ flip) for i in range(lax.axis_size(axis))])


def transpose_heads(x):
    return lax.all_to_all(x, "node", 0, 0, axis_index_groups=GROUPS, tiled=True)


def on_device(queries, keys, values):
    q3, mean, half, pay = pool_call(queries, keys, values)
    got = transpose_heads(pay)
    one = local_call(queries, keys, values, 0, CALLS[0])
    mean, half, one, queries = lax.optimization_barrier((mean, half, one, queries))
    mean3 = hop(mean, "node", 1)
    kv4a = hop(mean, "node", 3)
    two = local_call(queries, keys, values, CALLS[0], CALLS[1])
    got, two = lax.optimization_barrier((got, two))
    a6, a7, a8, a9 = rise_call(got)

    kv6 = hop(a6, "node", 12)
    c7 = hop(a7, "seq", 1)
    r8 = hop(a8, "seq", 2)
    r9a = hop(a9, "seq", 4)
    r9b = hop(a9, "seq", 6)
    fetched = jnp.concatenate([r8, r9a, r9b], axis=1)
    fetched, kv6, mean3, kv4a, half = lax.optimization_barrier((fetched, kv6, mean3, kv4a, half))
    half3 = hop(half, "node", 1)
    kv4b = hop(mean3, "node", 3)
    passed = hop(fetched, "seq", 1)
    near = jnp.concatenate([c7, fetched[:, :32], passed[:, :32], fetched[:, 32:], passed[:, 32:]], axis=1)
    across = hop(near, "node", 12)

    far = far_call(got, kv6, near, across)
    back = transpose_heads(far)
    queries, keys, values, far = lax.optimization_barrier((queries, keys, values, far))
    three = local_call(queries, keys, values, CALLS[0] + CALLS[1], CALLS[2])
    o34, lse34 = near_call(q3, mean3, half3, kv4a, kv4b)
    return join_call([one, two, three], o34, lse34, back)


def solution(mesh):
    spec = P(("seq", "node"), None)
    return jax.shard_map(on_device, mesh=mesh, in_specs=(spec, spec, spec), out_specs=spec, check_vma=False)
```

time: 93.9 us -> 78.9 us (0.84)
  blocking collectives: 14.9 us -> 0 us
  starting transfers between devices: 14.8 us -> 24.2 us
  Pallas kernels: 47.5 us -> 39.9 us
  local copies, waits for them, and re-layouts: 6.05 us -> 0.03 us
  waiting for transfers between devices: 9.88 us -> 13.9 us
    all_to_all x1 -> x0, blocking collectives: 14.9 us -> none  [transpose_heads(): return lax.all_to_all(x, 'node', 0, 0, axis_index_groups=GROUPS, tiled=True)]
    all_to_all x1 -> x2, starting transfers between devices: 3.41 us -> 10 us  [transpose_heads(): return lax.all_to_all(x, 'node', 0, 0, axis_index_groups=GROUPS, tiled=True)]
    unnamed x13 -> x8, local copies, waits for them, and re-layouts: 6.05 us -> 0.03 us
    pallas_call x4 -> x6, Pallas kernels: 42.5 us -> 36.6 us  [the longest x3 21.6 us: local_call(): pl.pallas_call(functools.partial(local_body, first), name='local_levels',...]
    ppermute x10 -> x11, waiting for transfers between devices: 9.88 us -> 13.9 us  [hop(): lax.ppermute(x, axis, [(i, i ^ flip) for i in range(lax.axis_size(axis))])]
    ppermute x10 -> x11, starting transfers between devices: 11.4 us -> 14.2 us  [hop(): lax.ppermute(x, axis, [(i, i ^ flip) for i in range(lax.axis_size(axis))])]
    pallas_call x1, Pallas kernels: 4.97 us -> 3.2 us  [near_call(): pl.pallas_call(functools.partial(near_body, step=step), name='near_levels...]
  transfers between devices with their start and end apart: 11 -> 13, of which waited for: 4 -> 5; matrix products, arithmetic and copies ran while one was open for 0% -> 0% of each run, Pallas kernels for 36% -> 34%
where the time goes in v2:
time: 78.9 us; the launch traced here: 78.3 us
  Pallas kernels  39.9 us (51%)
  starting transfers between devices  24.2 us (31%)
  waiting for transfers between devices  13.9 us (18%)
    pallas_call x3, Pallas kernels, local_call(): pl.pallas_call(functools.partial(local_body, first), name='local_levels',...  21.6 us
    ppermute x11, starting transfers between devices, hop(): lax.ppermute(x, axis, [(i, i ^ flip) for i in range(lax.axis_size(axis))])  14.2 us
    ppermute x11, waiting for transfers between devices, hop(): lax.ppermute(x, axis, [(i, i ^ flip) for i in range(lax.axis_size(axis))])  13.9 us
    all_to_all x2, starting transfers between devices, transpose_heads(): return lax.all_to_all(x, 'node', 0, 0, axis_index_groups=GROUPS, tiled=True)  10 us
    pallas_call x1, Pallas kernels, join_call(): pl.pallas_call(join_body, name='join_levels', in_specs=[anywhere] * (2 *...  6.82 us
    pallas_call x1, Pallas kernels, pool_call(): pl.pallas_call(pool_body, name='pool_rows', in_specs=[pl.BlockSpec(memory...  6.32 us
    pallas_call x1, Pallas kernels, near_call(): pl.pallas_call(functools.partial(near_body, step=step), name='near_levels...  3.2 us
    pallas_call x1, Pallas kernels, far_call(): pl.pallas_call(far_body, name='far_levels', out_shape=pltpu.HBM((HEADS, 6...  1.8 us
  transfers between devices with their start and end apart: 13, of which 5 were waited for; matrix products, arithmetic and copies ran while one was open for 0% of the time, Pallas kernels for 34%

profile of v2, /device:TPU:0, one launch (start us, length us, event | category | flops | bytes accessed | tf_op | source)
XLA Modules:
  0.0 78.3 jit_solution(9929624668951561891)
XLA Ops:
  0.0 6.3 %pool_rows.1 = (f32[128,1024]{1,0:T(8,128)}, f32[2,64,1024]{2,1,0:T(8,128)}, f32[2,64,1024]{2,1,0:T(8,128)}, f32[8,96,128]{2,1,0:T(8,128)}) custom-call(f32[1024,1024]{1,0:T(8,128)} %q_ref.3, f32[1024,1024]{1,0:T(8,128)} %k_ref.4, f32[1024,1024]{1,0:T(8,128)} %v_ref.4), custom_call_target="tpu_custom_call" | custom-call | flops 3145728 | bytes 14680064 | tf_op jit(solution)/shard_map/pool_rows/pallas_call | solution.py:130
  6.3 6.4 %all-to-all-start = ((f32[8,96,128]{2,1,0:T(8,128)}), f32[8,96,128]{2,1,0:T(8,128)S(1)}, u32[]{:S(2)}, u32[]{:S(2)}) async-start(f32[8,96,128]{2,1,0:T(8,128)} %get-tuple-element.42), calls=%async_computation | async-start | bytes 786432 | tf_op jit(solution)/shard_map/all_to_all | solution.py:442
  12.8 6.0 %local_levels.3 = (f32[1024,256]{1,0:T(8,128)}, f32[1024,128]{1,0:T(8,128)}) custom-call(f32[1024,1024]{1,0:T(8,128)} %q_ref.3, f32[1024,1024]{1,0:T(8,128)} %k_ref.4, f32[1024,1024]{1,0:T(8,128)} %v_ref.4), custom_call_target="tpu_custom_call" | custom-call | flops 2147483648 | bytes 4194304 | tf_op jit(solution)/shard_map/local_levels/pallas_call | solution.py:199
  18.7 3.3 %collective-permute-start.5 = (f32[2,64,1024]{2,1,0:T(8,128)S(1)}, f32[2,64,1024]{2,1,0:T(8,128)S(1)}, u32[]{:S(2)}, u32[]{:S(2)}) collective-permute-start(f32[2,64,1024]{2,1,0:T(8,128)S(1)} %copy-done.1), channel_id=1, source_target_pairs={{0,3},{1,2},{2,1},{3,0},{4,7},{5,6},{6,5},{7,4},{8,11},{9,10},{10,... | collective-permute-start | bytes 1572872 | tf_op jit(solution)/shard_map/ppermute | solution.py:438
  22.1 0.2 collective-permute-start.4
  22.3 4.1 %local_levels.4 = (f32[1024,128]{1,0:T(8,128)}, f32[1024,128]{1,0:T(8,128)}) custom-call(f32[1024,1024]{1,0:T(8,128)} %q_ref.3, f32[1024,1024]{1,0:T(8,128)} %k_ref.4, f32[1024,1024]{1,0:T(8,128)} %v_ref.4), custom_call_target="tpu_custom_call" | custom-call | flops 1073741824 | bytes 2097152 | tf_op jit(solution)/shard_map/local_levels/pallas_call | solution.py:199
  26.4 0.0 all-to-all-done.got_ref
  26.4 0.1 rise_rows.1
  26.5 1.6 %collective-permute-start = (f32[2,32,128]{2,1,0:T(8,128)S(1)}, f32[2,32,128]{2,1,0:T(8,128)S(1)}, u32[]{:S(2)}, u32[]{:S(2)}) collective-permute-start(f32[2,32,128]{2,1,0:T(8,128)S(1)} %get-tuple-element.48), channel_id=1, source_target_pairs={{0,32},{16,48},{32,0},{48,16},{64,96},{80,112},{96,64},{112,80},{1... | collective-permute-start | bytes 98312 | tf_op jit(solution)/shard_map/ppermute | solution.py:438
  28.1 2.1 %collective-permute-start.2 = (f32[2,16,128]{2,1,0:T(8,128)S(1)}, f32[2,16,128]{2,1,0:T(8,128)S(1)}, u32[]{:S(2)}, u32[]{:S(2)}) collective-permute-start(f32[2,16,128]{2,1,0:T(8,128)S(1)} %get-tuple-element.49), channel_id=1, source_target_pairs={{0,96},{16,112},{32,64},{48,80},{64,32},{80,48},{96,0},{112,16},{1... | collective-permute-start | bytes 49160 | tf_op jit(solution)/shard_map/ppermute | solution.py:438
  30.2 0.7 collective-permute-start.1
  30.8 2.2 %collective-permute-done.2 = f32[2,16,128]{2,1,0:T(8,128)S(1)} collective-permute-done((f32[2,16,128]{2,1,0:T(8,128)S(1)}, f32[2,16,128]{2,1,0:T(8,128)S(1)}, u32[]{:S(2)}, u32[]{:S(2)}) %collective-permute-start.2) | collective-permute-done | bytes 16416 | tf_op jit(solution)/shard_map/ppermute | solution.py:438
  33.0 0.0 collective-permute-start.6
  33.0 2.4 %collective-permute-done.1 = f32[2,16,128]{2,1,0:T(8,128)S(1)} collective-permute-done((f32[2,16,128]{2,1,0:T(8,128)S(1)}, f32[2,16,128]{2,1,0:T(8,128)S(1)}, u32[]{:S(2)}, u32[]{:S(2)}) %collective-permute-start.1) | collective-permute-done | bytes 16416 | tf_op jit(solution)/shard_map/ppermute | solution.py:438
  35.4 2.2 %collective-permute-start.3 = (f32[2,128,128]{2,1,0:T(8,128)S(1)}, f32[2,128,128]{2,1,0:T(8,128)S(1)}, u32[]{:S(2)}, u32[]{:S(2)}) collective-permute-start(f32[2,128,128]{2,1,0:T(8,128)S(1)} %get-tuple-element.50), channel_id=1, source_target_pairs={{0,12},{1,13},{2,14},{3,15},{4,8},{5,9},{6,10},{7,11},{8,4},{9,5},... | collective-permute-start | bytes 393224 | tf_op jit(solution)/shard_map/ppermute | solution.py:438
  37.6 0.0 collective-permute-done
  37.6 0.0 collective-permute-done.6
  37.6 4.0 %collective-permute-done.3.kv6_ref = f32[2,128,128]{2,1,0:T(8,128)S(1)} collective-permute-done((f32[2,128,128]{2,1,0:T(8,128)S(1)}, f32[2,128,128]{2,1,0:T(8,128)S(1)}, u32[]{:S(2)}, u32[]{:S(2)}) %collective-permute-start.3) | collective-permute-done | bytes 131104 | tf_op jit(solution)/shard_map/ppermute | solution.py:438
  41.6 0.0 collective-permute-done.5.kv4a_ref
  41.6 0.0 collective-permute-done.4.mean_ref
  41.6 1.2 %collective-permute-done.7 = f32[2,64,128]{2,1,0:T(8,128)S(1)} collective-permute-done((f32[2,64,128]{2,1,0:T(8,128)S(1)}, f32[2,64,128]{2,1,0:T(8,128)S(1)}, u32[]{:S(2)}, u32[]{:S(2)}) %collective-permute-start.7) | collective-permute-done | bytes 65568 | tf_op jit(solution)/shard_map/ppermute | solution.py:438
  42.9 2.3 %collective-permute-start.8 = (f32[2,192,128]{2,1,0:T(8,128)S(1)}, f32[2,192,128]{2,1,0:T(8,128)S(1)}, u32[]{:S(2)}, u32[]{:S(2)}) collective-permute-start(f32[2,192,128]{2,1,0:T(8,128)S(1)} %slice_dynamic-update-slice_fusion.near_ref), channel_id=1, source_target_pairs={{0,12},{1,13},{2,14},{3,15},{4,8},{5,9},{6,10},{7,11},{8,4},{9,5},... | collective-permute-start | bytes 589832 | tf_op jit(solution)/shard_map/ppermute | solution.py:438
  45.1 1.8 %collective-permute-start.9 = (f32[2,64,1024]{2,1,0:T(8,128)S(1)}, f32[2,64,1024]{2,1,0:T(8,128)S(1)}, u32[]{:S(2)}, u32[]{:S(2)}) collective-permute-start(f32[2,64,1024]{2,1,0:T(8,128)S(1)} %copy-done), channel_id=1, source_target_pairs={{0,1},{1,0},{2,3},{3,2},{4,5},{5,4},{6,7},{7,6},{8,9},{9,8},{10,11... | collective-permute-start | bytes 1572872 | tf_op jit(solution)/shard_map/ppermute | solution.py:438
  46.9 0.1 collective-permute-start.10
  47.0 4.1 %collective-permute-done.8.across_ref = f32[2,192,128]{2,1,0:T(8,128)S(1)} collective-permute-done((f32[2,192,128]{2,1,0:T(8,128)S(1)}, f32[2,192,128]{2,1,0:T(8,128)S(1)}, u32[]{:S(2)}, u32[]{:S(2)}) %collective-permute-start.8) | collective-permute-done | bytes 196640 | tf_op jit(solution)/shard_map/ppermute | solution.py:438
  51.1 1.8 %far_levels.1 = f32[8,64,128]{2,1,0:T(8,128)} custom-call(f32[8,96,128]{2,1,0:T(8,128)S(1)} %all-to-all-done.got_ref, f32[2,128,128]{2,1,0:T(8,128)S(1)} %collective-permute-done.3.kv6_ref, f32[2,192,128]{2,1,0:T(8,128)S(1)} %slice_dynamic-update-slice_fusion.near_ref, f32[2,192,128]{2,1,0:T(8,128)S(1)} %collective-permute-done.8.across_ref), custom_call_target="tpu_custom_call" | custom-call | flops 104857600 | bytes 1048576 | tf_op jit(solution)/shard_map/far_levels/pallas_call | solution.py:347
  52.9 3.6 %all-to-all-start.1 = ((f32[8,64,128]{2,1,0:T(8,128)}), f32[8,64,128]{2,1,0:T(8,128)S(1)}, u32[]{:S(2)}, u32[]{:S(2)}) async-start(f32[8,64,128]{2,1,0:T(8,128)} %far_levels.1), calls=%async_computation.1 | async-start | bytes 524288 | tf_op jit(solution)/shard_map/all_to_all | solution.py:442
  56.5 11.6 %local_levels.5 = (f32[1024,640]{1,0:T(8,128)}, f32[1024,128]{1,0:T(8,128)}) custom-call(f32[1024,1024]{1,0:T(8,128)} %q_ref.3, f32[1024,1024]{1,0:T(8,128)} %k_ref.4, f32[1024,1024]{1,0:T(8,128)} %v_ref.4), custom_call_target="tpu_custom_call" | custom-call | flops 5368709120 | bytes 10485760 | tf_op jit(solution)/shard_map/local_levels/pallas_call | solution.py:199
  68.1 0.0 collective-permute-done.10.kv4b_ref
  68.1 3.2 %near_levels.1 = (f32[128,1024]{1,0:T(8,128)}, f32[128,128]{1,0:T(8,128)}) custom-call(f32[128,1024]{1,0:T(8,128)} %get-tuple-element.63.q3_ref, f32[2,64,1024]{2,1,0:T(8,128)S(1)} %collective-permute-done.4.mean_ref, f32[2,64,1024]{2,1,0:T(8,128)S(1)} %collective-permute-done.9.half_ref, f32[2,64,1024]{2,1,0:T(8,128)S(1)} %collective-permute-done.5.kv4a_ref, ...), custom_call_target="tpu_custom_call" | custom-call | flops 419430400 | bytes 4194304 | tf_op jit(solution)/shard_map/near_levels/pallas_call | solution.py:251
  71.3 0.0 all-to-all-done.1.refs_8_
  71.3 6.8 %join_levels.1 = f32[1024,1024]{1,0:T(8,128)} custom-call(f32[1024,256]{1,0:T(8,128)} %get-tuple-element.41.refs_0_, f32[1024,128]{1,0:T(8,128)} %get-tuple-element.46.refs_1_, f32[1024,640]{1,0:T(8,128)} %get-tuple-element.59.refs_2_, f32[1024,128]{1,0:T(8,128)} %get-tuple-element.60.refs_3_, f32[1024,128]{1,0:T(8,128)} %get-tuple-element.61.refs_4_, ...), custom_call_target="tpu_custom_call" | custom-call | flops 16777216 | bytes 9437184 | tf_op jit(solution)/shard_map/join_levels/pallas_call | solution.py:415
  (12 shorter events, 0.0 us)
Async XLA Ops:
  6.3 20.1 %all-to-all-start = ((f32[8,96,128]{2,1,0:T(8,128)}), f32[8,96,128]{2,1,0:T(8,128)S(1)}, u32[]{:S(2)}, u32[]{:S(2)}) async-start(f32[8,96,128]{2,1,0:T(8,128)} %get-tuple-element.42), calls=%async_computation | async-start | bytes 786432 | tf_op jit(solution)/shard_map/all_to_all | solution.py:442
  12.7 6.0 %copy-start.1 = (f32[2,64,1024]{2,1,0:T(8,128)S(1)}, f32[2,64,1024]{2,1,0:T(8,128)}, u32[]{:S(2)}) copy-start(f32[2,64,1024]{2,1,0:T(8,128)} %get-tuple-element.51) | copy-start | bytes 1572868
  18.7 26.4 %copy-start = (f32[2,64,1024]{2,1,0:T(8,128)S(1)}, f32[2,64,1024]{2,1,0:T(8,128)}, u32[]{:S(2)}) copy-start(f32[2,64,1024]{2,1,0:T(8,128)} %get-tuple-element.65) | copy-start | bytes 1572868
  18.7 22.8 %collective-permute-start.5 = (f32[2,64,1024]{2,1,0:T(8,128)S(1)}, f32[2,64,1024]{2,1,0:T(8,128)S(1)}, u32[]{:S(2)}, u32[]{:S(2)}) collective-permute-start(f32[2,64,1024]{2,1,0:T(8,128)S(1)} %copy-done.1), channel_id=1, source_target_pairs={{0,3},{1,2},{2,1},{3,0},{4,7},{5,6},{6,5},{7,4},{8,11},{9,10},{10,... | collective-permute-start | bytes 1572872 | tf_op jit(solution)/shard_map/ppermute | solution.py:438
  22.1 19.5 %collective-permute-start.4 = (f32[2,64,1024]{2,1,0:T(8,128)S(1)}, f32[2,64,1024]{2,1,0:T(8,128)S(1)}, u32[]{:S(2)}, u32[]{:S(2)}) collective-permute-start(f32[2,64,1024]{2,1,0:T(8,128)S(1)} %copy-done.1), channel_id=1, source_target_pairs={{0,1},{1,0},{2,3},{3,2},{4,5},{5,4},{6,7},{7,6},{8,9},{9,8},{10,11... | collective-permute-start | bytes 1572872 | tf_op jit(solution)/shard_map/ppermute | solution.py:438
  26.5 11.1 %collective-permute-start = (f32[2,32,128]{2,1,0:T(8,128)S(1)}, f32[2,32,128]{2,1,0:T(8,128)S(1)}, u32[]{:S(2)}, u32[]{:S(2)}) collective-permute-start(f32[2,32,128]{2,1,0:T(8,128)S(1)} %get-tuple-element.48), channel_id=1, source_target_pairs={{0,32},{16,48},{32,0},{48,16},{64,96},{80,112},{96,64},{112,80},{1... | collective-permute-start | bytes 98312 | tf_op jit(solution)/shard_map/ppermute | solution.py:438
  28.1 4.9 %collective-permute-start.2 = (f32[2,16,128]{2,1,0:T(8,128)S(1)}, f32[2,16,128]{2,1,0:T(8,128)S(1)}, u32[]{:S(2)}, u32[]{:S(2)}) collective-permute-start(f32[2,16,128]{2,1,0:T(8,128)S(1)} %get-tuple-element.49), channel_id=1, source_target_pairs={{0,96},{16,112},{32,64},{48,80},{64,32},{80,48},{96,0},{112,16},{1... | collective-permute-start | bytes 49160 | tf_op jit(solution)/shard_map/ppermute | solution.py:438
  30.2 5.2 %collective-permute-start.1 = (f32[2,16,128]{2,1,0:T(8,128)S(1)}, f32[2,16,128]{2,1,0:T(8,128)S(1)}, u32[]{:S(2)}, u32[]{:S(2)}) collective-permute-start(f32[2,16,128]{2,1,0:T(8,128)S(1)} %get-tuple-element.49), channel_id=1, source_target_pairs={{0,64},{16,80},{32,96},{48,112},{64,0},{80,16},{96,32},{112,48},{1... | collective-permute-start | bytes 49160 | tf_op jit(solution)/shard_map/ppermute | solution.py:438
  33.0 4.6 %collective-permute-start.6 = (f32[2,64,128]{2,1,0:T(8,128)S(1)}, f32[2,64,128]{2,1,0:T(8,128)S(1)}, u32[]{:S(2)}, u32[]{:S(2)}) collective-permute-start(f32[2,64,128]{2,1,0:T(8,128)S(1)} %get-tuple-element.54), channel_id=1, source_target_pairs={{0,16},{16,0},{32,48},{48,32},{64,80},{80,64},{96,112},{112,96},{1... | collective-permute-start | bytes 196616 | tf_op jit(solution)/shard_map/ppermute | solution.py:438
  35.4 6.2 %collective-permute-start.3 = (f32[2,128,128]{2,1,0:T(8,128)S(1)}, f32[2,128,128]{2,1,0:T(8,128)S(1)}, u32[]{:S(2)}, u32[]{:S(2)}) collective-permute-start(f32[2,128,128]{2,1,0:T(8,128)S(1)} %get-tuple-element.50), channel_id=1, source_target_pairs={{0,12},{1,13},{2,14},{3,15},{4,8},{5,9},{6,10},{7,11},{8,4},{9,5},... | collective-permute-start | bytes 393224 | tf_op jit(solution)/shard_map/ppermute | solution.py:438
  41.6 1.3 %collective-permute-start.7 = (f32[2,64,128]{2,1,0:T(8,128)S(1)}, f32[2,64,128]{2,1,0:T(8,128)S(1)}, u32[]{:S(2)}, u32[]{:S(2)}) collective-permute-start(f32[2,64,128]{2,1,0:T(8,128)S(1)} %pad_maximum_fusion), channel_id=1, source_target_pairs={{0,16},{16,0},{32,48},{48,32},{64,80},{80,64},{96,112},{112,96},{1... | collective-permute-start | bytes 196616 | tf_op jit(solution)/shard_map/ppermute | solution.py:438
  42.9 8.2 %collective-permute-start.8 = (f32[2,192,128]{2,1,0:T(8,128)S(1)}, f32[2,192,128]{2,1,0:T(8,128)S(1)}, u32[]{:S(2)}, u32[]{:S(2)}) collective-permute-start(f32[2,192,128]{2,1,0:T(8,128)S(1)} %slice_dynamic-update-slice_fusion.near_ref), channel_id=1, source_target_pairs={{0,12},{1,13},{2,14},{3,15},{4,8},{5,9},{6,10},{7,11},{8,4},{9,5},... | collective-permute-start | bytes 589832 | tf_op jit(solution)/shard_map/ppermute | solution.py:438
  45.1 22.9 %collective-permute-start.9 = (f32[2,64,1024]{2,1,0:T(8,128)S(1)}, f32[2,64,1024]{2,1,0:T(8,128)S(1)}, u32[]{:S(2)}, u32[]{:S(2)}) collective-permute-start(f32[2,64,1024]{2,1,0:T(8,128)S(1)} %copy-done), channel_id=1, source_target_pairs={{0,1},{1,0},{2,3},{3,2},{4,5},{5,4},{6,7},{7,6},{8,9},{9,8},{10,11... | collective-permute-start | bytes 1572872 | tf_op jit(solution)/shard_map/ppermute | solution.py:438
  46.9 21.2 %collective-permute-start.10 = (f32[2,64,1024]{2,1,0:T(8,128)S(1)}, f32[2,64,1024]{2,1,0:T(8,128)S(1)}, u32[]{:S(2)}, u32[]{:S(2)}) collective-permute-start(f32[2,64,1024]{2,1,0:T(8,128)S(1)} %collective-permute-done.4.mean_ref), channel_id=1, source_target_pairs={{0,3},{1,2},{2,1},{3,0},{4,7},{5,6},{6,5},{7,4},{8,11},{9,10},{10,... | collective-permute-start | bytes 1572872 | tf_op jit(solution)/shard_map/ppermute | solution.py:438
  52.9 18.4 %all-to-all-start.1 = ((f32[8,64,128]{2,1,0:T(8,128)}), f32[8,64,128]{2,1,0:T(8,128)S(1)}, u32[]{:S(2)}, u32[]{:S(2)}) async-start(f32[8,64,128]{2,1,0:T(8,128)} %far_levels.1), calls=%async_computation.1 | async-start | bytes 524288 | tf_op jit(solution)/shard_map/all_to_all | solution.py:442

commit v3 on v2

v3 whole, which is shorter than its diff:
```python
import functools
import math

import jax
import jax.numpy as jnp
from jax import lax
from jax.experimental import pallas as pl
from jax.experimental.pallas import tpu as pltpu
from jax.sharding import PartitionSpec as P

HEADS = 8
PACK = 208
BACK = 72
CALLS = (4, 2, 2)
WIDTH = 128
ROWS = 1024
F32 = jnp.float32
BF16 = jnp.bfloat16
SCALE = WIDTH ** (-0.5) / math.log(2.0)
MIB = 1024 * 1024

GROUPS = [list(range(8)), [12, 13, 14, 15, 8, 9, 10, 11]]


def params(mib=12):
    return pltpu.CompilerParams(vmem_limit_bytes=mib * MIB)


def in_hbm(x):
    return pltpu.with_memory_space_constraint(x, pltpu.HBM)


def split(x):
    hi = x.astype(BF16)
    lo = (x - hi.astype(F32)).astype(BF16)
    return hi, lo


def dot_nt(a, b):
    return lax.dot_general(a, b, (((1,), (1,)), ((), ())), preferred_element_type=F32)


def dot_nn(a, b):
    return lax.dot_general(a, b, (((1,), (0,)), ((), ())), preferred_element_type=F32)


def key_side(k):
    hi, lo = split(k)
    return jnp.concatenate([hi, hi], axis=1), jnp.concatenate([lo, jnp.zeros_like(lo)], axis=1)


def scores(q, sides):
    hi, lo = split(q)
    both = jnp.concatenate([hi, lo], axis=1)
    first, second = sides
    n = first.shape[0]
    if n == 128:
        s = dot_nt(both, jnp.concatenate([first, second], axis=0))
        return s[:, :n] + s[:, n:]
    return dot_nt(both, first) + dot_nt(both, second)


def weigh(p, side):
    hi, lo = side
    p_hi, p_lo = split(p)
    if hi.shape[0] == 128:
        left = jnp.concatenate([p_hi, p_lo], axis=1)
        right = jnp.concatenate(
            [jnp.concatenate([hi, lo], axis=1), jnp.concatenate([hi, jnp.zeros_like(lo)], axis=1)], axis=0
        )
        r = dot_nn(left, right)
        return r[:, :WIDTH] + r[:, WIDTH:]
    r = dot_nn(p_hi, jnp.concatenate([hi, lo], axis=1))
    return r[:, :WIDTH] + r[:, WIDTH:] + dot_nn(p_lo, hi)


def attend_all(tasks):
    grids = [scores(q, key_side(k)) for q, k, _, _ in tasks]
    peaks = [jnp.max(s, axis=1, keepdims=True) for s in grids]
    weights = [jnp.exp2(s - peak) for s, peak in zip(grids, peaks)]
    totals = [jnp.sum(p, axis=1, keepdims=True) for p in weights]
    numerators = [weigh(p, split(task[2])) for p, task in zip(weights, tasks)]
    return [(peak + float(task[3]), t, n) for peak, t, n, task in zip(peaks, totals, numerators, tasks)]


def merge(a, b):
    ma, sa, na = a
    mb, sb, nb = b
    m = jnp.maximum(ma, mb)
    fa, fb = jnp.exp2(ma - m), jnp.exp2(mb - m)
    return m, sa * fa + sb * fb, na * fa + nb * fb


def pool_eight(ref):
    total = ref[pl.ds(0, 128, stride=8), :]
    for k in range(1, 8):
        total = total + ref[pl.ds(k, 128, stride=8), :]
    return total


def pool_pairs(ref, n):
    return 0.5 * (ref[pl.ds(0, n, stride=2), :] + ref[pl.ds(1, n, stride=2), :])


def pool_kv_body(k_hbm, v_hbm, k3_hbm, v3_hbm, pay_hbm, x8_ref, x9_ref, rows, three, four, more, sems, sems3, sems4):
    arrays, outs = (k_hbm, v_hbm), (k3_hbm, v3_hbm)

    def cols(h):
        return slice(WIDTH * h, WIDTH * h + WIDTH)

    def fetch(i, h):
        return pltpu.make_async_copy(arrays[i].at[:, cols(h)], rows.at[i, h], sems.at[i, h])

    def send3(i, h):
        return pltpu.make_async_copy(three.at[i, h], outs[i].at[:, cols(h)], sems3.at[i, h])

    def send4(i, h):
        return pltpu.make_async_copy(four.at[i, h], pay_hbm.at[h, 64 * i + 64 : 64 * i + 128, :], sems4.at[i, h])

    every = [(i, h) for h in range(HEADS) for i in range(2)]
    for i, h in every:
        fetch(i, h).start()
    for i, h in every:
        fetch(i, h).wait()
        three[i, h] = 0.125 * pool_eight(rows.at[i, h])
        send3(i, h).start()
        four[i, h] = pool_pairs(three.at[i, h], 64)
        send4(i, h).start()
        x7 = four[i, h, pl.ds(0, 8, stride=8), :]
        for k in range(1, 8):
            x7 = x7 + four[i, h, pl.ds(k, 8, stride=8), :]
        more[i] = 0.125 * x7
        x8 = pool_pairs(more.at[i], 4)
        x8_ref[h, 4 * i : 4 * i + 4, :] = x8
        x9_ref[h, 2 * i : 2 * i + 2, :] = jnp.concatenate(
            [0.5 * (x8[0:1] + x8[1:2]), 0.5 * (x8[2:3] + x8[3:4])], axis=0
        )
    for i, h in every:
        send3(i, h).wait()
        send4(i, h).wait()


def pool_kv_call(k, v):
    anywhere = pl.BlockSpec(memory_space=pl.ANY)
    vmem = pl.BlockSpec(memory_space=pltpu.VMEM)
    return pl.pallas_call(
        pool_kv_body,
        name="pool_keys",
        in_specs=[anywhere] * 2,
        out_specs=[anywhere] * 3 + [vmem] * 2,
        out_shape=[
            pltpu.HBM((128, HEADS * WIDTH), F32),
            pltpu.HBM((128, HEADS * WIDTH), F32),
            pltpu.HBM((HEADS, PACK, WIDTH), F32),
            jax.ShapeDtypeStruct((HEADS, 8, WIDTH), F32),
            jax.ShapeDtypeStruct((HEADS, 4, WIDTH), F32),
        ],
        scratch_shapes=[
            pltpu.VMEM((2, HEADS, ROWS, WIDTH), F32),
            pltpu.VMEM((2, HEADS, 128, WIDTH), F32),
            pltpu.VMEM((2, HEADS, 64, WIDTH), F32),
            pltpu.VMEM((2, 8, WIDTH), F32),
            pltpu.SemaphoreType.DMA((2, HEADS)),
            pltpu.SemaphoreType.DMA((2, HEADS)),
            pltpu.SemaphoreType.DMA((2, HEADS)),
        ],
        compiler_params=params(20),
        cost_estimate=pl.CostEstimate(flops=2 << 20, bytes_accessed=10 << 20, transcendentals=0),
    )(in_hbm(k), in_hbm(v))


def pool_q_body(q_hbm, pay_in, q3_hbm, pay_hbm, rows, three, four, sems, sems3, sems4):
    def cols(h):
        return slice(WIDTH * h, WIDTH * h + WIDTH)

    def fetch(h):
        return pltpu.make_async_copy(q_hbm.at[:, cols(h)], rows.at[h], sems.at[h])

    def send3(h):
        return pltpu.make_async_copy(three.at[h], q3_hbm.at[:, cols(h)], sems3.at[h])

    def send4(h):
        return pltpu.make_async_copy(four.at[h], pay_hbm.at[h, 0:64, :], sems4.at[h])

    for h in range(HEADS):
        fetch(h).start()
    for h in range(HEADS):
        fetch(h).wait()
        three[h] = (0.125 * SCALE) * pool_eight(rows.at[h])
        send3(h).start()
        four[h] = pool_pairs(three.at[h], 64)
        send4(h).start()
    for h in range(HEADS):
        send3(h).wait()
        send4(h).wait()


def pool_q_call(q, pay):
    anywhere = pl.BlockSpec(memory_space=pl.ANY)
    return pl.pallas_call(
        pool_q_body,
        name="pool_queries",
        in_specs=[anywhere] * 2,
        out_specs=[anywhere] * 2,
        out_shape=[pltpu.HBM((128, HEADS * WIDTH), F32), pltpu.HBM((HEADS, PACK, WIDTH), F32)],
        input_output_aliases={1: 1},
        scratch_shapes=[
            pltpu.VMEM((HEADS, ROWS, WIDTH), F32),
            pltpu.VMEM((HEADS, 128, WIDTH), F32),
            pltpu.VMEM((HEADS, 64, WIDTH), F32),
            pltpu.SemaphoreType.DMA((HEADS,)),
            pltpu.SemaphoreType.DMA((HEADS,)),
            pltpu.SemaphoreType.DMA((HEADS,)),
        ],
        compiler_params=params(),
        cost_estimate=pl.CostEstimate(flops=2 << 30, bytes_accessed=5 << 20, transcendentals=0),
    )(in_hbm(q), in_hbm(pay))


def pack_body(pay_hbm, r8_ref, r9a_ref, r9b_ref, out_hbm, rows, sem):
    rows[:, 0:8, :] = r8_ref[...]
    rows[:, 8:12, :] = r9a_ref[...]
    rows[:, 12:16, :] = r9b_ref[...]
    copy = pltpu.make_async_copy(rows, out_hbm.at[:, 192:208, :], sem)
    copy.start()
    copy.wait()


def pack_call(pay, r8, r9a, r9b):
    vmem = pl.BlockSpec(memory_space=pltpu.VMEM)
    anywhere = pl.BlockSpec(memory_space=pl.ANY)
    return pl.pallas_call(
        pack_body,
        name="pack_rows",
        in_specs=[anywhere, vmem, vmem, vmem],
        out_specs=anywhere,
        out_shape=pltpu.HBM((HEADS, PACK, WIDTH), F32),
        input_output_aliases={0: 0},
        scratch_shapes=[pltpu.VMEM((HEADS, 16, WIDTH), F32), pltpu.SemaphoreType.DMA],
        compiler_params=params(4),
        cost_estimate=pl.CostEstimate(flops=0, bytes_accessed=1 << 17, transcendentals=0),
    )(in_hbm(pay), r8, r9a, r9b)


def local_body(first, q_ref, k_ref, v_ref, o_ref, lse_ref):
    head = pl.program_id(0) + first

    def load(ref):
        return [ref[pl.ds(k, 128, stride=8), :] for k in range(8)]

    def pool(parts):
        return [0.5 * (parts[2 * i] + parts[2 * i + 1]) for i in range(len(parts) // 2)]

    def rows(parts, begin, count):
        return jnp.concatenate([x[begin : begin + count] for x in parts], axis=0)

    q0 = [x * SCALE for x in load(q_ref)]
    k0, v0 = load(k_ref), load(v_ref)
    q1, k1, v1 = pool(q0), pool(k0), pool(v0)
    q2, k2, v2 = pool(q1), pool(k1), pool(v1)
    tasks = []
    for b in range(2):
        c = 64 * (b ^ 1)
        tasks.append((rows(q2, 64 * b, 64), rows(k2, c, 64), rows(v2, c, 64), 2))
    for p in range(4):
        c = 32 * (p ^ 1)
        tasks.append((rows(q1, 32 * p, 32), rows(k1, c, 32), rows(v1, c, 32), 1))
    for p in range(4):
        c = 32 * p
        tasks.append((rows(q0, c, 32), rows(k0, c, 32), rows(v0, c, 32), 0))
    done = attend_all(tasks)
    at2, at1, at0 = done[:2], done[2:6], done[6:]

    lane = lax.broadcasted_iota(jnp.int32, (128, WIDTH), 1)
    lses = [[None] * 4 for _ in range(8)]
    for p in range(4):
        off = 32 * (p % 2)
        for j in range(4):
            i = j // 2
            one = tuple(x[32 * j : 32 * j + 32] for x in at1[p])
            two = tuple(x[64 * i + off : 64 * i + off + 32] for x in at2[p // 2])
            coarse = merge(one, two)
            for k in (2 * j, 2 * j + 1):
                m, s, n = merge(tuple(x[32 * k : 32 * k + 32] for x in at0[p]), coarse)
                o_ref[128 * k + 32 * p : 128 * k + 32 * p + 32, :] = n / s
                lses[k][p] = m + jnp.log2(s)
    for k in range(8):
        old = lse_ref[128 * k : 128 * k + 128, :]
        lse_ref[128 * k : 128 * k + 128, :] = jnp.where(lane == head, jnp.concatenate(lses[k], axis=0), old)


def local_call(q, k, v, first, count):
    block = pl.BlockSpec((ROWS, WIDTH), lambda h: (0, h + first))
    return pl.pallas_call(
        functools.partial(local_body, first),
        name="local_levels",
        grid=(count,),
        in_specs=[block] * 3,
        out_specs=[pl.BlockSpec((ROWS, WIDTH), lambda h: (0, h)), pl.BlockSpec((ROWS, WIDTH), lambda h: (0, 0))],
        out_shape=[
            pltpu.HBM((ROWS, count * WIDTH), F32),
            pltpu.HBM((ROWS, WIDTH), F32),
        ],
        compiler_params=params(16),
        cost_estimate=pl.CostEstimate(
            flops=(count << 30), bytes_accessed=count << 21, transcendentals=count << 19
        ),
    )(in_hbm(q), in_hbm(k), in_hbm(v))


def rise_body(got_ref, six_ref, seven_ref, scratch):
    for i in range(2):
        for s in range(8):
            scratch[i, 64 * s : 64 * s + 64, :] = got_ref[s, 64 * (i + 1) : 64 * (i + 2), :]
            scratch[i, 640 + 4 * s : 644 + 4 * s, :] = got_ref[s, 192 + 4 * i : 196 + 4 * i, :]
            for j in range(2):
                begin = 200 + 4 * j + 2 * i
                place = 672 + 16 * j + 2 * s
                scratch[i, place : place + 2, :] = got_ref[s, begin : begin + 2, :]
        x6 = scratch[i, pl.ds(0, 128, stride=4), :]
        for k in range(1, 4):
            x6 = x6 + scratch[i, pl.ds(k, 128, stride=4), :]
        x6 = 0.25 * x6
        scratch[i, 512:640, :] = x6
        six_ref[i, 0:128, :] = x6
        seven_ref[i, 0:64, :] = 0.5 * (
            scratch[i, pl.ds(512, 64, stride=2), :] + scratch[i, pl.ds(513, 64, stride=2), :]
        )
        six_ref[i, 128:192, :] = scratch[i, 640:704, :]
        seven_ref[i, 64:128, :] = scratch[i, 640:704, :]


def rise_call(got):
    return pl.pallas_call(
        rise_body,
        name="rise_rows",
        out_shape=[jax.ShapeDtypeStruct((2, n, WIDTH), F32) for n in (192, 128)],
        scratch_shapes=[pltpu.VMEM((2, 704, WIDTH), F32)],
        compiler_params=params(),
        cost_estimate=pl.CostEstimate(flops=1 << 18, bytes_accessed=1 << 19, transcendentals=0),
    )(got)


def far_body(got_ref, here_ref, six_ref, core_ref, seven_ref, out_ref, scratch, es):
    def gather(i, sources):
        return jnp.concatenate([got_ref[s, 64 * i : 64 * i + 64, :] for s in sources], axis=0)

    def halve(i, base, count):
        return 0.5 * (scratch[i, pl.ds(base, count, stride=2), :] + scratch[i, pl.ds(base + 1, count, stride=2), :])

    for i in range(3):
        scratch[i, 0:512, :] = gather(i, range(8))
        base, count = 0, 256
        while count >= (16 if i == 0 else 256):
            x = halve(i, base, count)
            base = base + 2 * count
            scratch[i, base : base + count, :] = x
            count = count // 2

    def sibling(i, level):
        if level == 6:
            return six_ref[i, 0:128, :]
        if level == 7:
            return jnp.concatenate([core_ref[i, 0:64, :], seven_ref[i, 0:64, :]], axis=0)
        low = 64 + 32 * (level - 8)
        return jnp.concatenate(
            [
                here_ref[i, 64 + low : 96 + low, :],
                core_ref[i, low : low + 32, :],
                six_ref[i, 64 + low : 96 + low, :],
                seven_ref[i, low : low + 32, :],
            ],
            axis=0,
        )

    tasks = []
    for level, base, blocks in ((4, 0, 4), (5, 512, 2)):
        for g in range(blocks):
            mine = slice(base + 128 * g, base + 128 * g + 128)
            other = slice(base + 128 * (g ^ 1), base + 128 * (g ^ 1) + 128)
            tasks.append((scratch[0, mine, :], scratch[1, other, :], scratch[2, other, :], level))
    base, count = 768, 128
    for level in range(6, 10):
        tasks.append((scratch[0, base : base + count, :], sibling(0, level), sibling(1, level), level))
        base, count = base + count, count // 2
    done = attend_all(tasks)
    levels = []
    for few in (done[0:4], done[4:6]):
        levels.append(tuple(jnp.concatenate(x, axis=0) for x in zip(*few)))
    levels.extend(done[6:])
    running = levels[-1]
    base = 0
    for finer in reversed(levels[:-1]):
        n = running[0].shape[0]
        wide = []
        for i, x in enumerate(running):
            x = jnp.broadcast_to(x, (n, WIDTH))
            es[i, pl.ds(base, n, stride=2), :] = x
            es[i, pl.ds(base + 1, n, stride=2), :] = x
            wide.append(es[i, base : base + 2 * n, :])
        base = base + 2 * n
        running = merge(finer, tuple(wide))
    m, s, n = running
    o = n / s
    lse = jnp.broadcast_to(m + jnp.log2(s), (512, WIDTH))
    for g in range(4):
        row = jnp.transpose(lse[128 * g : 128 * g + 128])[0:8]
        for d in range(2):
            out_ref[2 * g + d, 0:64, :] = o[128 * g + 64 * d : 128 * g + 64 * d + 64]
            out_ref[2 * g + d, 64:72, :] = row if d == 0 else pltpu.roll(row, 64, 1)


def far_call(got, here, six, core, seven):
    return pl.pallas_call(
        far_body,
        name="far_levels",
        out_shape=pltpu.HBM((HEADS, BACK, WIDTH), F32),
        scratch_shapes=[pltpu.VMEM((3, 1024, WIDTH), F32), pltpu.VMEM((3, 1024, WIDTH), F32)],
        compiler_params=params(),
        cost_estimate=pl.CostEstimate(flops=100 << 20, bytes_accessed=1 << 20, transcendentals=1 << 17),
    )(got, here, six, core, seven)


def near_body(q3_ref, k3_ref, v3_ref, o_ref, lse_ref):
    lane = lax.broadcasted_iota(jnp.int32, (128, WIDTH), 1)
    packed = jnp.zeros((128, WIDTH), F32)
    cols = [slice(WIDTH * h, WIDTH * h + WIDTH) for h in range(HEADS)]
    done = attend_all([(q3_ref[:, c], k3_ref[:, c], v3_ref[:, c], 3) for c in cols])
    for h, (m, s, n) in enumerate(done):
        o_ref[:, cols[h]] = n / s
        packed = jnp.where(lane == h, m + jnp.log2(s), packed)
    lse_ref[...] = packed


def near_call(q3, k3, v3):
    return pl.pallas_call(
        near_body,
        name="near_level",
        out_shape=[pltpu.HBM((128, HEADS * WIDTH), F32), pltpu.HBM((128, WIDTH), F32)],
        compiler_params=params(),
        cost_estimate=pl.CostEstimate(flops=200 << 20, bytes_accessed=2 << 20, transcendentals=1 << 17),
    )(in_hbm(q3), k3, v3)


def share(a, b):
    return 1.0 / (1.0 + jnp.exp2(b - a))


def join_body(*refs):
    n = len(CALLS)
    own_hbm, own_lse_hbm = refs[:n], refs[n : 2 * n]
    o3_hbm, lse3_hbm, far_ref, out_hbm = refs[2 * n : 2 * n + 4]
    own, own_lse, o3, lse3, wide, stage, own_sems, sems, out_sems = refs[2 * n + 4 :]
    place = [(c, i) for c, count in enumerate(CALLS) for i in range(count)]

    def columns(h):
        return slice(WIDTH * h, WIDTH * h + WIDTH)

    def fetch(h):
        c, i = place[h]
        return pltpu.make_async_copy(own_hbm[c].at[:, columns(i)], own.at[h], own_sems.at[h])

    def send(h):
        return pltpu.make_async_copy(stage.at[h % 4], out_hbm.at[:, columns(h)], out_sems.at[h % 4])

    fetch(0).start()
    others = [pltpu.make_async_copy(lse3_hbm, lse3, sems.at[0]), pltpu.make_async_copy(o3_hbm, o3, sems.at[1])]
    others += [pltpu.make_async_copy(own_lse_hbm[c], own_lse.at[c], sems.at[c + 2]) for c in range(n)]
    for copy in others:
        copy.start()
    for h in range(1, HEADS):
        fetch(h).start()
    for copy in others:
        copy.wait()

    for h in range(HEADS):
        lse = jnp.transpose(jnp.broadcast_to(far_ref[h, 64:65, :], (128, WIDTH)))[0:64]
        for i, x in enumerate((far_ref[h, 0:64, :], lse)):
            for c in range(2):
                wide[h % 2, i, pl.ds(c, 64, stride=2), :] = x
        far_o, far_lse = wide[h % 2, 0], wide[h % 2, 1]
        near_lse = jnp.broadcast_to(lse3[:, h : h + 1], (128, WIDTH))
        top = jnp.maximum(far_lse, near_lse)
        rest_lse = top + jnp.log2(jnp.exp2(far_lse - top) + jnp.exp2(near_lse - top))
        rest = far_o + (o3[:, columns(h)] - far_o) * share(near_lse, far_lse)
        fetch(h).wait()
        if h >= 4:
            send(h - 4).wait()
        for k in range(8):
            part = slice(128 * k, 128 * k + 128)
            lse = jnp.broadcast_to(own_lse[place[h][0], part, h : h + 1], (128, WIDTH))
            stage[h % 4, pl.ds(k, 128, stride=8), :] = rest + (own[h, part, :] - rest) * share(lse, rest_lse)
        send(h).start()
    for h in range(HEADS - 4, HEADS):
        send(h).wait()


def join_call(own, o3, lse3, far):
    n = len(CALLS)
    anywhere = pl.BlockSpec(memory_space=pl.ANY)
    return pl.pallas_call(
        join_body,
        name="join_levels",
        in_specs=[anywhere] * (2 * n + 2) + [pl.BlockSpec(memory_space=pltpu.VMEM)],
        out_specs=anywhere,
        out_shape=pltpu.HBM((ROWS, HEADS * WIDTH), F32),
        scratch_shapes=[
            pltpu.VMEM((HEADS, ROWS, WIDTH), F32),
            pltpu.VMEM((n, ROWS, WIDTH), F32),
            pltpu.VMEM((128, HEADS * WIDTH), F32),
            pltpu.VMEM((128, WIDTH), F32),
            pltpu.VMEM((2, 2, 128, WIDTH), F32),
            pltpu.VMEM((4, ROWS, WIDTH), F32),
            pltpu.SemaphoreType.DMA((HEADS,)),
            pltpu.SemaphoreType.DMA((n + 2,)),
            pltpu.SemaphoreType.DMA((4,)),
        ],
        compiler_params=params(20),
        cost_estimate=pl.CostEstimate(flops=16 << 20, bytes_accessed=9 << 20, transcendentals=1 << 20),
    )(*[in_hbm(o) for o, _ in own], *[in_hbm(lse) for _, lse in own], in_hbm(o3), in_hbm(lse3), far)


def hop(x, axis, flip):
    return lax.ppermute(x, axis, [(i, i ^ flip) for i in range(lax.axis_size(axis))])


def transpose_heads(x):
    return lax.all_to_all(x, "node", 0, 0, axis_index_groups=GROUPS, tiled=True)


def on_device(queries, keys, values):
    k3, v3, pay, x8, x9 = pool_kv_call(keys, values)
    first = [sum(CALLS[:i]) for i in range(len(CALLS))]
    local = []

    def local_part(i, *after):
        q, k, v = lax.optimization_barrier((queries, keys, values) + after)[:3]
        return local_call(q, k, v, first[i], CALLS[i])

    r8, r9a, r9b = hop(x8, "seq", 2), hop(x9, "seq", 4), hop(x9, "seq", 6)
    q3, pay = pool_q_call(queries, pay)
    pay = pack_call(pay, r8, r9a, r9b)
    got = transpose_heads(pay)
    part = local_part(0, pay)
    got, part = lax.optimization_barrier((got, part))
    local.append(part)
    _, k3, v3 = lax.optimization_barrier((part, k3, v3))
    sib_k3, sib_v3 = hop(k3, "node", 1), hop(v3, "node", 1)

    here6, here7 = rise_call(got)
    six = hop(here6, "node", 12)
    core = hop(here7, "seq", 1)
    seven = hop(core, "node", 12)
    part = local_part(1, core)
    six, seven, part = lax.optimization_barrier((six, seven, part))
    local.append(part)

    far = far_call(got, here6, six, core, seven)
    back = transpose_heads(far)
    local.append(local_part(2, far))
    o3, lse3 = near_call(q3, sib_k3, sib_v3)
    return join_call(local, o3, lse3, back)


def solution(mesh):
    spec = P(("seq", "node"), None)
    return jax.shard_map(on_device, mesh=mesh, in_specs=(spec, spec, spec), out_specs=spec, check_vma=False)
```

time: 78.9 us -> 68.9 us (0.87)
  waiting for transfers between devices: 13.9 us -> 6.05 us
  starting transfers between devices: 24.2 us -> 19.5 us
  Pallas kernels: 39.9 us -> 42.6 us
    ppermute x11 -> x8, waiting for transfers between devices: 13.9 us -> 4.42 us  [hop(): lax.ppermute(x, axis, [(i, i ^ flip) for i in range(lax.axis_size(axis))])]
    ppermute x11 -> x8, starting transfers between devices: 14.2 us -> 9.6 us  [hop(): lax.ppermute(x, axis, [(i, i ^ flip) for i in range(lax.axis_size(axis))])]
    pallas_call x3 -> x5, Pallas kernels: 11.3 us -> 14.4 us  [the longest x1 4.99 us: pool_kv_call(): pl.pallas_call(pool_kv_body, name='pool_keys', in_specs=[anywhere] * 2, o...]
    all_to_all x2, waiting for transfers between devices: 0.01 us -> 1.63 us  [transpose_heads(): return lax.all_to_all(x, 'node', 0, 0, axis_index_groups=GROUPS, tiled=True)]
  transfers between devices with their start and end apart: 13 -> 10, of which waited for: 5 -> 4; matrix products, arithmetic and copies ran while one was open for 0% -> 0% of each run, Pallas kernels for 34% -> 45%
where the time goes in v3:
time: 68.9 us; the launch traced here: 68.5 us
  Pallas kernels  42.6 us (62%)
  starting transfers between devices  19.5 us (28%)
  waiting for transfers between devices  6.05 us (9%)
    pallas_call x3, Pallas kernels, local_call(): pl.pallas_call(functools.partial(local_body, first), name='local_levels',...  22 us
    all_to_all x2, starting transfers between devices, transpose_heads(): return lax.all_to_all(x, 'node', 0, 0, axis_index_groups=GROUPS, tiled=True)  9.94 us
    ppermute x8, starting transfers between devices, hop(): lax.ppermute(x, axis, [(i, i ^ flip) for i in range(lax.axis_size(axis))])  9.6 us
    pallas_call x1, Pallas kernels, join_call(): pl.pallas_call(join_body, name='join_levels', in_specs=[anywhere] * (2 *...  6.16 us
    pallas_call x1, Pallas kernels, pool_kv_call(): pl.pallas_call(pool_kv_body, name='pool_keys', in_specs=[anywhere] * 2, o...  4.99 us
    ppermute x8, waiting for transfers between devices, hop(): lax.ppermute(x, axis, [(i, i ^ flip) for i in range(lax.axis_size(axis))])  4.42 us
    pallas_call x1, Pallas kernels, pool_q_call(): pl.pallas_call(pool_q_body, name='pool_queries', in_specs=[anywhere] * 2,...  3.2 us
    pallas_call x1, Pallas kernels, far_call(): pl.pallas_call(far_body, name='far_levels', out_shape=pltpu.HBM((HEADS, B...  2.9 us
  transfers between devices with their start and end apart: 10, of which 4 were waited for; matrix products, arithmetic and copies ran while one was open for 0% of the time, Pallas kernels for 45%

profile of v3, /device:TPU:0, one launch (start us, length us, event | category | flops | bytes accessed | tf_op | source)
XLA Modules:
  0.0 68.5 jit_solution(16228651040378314431)
XLA Ops:
  0.0 5.0 %pool_keys.1 = (f32[128,1024]{1,0:T(8,128)}, f32[128,1024]{1,0:T(8,128)}, f32[8,208,128]{2,1,0:T(8,128)}, f32[8,8,128]{2,1,0:T(8,128)S(1)}, f32[8,4,128]{2,1,0:T(4,128)S(1)}) custom-call(f32[1024,1024]{1,0:T(8,128)} %k_ref.2, f32[1024,1024]{1,0:T(8,128)} %v_ref.2), custom_call_target="tpu_custom_call" | custom-call | flops 2097152 | bytes 10485760 | tf_op jit(solution)/shard_map/pool_keys/pallas_call | solution.py:146
  5.0 2.9 %collective-permute-start.2 = (f32[8,4,128]{2,1,0:T(4,128)S(1)}, f32[8,4,128]{2,1,0:T(4,128)S(1)}, u32[]{:S(2)}, u32[]{:S(2)}) collective-permute-start(f32[8,4,128]{2,1,0:T(4,128)S(1)} %get-tuple-element.43), channel_id=1, source_target_pairs={{0,96},{16,112},{32,64},{48,80},{64,32},{80,48},{96,0},{112,16},{1... | collective-permute-start | bytes 49160 | tf_op jit(solution)/shard_map/ppermute | solution.py:524
  7.9 0.8 %collective-permute-start.1 = (f32[8,4,128]{2,1,0:T(4,128)S(1)}, f32[8,4,128]{2,1,0:T(4,128)S(1)}, u32[]{:S(2)}, u32[]{:S(2)}) collective-permute-start(f32[8,4,128]{2,1,0:T(4,128)S(1)} %get-tuple-element.43), channel_id=1, source_target_pairs={{0,64},{16,80},{32,96},{48,112},{64,0},{80,16},{96,32},{112,48},{1... | collective-permute-start | bytes 49160 | tf_op jit(solution)/shard_map/ppermute | solution.py:524
  8.7 0.5 collective-permute-start
  9.2 3.2 %pool_queries.1 = (f32[128,1024]{1,0:T(8,128)}, f32[8,208,128]{2,1,0:T(8,128)}) custom-call(f32[1024,1024]{1,0:T(8,128)} %q_ref.2, f32[8,208,128]{2,1,0:T(8,128)} %get-tuple-element.40.pay_in), custom_call_target="tpu_custom_call", output_to_operand_aliasing={{1}: (1, {})} | custom-call | flops 2147483648 | bytes 5242880 | tf_op jit(solution)/shard_map/pool_queries/pallas_call | solution.py:200
  12.4 0.0 collective-permute-done.2.r9b_ref
  12.4 0.8 %collective-permute-done.1.r9a_ref = f32[8,4,128]{2,1,0:T(4,128)S(1)} collective-permute-done((f32[8,4,128]{2,1,0:T(4,128)S(1)}, f32[8,4,128]{2,1,0:T(4,128)S(1)}, u32[]{:S(2)}, u32[]{:S(2)}) %collective-permute-start.1) | collective-permute-done | bytes 16416 | tf_op jit(solution)/shard_map/ppermute | solution.py:524
  13.2 0.0 collective-permute-done.r8_ref
  13.2 0.6 pack_rows.1
  13.8 6.3 %all-to-all-start = ((f32[8,208,128]{2,1,0:T(8,128)}), f32[8,208,128]{2,1,0:T(8,128)S(1)}, u32[]{:S(2)}, u32[]{:S(2)}) async-start(f32[8,208,128]{2,1,0:T(8,128)} %pack_rows.1), calls=%async_computation | async-start | bytes 1703936 | tf_op jit(solution)/shard_map/all_to_all | solution.py:528
  20.2 0.0 copy-start
  20.2 9.9 %local_levels.3 = (f32[1024,512]{1,0:T(8,128)}, f32[1024,128]{1,0:T(8,128)}) custom-call(f32[1024,1024]{1,0:T(8,128)} %q_ref.2, f32[1024,1024]{1,0:T(8,128)} %k_ref.2, f32[1024,1024]{1,0:T(8,128)} %v_ref.2), custom_call_target="tpu_custom_call" | custom-call | flops 4294967296 | bytes 8388608 | tf_op jit(solution)/shard_map/local_levels/pallas_call | solution.py:294
  30.0 1.6 %all-to-all-done.got_ref = f32[8,208,128]{2,1,0:T(8,128)S(1)} async-done(((f32[8,208,128]{2,1,0:T(8,128)}), f32[8,208,128]{2,1,0:T(8,128)S(1)}, u32[]{:S(2)}, u32[]{:S(2)}) %all-to-all-start) | async-done | bytes 852000 | tf_op jit(solution)/shard_map/all_to_all | solution.py:528
  31.7 0.1 rise_rows.1
  31.8 0.1 collective-permute-start.4
  31.9 0.0 copy-done.1
  31.9 0.7 %collective-permute-start.6 = (f32[128,1024]{1,0:T(8,128)S(1)}, f32[128,1024]{1,0:T(8,128)S(1)}, u32[]{:S(2)}, u32[]{:S(2)}) collective-permute-start(f32[128,1024]{1,0:T(8,128)S(1)} %copy-done.1), channel_id=1, source_target_pairs={{0,1},{1,0},{2,3},{3,2},{4,5},{5,4},{6,7},{7,6},{8,9},{9,8},{10,11... | collective-permute-start | bytes 1572872 | tf_op jit(solution)/shard_map/ppermute | solution.py:524
  32.6 1.4 %collective-permute-start.7 = (f32[128,1024]{1,0:T(8,128)S(1)}, f32[128,1024]{1,0:T(8,128)S(1)}, u32[]{:S(2)}, u32[]{:S(2)}) collective-permute-start(f32[128,1024]{1,0:T(8,128)S(1)} %copy-done), channel_id=1, source_target_pairs={{0,1},{1,0},{2,3},{3,2},{4,5},{5,4},{6,7},{7,6},{8,9},{9,8},{10,11... | collective-permute-start | bytes 1572872 | tf_op jit(solution)/shard_map/ppermute | solution.py:524
  34.0 2.2 %collective-permute-start.3 = (f32[2,192,128]{2,1,0:T(8,128)S(1)}, f32[2,192,128]{2,1,0:T(8,128)S(1)}, u32[]{:S(2)}, u32[]{:S(2)}) collective-permute-start(f32[2,192,128]{2,1,0:T(8,128)S(1)} %get-tuple-element.51.here_ref), channel_id=1, source_target_pairs={{0,12},{1,13},{2,14},{3,15},{4,8},{5,9},{6,10},{7,11},{8,4},{9,5},... | collective-permute-start | bytes 589832 | tf_op jit(solution)/shard_map/ppermute | solution.py:524
  36.2 0.0 collective-permute-done.4.core_ref
  36.2 1.1 %collective-permute-start.5 = (f32[2,128,128]{2,1,0:T(8,128)S(1)}, f32[2,128,128]{2,1,0:T(8,128)S(1)}, u32[]{:S(2)}, u32[]{:S(2)}) collective-permute-start(f32[2,128,128]{2,1,0:T(8,128)S(1)} %collective-permute-done.4.core_ref), channel_id=1, source_target_pairs={{0,12},{1,13},{2,14},{3,15},{4,8},{5,9},{6,10},{7,11},{8,4},{9,5},... | collective-permute-start | bytes 393224 | tf_op jit(solution)/shard_map/ppermute | solution.py:524
  37.2 6.1 %local_levels.4 = (f32[1024,256]{1,0:T(8,128)}, f32[1024,128]{1,0:T(8,128)}) custom-call(f32[1024,1024]{1,0:T(8,128)} %q_ref.2, f32[1024,1024]{1,0:T(8,128)} %k_ref.2, f32[1024,1024]{1,0:T(8,128)} %v_ref.2), custom_call_target="tpu_custom_call" | custom-call | flops 2147483648 | bytes 4194304 | tf_op jit(solution)/shard_map/local_levels/pallas_call | solution.py:294
  43.3 0.0 collective-permute-done.3.six_ref
  43.3 1.4 %collective-permute-done.5.seven_ref = f32[2,128,128]{2,1,0:T(8,128)S(1)} collective-permute-done((f32[2,128,128]{2,1,0:T(8,128)S(1)}, f32[2,128,128]{2,1,0:T(8,128)S(1)}, u32[]{:S(2)}, u32[]{:S(2)}) %collective-permute-start.5) | collective-permute-done | bytes 131104 | tf_op jit(solution)/shard_map/ppermute | solution.py:524
  44.7 2.9 %far_levels.1 = f32[8,72,128]{2,1,0:T(8,128)} custom-call(f32[8,208,128]{2,1,0:T(8,128)S(1)} %all-to-all-done.got_ref, f32[2,192,128]{2,1,0:T(8,128)S(1)} %get-tuple-element.51.here_ref, f32[2,192,128]{2,1,0:T(8,128)S(1)} %collective-permute-done.3.six_ref, f32[2,128,128]{2,1,0:T(8,128)S(1)} %collective-permute-done.4.core_ref, ...), custom_call_target="tpu_custom_call" | custom-call | flops 104857600 | bytes 1048576 | tf_op jit(solution)/shard_map/far_levels/pallas_call | solution.py:414
  47.6 3.6 %all-to-all-start.1 = ((f32[8,72,128]{2,1,0:T(8,128)}), f32[8,72,128]{2,1,0:T(8,128)S(1)}, u32[]{:S(2)}, u32[]{:S(2)}) async-start(f32[8,72,128]{2,1,0:T(8,128)} %far_levels.1), calls=%async_computation.1 | async-start | bytes 589824 | tf_op jit(solution)/shard_map/all_to_all | solution.py:528
  51.2 6.1 %local_levels.5 = (f32[1024,256]{1,0:T(8,128)}, f32[1024,128]{1,0:T(8,128)}) custom-call(f32[1024,1024]{1,0:T(8,128)} %q_ref.2, f32[1024,1024]{1,0:T(8,128)} %k_ref.2, f32[1024,1024]{1,0:T(8,128)} %v_ref.2), custom_call_target="tpu_custom_call" | custom-call | flops 2147483648 | bytes 4194304 | tf_op jit(solution)/shard_map/local_levels/pallas_call | solution.py:294
  57.2 0.0 collective-permute-done.6.k3_ref
  57.2 2.2 %collective-permute-done.7.v3_ref = f32[128,1024]{1,0:T(8,128)S(1)} collective-permute-done((f32[128,1024]{1,0:T(8,128)S(1)}, f32[128,1024]{1,0:T(8,128)S(1)}, u32[]{:S(2)}, u32[]{:S(2)}) %collective-permute-start.7) | collective-permute-done | bytes 524320 | tf_op jit(solution)/shard_map/ppermute | solution.py:524
  59.5 2.6 %near_level.1 = (f32[128,1024]{1,0:T(8,128)}, f32[128,128]{1,0:T(8,128)}) custom-call(f32[128,1024]{1,0:T(8,128)} %get-tuple-element.68.q3_ref, f32[128,1024]{1,0:T(8,128)S(1)} %collective-permute-done.6.k3_ref, f32[128,1024]{1,0:T(8,128)S(1)} %collective-permute-done.7.v3_ref), custom_call_target="tpu_custom_call" | custom-call | flops 209715200 | bytes 2097152 | tf_op jit(solution)/shard_map/near_level/pallas_call | solution.py:436
  62.1 0.0 all-to-all-done.1.refs_8_
  62.1 6.2 %join_levels.1 = f32[1024,1024]{1,0:T(8,128)} custom-call(f32[1024,512]{1,0:T(8,128)} %get-tuple-element.49.refs_0_, f32[1024,256]{1,0:T(8,128)} %get-tuple-element.58.refs_1_, f32[1024,256]{1,0:T(8,128)} %get-tuple-element.64.refs_2_, f32[1024,128]{1,0:T(8,128)} %get-tuple-element.65.refs_3_, f32[1024,128]{1,0:T(8,128)} %get-tuple-element.66.refs_4_, ...), custom_call_target="tpu_custom_call" | custom-call | flops 16777216 | bytes 9437184 | tf_op jit(solution)/shard_map/join_levels/pallas_call | solution.py:501
  (2 shorter events, 0.0 us)
Async XLA Ops:
  5.0 7.4 %collective-permute-start.2 = (f32[8,4,128]{2,1,0:T(4,128)S(1)}, f32[8,4,128]{2,1,0:T(4,128)S(1)}, u32[]{:S(2)}, u32[]{:S(2)}) collective-permute-start(f32[8,4,128]{2,1,0:T(4,128)S(1)} %get-tuple-element.43), channel_id=1, source_target_pairs={{0,96},{16,112},{32,64},{48,80},{64,32},{80,48},{96,0},{112,16},{1... | collective-permute-start | bytes 49160 | tf_op jit(solution)/shard_map/ppermute | solution.py:524
  7.9 5.2 %collective-permute-start.1 = (f32[8,4,128]{2,1,0:T(4,128)S(1)}, f32[8,4,128]{2,1,0:T(4,128)S(1)}, u32[]{:S(2)}, u32[]{:S(2)}) collective-permute-start(f32[8,4,128]{2,1,0:T(4,128)S(1)} %get-tuple-element.43), channel_id=1, source_target_pairs={{0,64},{16,80},{32,96},{48,112},{64,0},{80,16},{96,32},{112,48},{1... | collective-permute-start | bytes 49160 | tf_op jit(solution)/shard_map/ppermute | solution.py:524
  8.7 4.4 %collective-permute-start = (f32[8,8,128]{2,1,0:T(8,128)S(1)}, f32[8,8,128]{2,1,0:T(8,128)S(1)}, u32[]{:S(2)}, u32[]{:S(2)}) collective-permute-start(f32[8,8,128]{2,1,0:T(8,128)S(1)} %get-tuple-element.42), channel_id=1, source_target_pairs={{0,32},{16,48},{32,0},{48,16},{64,96},{80,112},{96,64},{112,80},{1... | collective-permute-start | bytes 98312 | tf_op jit(solution)/shard_map/ppermute | solution.py:524
  13.8 17.8 %all-to-all-start = ((f32[8,208,128]{2,1,0:T(8,128)}), f32[8,208,128]{2,1,0:T(8,128)S(1)}, u32[]{:S(2)}, u32[]{:S(2)}) async-start(f32[8,208,128]{2,1,0:T(8,128)} %pack_rows.1), calls=%async_computation | async-start | bytes 1703936 | tf_op jit(solution)/shard_map/all_to_all | solution.py:528
  20.2 11.7 %copy-start.1 = (f32[128,1024]{1,0:T(8,128)S(1)}, f32[128,1024]{1,0:T(8,128)}, u32[]{:S(2)}) copy-start(f32[128,1024]{1,0:T(8,128)} %get-tuple-element.71) | copy-start | bytes 1572868
  20.2 12.4 %copy-start = (f32[128,1024]{1,0:T(8,128)S(1)}, f32[128,1024]{1,0:T(8,128)}, u32[]{:S(2)}) copy-start(f32[128,1024]{1,0:T(8,128)} %get-tuple-element.72) | copy-start | bytes 1572868
  31.8 4.4 %collective-permute-start.4 = (f32[2,128,128]{2,1,0:T(8,128)S(1)}, f32[2,128,128]{2,1,0:T(8,128)S(1)}, u32[]{:S(2)}, u32[]{:S(2)}) collective-permute-start(f32[2,128,128]{2,1,0:T(8,128)S(1)} %get-tuple-element.52), channel_id=1, source_target_pairs={{0,16},{16,0},{32,48},{48,32},{64,80},{80,64},{96,112},{112,96},{1... | collective-permute-start | bytes 393224 | tf_op jit(solution)/shard_map/ppermute | solution.py:524
  31.9 25.4 %collective-permute-start.6 = (f32[128,1024]{1,0:T(8,128)S(1)}, f32[128,1024]{1,0:T(8,128)S(1)}, u32[]{:S(2)}, u32[]{:S(2)}) collective-permute-start(f32[128,1024]{1,0:T(8,128)S(1)} %copy-done.1), channel_id=1, source_target_pairs={{0,1},{1,0},{2,3},{3,2},{4,5},{5,4},{6,7},{7,6},{8,9},{9,8},{10,11... | collective-permute-start | bytes 1572872 | tf_op jit(solution)/shard_map/ppermute | solution.py:524
  32.6 26.9 %collective-permute-start.7 = (f32[128,1024]{1,0:T(8,128)S(1)}, f32[128,1024]{1,0:T(8,128)S(1)}, u32[]{:S(2)}, u32[]{:S(2)}) collective-permute-start(f32[128,1024]{1,0:T(8,128)S(1)} %copy-done), channel_id=1, source_target_pairs={{0,1},{1,0},{2,3},{3,2},{4,5},{5,4},{6,7},{7,6},{8,9},{9,8},{10,11... | collective-permute-start | bytes 1572872 | tf_op jit(solution)/shard_map/ppermute | solution.py:524
  34.0 9.3 %collective-permute-start.3 = (f32[2,192,128]{2,1,0:T(8,128)S(1)}, f32[2,192,128]{2,1,0:T(8,128)S(1)}, u32[]{:S(2)}, u32[]{:S(2)}) collective-permute-start(f32[2,192,128]{2,1,0:T(8,128)S(1)} %get-tuple-element.51.here_ref), channel_id=1, source_target_pairs={{0,12},{1,13},{2,14},{3,15},{4,8},{5,9},{6,10},{7,11},{8,4},{9,5},... | collective-permute-start | bytes 589832 | tf_op jit(solution)/shard_map/ppermute | solution.py:524
  36.2 8.5 %collective-permute-start.5 = (f32[2,128,128]{2,1,0:T(8,128)S(1)}, f32[2,128,128]{2,1,0:T(8,128)S(1)}, u32[]{:S(2)}, u32[]{:S(2)}) collective-permute-start(f32[2,128,128]{2,1,0:T(8,128)S(1)} %collective-permute-done.4.core_ref), channel_id=1, source_target_pairs={{0,12},{1,13},{2,14},{3,15},{4,8},{5,9},{6,10},{7,11},{8,4},{9,5},... | collective-permute-start | bytes 393224 | tf_op jit(solution)/shard_map/ppermute | solution.py:524
  47.6 14.6 %all-to-all-start.1 = ((f32[8,72,128]{2,1,0:T(8,128)}), f32[8,72,128]{2,1,0:T(8,128)S(1)}, u32[]{:S(2)}, u32[]{:S(2)}) async-start(f32[8,72,128]{2,1,0:T(8,128)} %far_levels.1), calls=%async_computation.1 | async-start | bytes 589824 | tf_op jit(solution)/shard_map/all_to_all | solution.py:528

commit v4 on v3

--- a/solution.py
+++ b/solution.py
@@ -11,7 +11,7 @@
 HEADS = 8
 PACK = 208
 BACK = 72
-CALLS = (4, 2, 2)
+CALLS = (5, 2, 1)
 WIDTH = 128
 ROWS = 1024
 F32 = jnp.float32
@@ -89,6 +89,10 @@
     m = jnp.maximum(ma, mb)
     fa, fb = jnp.exp2(ma - m), jnp.exp2(mb - m)
     return m, sa * fa + sb * fb, na * fa + nb * fb
+
+
+def share(a, b):
+    return 1.0 / (1.0 + jnp.exp2(b - a))
 
 
 def pool_eight(ref):
@@ -242,8 +246,8 @@
     )(in_hbm(pay), r8, r9a, r9b)
 
 
-def local_body(first, q_ref, k_ref, v_ref, o_ref, lse_ref):
-    head = pl.program_id(0) + first
+def local_body(count, q_ref, k_ref, v_ref, o_ref, lse_ref, columns):
+    head = pl.program_id(0)
 
     def load(ref):
         return [ref[pl.ds(k, 128, stride=8), :] for k in range(8)]
@@ -285,25 +289,31 @@
                 o_ref[128 * k + 32 * p : 128 * k + 32 * p + 32, :] = n / s
                 lses[k][p] = m + jnp.log2(s)
     for k in range(8):
-        old = lse_ref[128 * k : 128 * k + 128, :]
-        lse_ref[128 * k : 128 * k + 128, :] = jnp.where(lane == head, jnp.concatenate(lses[k], axis=0), old)
-
-
-def local_call(q, k, v, first, count):
+        old = columns[128 * k : 128 * k + 128, :]
+        columns[128 * k : 128 * k + 128, :] = jnp.where(lane == head, jnp.concatenate(lses[k], axis=0), old)
+
+    @pl.when(head == count - 1)
+    def _():
+        for k in range(8):
+            lse_ref[:, 128 * k : 128 * k + 128] = jnp.transpose(columns[128 * k : 128 * k + 128, :])[0:8]
+
+
+def local_call(q, k, v, first, count, weight):
     block = pl.BlockSpec((ROWS, WIDTH), lambda h: (0, h + first))
     return pl.pallas_call(
-        functools.partial(local_body, first),
+        functools.partial(local_body, count),
         name="local_levels",
         grid=(count,),
         in_specs=[block] * 3,
-        out_specs=[pl.BlockSpec((ROWS, WIDTH), lambda h: (0, h)), pl.BlockSpec((ROWS, WIDTH), lambda h: (0, 0))],
+        out_specs=[pl.BlockSpec((ROWS, WIDTH), lambda h: (0, h)), pl.BlockSpec((HEADS, ROWS), lambda h: (0, 0))],
         out_shape=[
             pltpu.HBM((ROWS, count * WIDTH), F32),
-            pltpu.HBM((ROWS, WIDTH), F32),
+            pltpu.HBM((HEADS, ROWS), F32),
         ],
+        scratch_shapes=[pltpu.VMEM((ROWS, WIDTH), F32)],
         compiler_params=params(16),
         cost_estimate=pl.CostEstimate(
-            flops=(count << 30), bytes_accessed=count << 21, transcendentals=count << 19
+            flops=count * weight << 20, bytes_accessed=count * weight << 11, transcendentals=count * weight << 9
         ),
     )(in_hbm(q), in_hbm(k), in_hbm(v))
 
@@ -341,22 +351,46 @@
     )(got)
 
 
-def far_body(got_ref, here_ref, six_ref, core_ref, seven_ref, out_ref, scratch, es):
-    def gather(i, sources):
-        return jnp.concatenate([got_ref[s, 64 * i : 64 * i + 64, :] for s in sources], axis=0)
-
-    def halve(i, base, count):
-        return 0.5 * (scratch[i, pl.ds(base, count, stride=2), :] + scratch[i, pl.ds(base + 1, count, stride=2), :])
-
+def middle_body(got_ref, o_ref, lse_ref, q_ref, scratch, es):
     for i in range(3):
-        scratch[i, 0:512, :] = gather(i, range(8))
+        for s in range(8):
+            scratch[i, 64 * s : 64 * s + 64, :] = got_ref[s, 64 * i : 64 * i + 64, :]
         base, count = 0, 256
         while count >= (16 if i == 0 else 256):
-            x = halve(i, base, count)
+            x = pool_pairs(scratch.at[i, base : base + 2 * count], count)
             base = base + 2 * count
             scratch[i, base : base + count, :] = x
             count = count // 2
-
+    q_ref[...] = scratch[0, 768:1008, :]
+    tasks = []
+    for level, base, blocks in ((4, 0, 4), (5, 512, 2)):
+        for g in range(blocks):
+            mine = slice(base + 128 * g, base + 128 * g + 128)
+            other = slice(base + 128 * (g ^ 1), base + 128 * (g ^ 1) + 128)
+            tasks.append((scratch[0, mine, :], scratch[1, other, :], scratch[2, other, :], level))
+    done = attend_all(tasks)
+    four, five = (tuple(jnp.concatenate(x, axis=0) for x in zip(*few)) for few in (done[0:4], done[4:6]))
+    for i, x in enumerate(five):
+        x = jnp.broadcast_to(x, (256, WIDTH))
+        for c in range(2):
+            es[i, pl.ds(c, 256, stride=2), :] = x
+    m, s, n = merge(four, (es[0], es[1], es[2]))
+    o_ref[...] = n / s
+    lse_ref[...] = m + jnp.log2(s)
+
+
+def middle_call(got):
+    return pl.pallas_call(
+        middle_body,
+        name="middle_levels",
+        out_shape=[jax.ShapeDtypeStruct((n, WIDTH), F32) for n in (512, 512, 240)],
+        scratch_shapes=[pltpu.VMEM((3, 1024, WIDTH), F32), pltpu.VMEM((3, 512, WIDTH), F32)],
+        compiler_params=params(),
+        cost_estimate=pl.CostEstimate(flops=1 << 20, bytes_accessed=1 << 16, transcendentals=1 << 10),
+    )(got)
+
+
+def far_body(o_ref, lse_ref, q_ref, here_ref, six_ref, core_ref, seven_ref, out_ref, es):
     def sibling(i, level):
         if level == 6:
             return six_ref[i, 0:128, :]
@@ -374,35 +408,31 @@
         )
 
     tasks = []
-    for level, base, blocks in ((4, 0, 4), (5, 512, 2)):
-        for g in range(blocks):
-            mine = slice(base + 128 * g, base + 128 * g + 128)
-            other = slice(base + 128 * (g ^ 1), base + 128 * (g ^ 1) + 128)
-            tasks.append((scratch[0, mine, :], scratch[1, other, :], scratch[2, other, :], level))
-    base, count = 768, 128
+    base, count = 0, 128
     for level in range(6, 10):
-        tasks.append((scratch[0, base : base + count, :], sibling(0, level), sibling(1, level), level))
+        tasks.append((q_ref[base : base + count, :], sibling(0, level), sibling(1, level), level))
         base, count = base + count, count // 2
-    done = attend_all(tasks)
-    levels = []
-    for few in (done[0:4], done[4:6]):
-        levels.append(tuple(jnp.concatenate(x, axis=0) for x in zip(*few)))
-    levels.extend(done[6:])
+    levels = attend_all(tasks)
+
+    def spread(i, base, x, times):
+        n = x.shape[0]
+        x = jnp.broadcast_to(x, (n, WIDTH))
+        for c in range(times):
+            es[i, pl.ds(base + c, n, stride=times), :] = x
+        return es[i, base : base + times * n, :]
+
     running = levels[-1]
     base = 0
     for finer in reversed(levels[:-1]):
         n = running[0].shape[0]
-        wide = []
-        for i, x in enumerate(running):
-            x = jnp.broadcast_to(x, (n, WIDTH))
-            es[i, pl.ds(base, n, stride=2), :] = x
-            es[i, pl.ds(base + 1, n, stride=2), :] = x
-            wide.append(es[i, base : base + 2 * n, :])
+        running = merge(finer, tuple(spread(i, base, x, 2) for i, x in enumerate(running)))
         base = base + 2 * n
-        running = merge(finer, tuple(wide))
     m, s, n = running
-    o = n / s
-    lse = jnp.broadcast_to(m + jnp.log2(s), (512, WIDTH))
+    high_o, high_lse = spread(0, 256, n / s, 4), spread(1, 256, m + jnp.log2(s), 4)
+    low_o, low_lse = o_ref[...], lse_ref[...]
+    top = jnp.maximum(low_lse, high_lse)
+    lse = top + jnp.log2(jnp.exp2(low_lse - top) + jnp.exp2(high_lse - top))
+    o = high_o + (low_o - high_o) * share(low_lse, high_lse)
     for g in range(4):
         row = jnp.transpose(lse[128 * g : 128 * g + 128])[0:8]
         for d in range(2):
@@ -410,15 +440,15 @@
             out_ref[2 * g + d, 64:72, :] = row if d == 0 else pltpu.roll(row, 64, 1)
 
 
-def far_call(got, here, six, core, seven):
+def far_call(middle, here, six, core, seven):
     return pl.pallas_call(
         far_body,
         name="far_levels",
         out_shape=pltpu.HBM((HEADS, BACK, WIDTH), F32),
-        scratch_shapes=[pltpu.VMEM((3, 1024, WIDTH), F32), pltpu.VMEM((3, 1024, WIDTH), F32)],
+        scratch_shapes=[pltpu.VMEM((3, 768, WIDTH), F32)],
         compiler_params=params(),
         cost_estimate=pl.CostEstimate(flops=100 << 20, bytes_accessed=1 << 20, transcendentals=1 << 17),
-    )(got, here, six, core, seven)
+    )(*middle, here, six, core, seven)
 
 
 def near_body(q3_ref, k3_ref, v3_ref, o_ref, lse_ref):
@@ -442,54 +472,62 @@
     )(in_hbm(q3), k3, v3)
 
 
-def share(a, b):
-    return 1.0 / (1.0 + jnp.exp2(b - a))
-
-
 def join_body(*refs):
     n = len(CALLS)
     own_hbm, own_lse_hbm = refs[:n], refs[n : 2 * n]
     o3_hbm, lse3_hbm, far_ref, out_hbm = refs[2 * n : 2 * n + 4]
-    own, own_lse, o3, lse3, wide, stage, own_sems, sems, out_sems = refs[2 * n + 4 :]
-    place = [(c, i) for c, count in enumerate(CALLS) for i in range(count)]
-
-    def columns(h):
+    own, own_lse, shares, o3, lse3, wide, stage, own_sems, sems, out_sems = refs[2 * n + 4 :]
+    place = [(call, i) for call, count in enumerate(CALLS) for i in range(count)]
+
+    def cols(h):
         return slice(WIDTH * h, WIDTH * h + WIDTH)
 
     def fetch(h):
-        c, i = place[h]
-        return pltpu.make_async_copy(own_hbm[c].at[:, columns(i)], own.at[h], own_sems.at[h])
+        call, i = place[h]
+        return pltpu.make_async_copy(own_hbm[call].at[:, cols(i)], own.at[h], own_sems.at[h])
 
     def send(h):
-        return pltpu.make_async_copy(stage.at[h % 4], out_hbm.at[:, columns(h)], out_sems.at[h % 4])
-
-    fetch(0).start()
+        return pltpu.make_async_copy(stage.at[h % 4], out_hbm.at[:, cols(h)], out_sems.at[h % 4])
+
     others = [pltpu.make_async_copy(lse3_hbm, lse3, sems.at[0]), pltpu.make_async_copy(o3_hbm, o3, sems.at[1])]
-    others += [pltpu.make_async_copy(own_lse_hbm[c], own_lse.at[c], sems.at[c + 2]) for c in range(n)]
+    others += [pltpu.make_async_copy(own_lse_hbm[call], own_lse.at[call], sems.at[call + 2]) for call in range(n)]
     for copy in others:
         copy.start()
-    for h in range(1, HEADS):
+    for h in range(HEADS):
         fetch(h).start()
+
+    for h in range(HEADS):
+        wide[1, h : h + 1, :] = far_ref[h, 64:65, :]
+    far_lse = jnp.transpose(wide[1])[0:64]
+    for c in range(2):
+        wide[0, pl.ds(c, 64, stride=2), :] = far_lse
+    far_lse = wide[0]
     for copy in others:
         copy.wait()
-
+    near_lse = lse3[...]
+    top = jnp.maximum(far_lse, near_lse)
+    rest_lse = top + jnp.log2(jnp.exp2(far_lse - top) + jnp.exp2(near_lse - top))
+    near_share = share(near_lse, far_lse)
     for h in range(HEADS):
-        lse = jnp.transpose(jnp.broadcast_to(far_ref[h, 64:65, :], (128, WIDTH)))[0:64]
-        for i, x in enumerate((far_ref[h, 0:64, :], lse)):
-            for c in range(2):
-                wide[h % 2, i, pl.ds(c, 64, stride=2), :] = x
-        far_o, far_lse = wide[h % 2, 0], wide[h % 2, 1]
-        near_lse = jnp.broadcast_to(lse3[:, h : h + 1], (128, WIDTH))
-        top = jnp.maximum(far_lse, near_lse)
-        rest_lse = top + jnp.log2(jnp.exp2(far_lse - top) + jnp.exp2(near_lse - top))
-        rest = far_o + (o3[:, columns(h)] - far_o) * share(near_lse, far_lse)
+        call, i = place[h]
+        own_lse[n, h : h + 1, :] = own_lse[call, i : i + 1, :]
+    for k in range(8):
+        part = slice(128 * k, 128 * k + 128)
+        lse = jnp.concatenate([own_lse[n, :, part], jnp.zeros((120, WIDTH), F32)], axis=0)
+        shares[part, :] = share(jnp.transpose(lse), rest_lse)
+
+    for h in range(HEADS):
+        for c in range(2):
+            wide[2 + h % 2, pl.ds(c, 64, stride=2), :] = far_ref[h, 0:64, :]
+        far = wide[2 + h % 2]
+        rest = far + (o3[:, cols(h)] - far) * jnp.broadcast_to(near_share[:, h : h + 1], (128, WIDTH))
         fetch(h).wait()
         if h >= 4:
             send(h - 4).wait()
         for k in range(8):
             part = slice(128 * k, 128 * k + 128)
-            lse = jnp.broadcast_to(own_lse[place[h][0], part, h : h + 1], (128, WIDTH))
-            stage[h % 4, pl.ds(k, 128, stride=8), :] = rest + (own[h, part, :] - rest) * share(lse, rest_lse)
+            weight = jnp.broadcast_to(shares[part, h : h + 1], (128, WIDTH))
+            stage[h % 4, pl.ds(k, 128, stride=8), :] = rest + (own[h, part, :] - rest) * weight
         send(h).start()
     for h in range(HEADS - 4, HEADS):
         send(h).wait()
@@ -506,10 +544,11 @@
         out_shape=pltpu.HBM((ROWS, HEADS * WIDTH), F32),
         scratch_shapes=[
             pltpu.VMEM((HEADS, ROWS, WIDTH), F32),
-            pltpu.VMEM((n, ROWS, WIDTH), F32),
+            pltpu.VMEM((n + 1, HEADS, ROWS), F32),
+            pltpu.VMEM((ROWS, WIDTH), F32),
             pltpu.VMEM((128, HEADS * WIDTH), F32),
             pltpu.VMEM((128, WIDTH), F32),
-            pltpu.VMEM((2, 2, 128, WIDTH), F32),
+            pltpu.VMEM((4, 128, WIDTH), F32),
             pltpu.VMEM((4, ROWS, WIDTH), F32),
             pltpu.SemaphoreType.DMA((HEADS,)),
             pltpu.SemaphoreType.DMA((n + 2,)),
@@ -533,15 +572,15 @@
     first = [sum(CALLS[:i]) for i in range(len(CALLS))]
     local = []
 
-    def local_part(i, *after):
+    def local_part(i, *after, weight=1024):
         q, k, v = lax.optimization_barrier((queries, keys, values) + after)[:3]
-        return local_call(q, k, v, first[i], CALLS[i])
+        return local_call(q, k, v, first[i], CALLS[i], weight)
 
     r8, r9a, r9b = hop(x8, "seq", 2), hop(x9, "seq", 4), hop(x9, "seq", 6)
     q3, pay = pool_q_call(queries, pay)
     pay = pack_call(pay, r8, r9a, r9b)
     got = transpose_heads(pay)
-    part = local_part(0, pay)
+    part = local_part(0, pay, weight=4096)
     got, part = lax.optimization_barrier((got, part))
     local.append(part)
     _, k3, v3 = lax.optimization_barrier((part, k3, v3))
@@ -551,13 +590,15 @@
     six = hop(here6, "node", 12)
     core = hop(here7, "seq", 1)
     seven = hop(core, "node", 12)
-    part = local_part(1, core)
-    six, seven, part = lax.optimization_barrier((six, seven, part))
+    middle = middle_call(lax.optimization_barrier((got, core))[0])
+    part = local_part(1, core, weight=1)
+    six, seven, part, middle = lax.optimization_barrier((six, seven, part, middle))
     local.append(part)
 
-    far = far_call(got, here6, six, core, seven)
+    far = far_call(middle, here6, six, core, seven)
     back = transpose_heads(far)
-    local.append(local_part(2, far))
+    local.append(local_part(2, far, sib_k3))
+    q3 = lax.optimization_barrier((q3, local[-1]))[0]
     o3, lse3 = near_call(q3, sib_k3, sib_v3)
     return join_call(local, o3, lse3, back)
 

time: 68.9 us -> 66.8 us (0.970)
  waiting for transfers between devices: 6.05 us -> 2.84 us
  starting transfers between devices: 19.5 us -> 21.1 us
  Pallas kernels: 42.6 us -> 41.7 us
    ppermute x8, waiting for transfers between devices: 4.42 us -> 2.05 us  [hop(): lax.ppermute(x, axis, [(i, i ^ flip) for i in range(lax.axis_size(axis))])]
    pallas_call x1, Pallas kernels: 2.9 us -> 1.5 us  [far_call(): pl.pallas_call(far_body, name='far_levels', out_shape=pltpu.HBM((HEADS, B...]
    pallas_call x3 -> x4, Pallas kernels: 22 us -> 23.3 us  [the longest x3 21.8 us: local_call(): pl.pallas_call(functools.partial(local_body, count), name='local_levels',...]
    all_to_all x2, starting transfers between devices: 9.94 us -> 11.1 us  [transpose_heads(): return lax.all_to_all(x, 'node', 0, 0, axis_index_groups=GROUPS, tiled=True)]
    all_to_all x2, waiting for transfers between devices: 1.63 us -> 0.79 us  [transpose_heads(): return lax.all_to_all(x, 'node', 0, 0, axis_index_groups=GROUPS, tiled=True)]
    pallas_call x1, Pallas kernels: 6.16 us -> 5.33 us  [join_call(): pl.pallas_call(join_body, name='join_levels', in_specs=[anywhere] * (2 *...]
  transfers between devices with their start and end apart: 10 -> 10, of which waited for: 4 -> 4; matrix products, arithmetic and copies ran while one was open for 0% -> 0% of each run, Pallas kernels for 45% -> 47%
where the time goes in v4:
time: 66.8 us; the launch traced here: 65.8 us
  Pallas kernels  41.7 us (62%)
  starting transfers between devices  21.1 us (32%)
  waiting for transfers between devices  2.84 us (4%)
    pallas_call x3, Pallas kernels, local_call(): pl.pallas_call(functools.partial(local_body, count), name='local_levels',...  21.8 us
    all_to_all x2, starting transfers between devices, transpose_heads(): return lax.all_to_all(x, 'node', 0, 0, axis_index_groups=GROUPS, tiled=True)  11.1 us
    ppermute x8, starting transfers between devices, hop(): lax.ppermute(x, axis, [(i, i ^ flip) for i in range(lax.axis_size(axis))])  9.96 us
    pallas_call x1, Pallas kernels, join_call(): pl.pallas_call(join_body, name='join_levels', in_specs=[anywhere] * (2 *...  5.33 us
    pallas_call x1, Pallas kernels, pool_kv_call(): pl.pallas_call(pool_kv_body, name='pool_keys', in_specs=[anywhere] * 2, o...  4.99 us
    pallas_call x1, Pallas kernels, pool_q_call(): pl.pallas_call(pool_q_body, name='pool_queries', in_specs=[anywhere] * 2,...  3.2 us
    pallas_call x1, Pallas kernels, near_call(): pl.pallas_call(near_body, name='near_level', out_shape=[pltpu.HBM((128, H...  2.64 us
    ppermute x8, waiting for transfers between devices, hop(): lax.ppermute(x, axis, [(i, i ^ flip) for i in range(lax.axis_size(axis))])  2.05 us
  transfers between devices with their start and end apart: 10, of which 4 were waited for; matrix products, arithmetic and copies ran while one was open for 0% of the time, Pallas kernels for 47%

profile of v4, /device:TPU:0, one launch (start us, length us, event | category | flops | bytes accessed | tf_op | source)
XLA Modules:
  0.0 65.8 jit_solution(858009037792664881)
XLA Ops:
  0.0 5.0 %pool_keys.1 = (f32[128,1024]{1,0:T(8,128)}, f32[128,1024]{1,0:T(8,128)}, f32[8,208,128]{2,1,0:T(8,128)}, f32[8,8,128]{2,1,0:T(8,128)S(1)}, f32[8,4,128]{2,1,0:T(4,128)S(1)}) custom-call(f32[1024,1024]{1,0:T(8,128)} %k_ref.2, f32[1024,1024]{1,0:T(8,128)} %v_ref.2), custom_call_target="tpu_custom_call" | custom-call | flops 2097152 | bytes 10485760 | tf_op jit(solution)/shard_map/pool_keys/pallas_call | solution.py:150
  5.0 2.9 %collective-permute-start.2 = (f32[8,4,128]{2,1,0:T(4,128)S(1)}, f32[8,4,128]{2,1,0:T(4,128)S(1)}, u32[]{:S(2)}, u32[]{:S(2)}) collective-permute-start(f32[8,4,128]{2,1,0:T(4,128)S(1)} %get-tuple-element.51), channel_id=1, source_target_pairs={{0,96},{16,112},{32,64},{48,80},{64,32},{80,48},{96,0},{112,16},{1... | collective-permute-start | bytes 49160 | tf_op jit(solution)/shard_map/ppermute | solution.py:563
  7.9 0.8 %collective-permute-start.1 = (f32[8,4,128]{2,1,0:T(4,128)S(1)}, f32[8,4,128]{2,1,0:T(4,128)S(1)}, u32[]{:S(2)}, u32[]{:S(2)}) collective-permute-start(f32[8,4,128]{2,1,0:T(4,128)S(1)} %get-tuple-element.51), channel_id=1, source_target_pairs={{0,64},{16,80},{32,96},{48,112},{64,0},{80,16},{96,32},{112,48},{1... | collective-permute-start | bytes 49160 | tf_op jit(solution)/shard_map/ppermute | solution.py:563
  8.7 0.5 collective-permute-start
  9.2 3.2 %pool_queries.1 = (f32[128,1024]{1,0:T(8,128)}, f32[8,208,128]{2,1,0:T(8,128)}) custom-call(f32[1024,1024]{1,0:T(8,128)} %q_ref.2, f32[8,208,128]{2,1,0:T(8,128)} %get-tuple-element.48.pay_in), custom_call_target="tpu_custom_call", output_to_operand_aliasing={{1}: (1, {})} | custom-call | flops 2147483648 | bytes 5242880 | tf_op jit(solution)/shard_map/pool_queries/pallas_call | solution.py:204
  12.4 0.0 collective-permute-done.2.r9b_ref
  12.4 0.8 %collective-permute-done.1.r9a_ref = f32[8,4,128]{2,1,0:T(4,128)S(1)} collective-permute-done((f32[8,4,128]{2,1,0:T(4,128)S(1)}, f32[8,4,128]{2,1,0:T(4,128)S(1)}, u32[]{:S(2)}, u32[]{:S(2)}) %collective-permute-start.1) | collective-permute-done | bytes 16416 | tf_op jit(solution)/shard_map/ppermute | solution.py:563
  13.2 0.0 collective-permute-done.r8_ref
  13.2 0.6 pack_rows.1
  13.8 6.3 %all-to-all-start = ((f32[8,208,128]{2,1,0:T(8,128)}), f32[8,208,128]{2,1,0:T(8,128)S(1)}, u32[]{:S(2)}, u32[]{:S(2)}) async-start(f32[8,208,128]{2,1,0:T(8,128)} %pack_rows.1), calls=%async_computation | async-start | bytes 1703936 | tf_op jit(solution)/shard_map/all_to_all | solution.py:567
  20.2 0.0 copy-start
  20.2 11.8 %local_levels.3 = (f32[1024,640]{1,0:T(8,128)}, f32[8,1024]{1,0:T(8,128)}) custom-call(f32[1024,1024]{1,0:T(8,128)} %q_ref.2, f32[1024,1024]{1,0:T(8,128)} %k_ref.2, f32[1024,1024]{1,0:T(8,128)} %v_ref.2), custom_call_target="tpu_custom_call" | custom-call | flops 21474836480 | bytes 41943040 | tf_op jit(solution)/shard_map/local_levels/pallas_call | solution.py:303
  31.9 0.0 all-to-all-done.got_ref
  31.9 2.1 %collective-permute-start.6 = (f32[128,1024]{1,0:T(8,128)S(1)}, f32[128,1024]{1,0:T(8,128)S(1)}, u32[]{:S(2)}, u32[]{:S(2)}) collective-permute-start(f32[128,1024]{1,0:T(8,128)S(1)} %copy-done.1), channel_id=1, source_target_pairs={{0,1},{1,0},{2,3},{3,2},{4,5},{5,4},{6,7},{7,6},{8,9},{9,8},{10,11... | collective-permute-start | bytes 1572872 | tf_op jit(solution)/shard_map/ppermute | solution.py:563
  34.0 0.1 collective-permute-start.7
  34.1 0.1 rise_rows.1
  34.2 0.1 collective-permute-start.4
  34.3 2.3 %collective-permute-start.3 = (f32[2,192,128]{2,1,0:T(8,128)S(1)}, f32[2,192,128]{2,1,0:T(8,128)S(1)}, u32[]{:S(2)}, u32[]{:S(2)}) collective-permute-start(f32[2,192,128]{2,1,0:T(8,128)S(1)} %get-tuple-element.59.here_ref), channel_id=1, source_target_pairs={{0,12},{1,13},{2,14},{3,15},{4,8},{5,9},{6,10},{7,11},{8,4},{9,5},... | collective-permute-start | bytes 589832 | tf_op jit(solution)/shard_map/ppermute | solution.py:563
  36.6 0.0 collective-permute-done.4.core_ref
  36.6 1.3 %collective-permute-start.5 = (f32[2,128,128]{2,1,0:T(8,128)S(1)}, f32[2,128,128]{2,1,0:T(8,128)S(1)}, u32[]{:S(2)}, u32[]{:S(2)}) collective-permute-start(f32[2,128,128]{2,1,0:T(8,128)S(1)} %collective-permute-done.4.core_ref), channel_id=1, source_target_pairs={{0,12},{1,13},{2,14},{3,15},{4,8},{5,9},{6,10},{7,11},{8,4},{9,5},... | collective-permute-start | bytes 393224 | tf_op jit(solution)/shard_map/ppermute | solution.py:563
  37.8 1.5 %middle_levels.1 = (f32[512,128]{1,0:T(8,128)S(1)}, f32[512,128]{1,0:T(8,128)S(1)}, f32[240,128]{1,0:T(8,128)S(1)}) custom-call(f32[8,208,128]{2,1,0:T(8,128)S(1)} %all-to-all-done.got_ref), custom_call_target="tpu_custom_call" | custom-call | flops 1048576 | bytes 65536 | tf_op jit(solution)/shard_map/middle_levels/pallas_call | solution.py:383
  39.4 6.0 %local_levels.4 = (f32[1024,256]{1,0:T(8,128)}, f32[8,1024]{1,0:T(8,128)}) custom-call(f32[1024,1024]{1,0:T(8,128)} %q_ref.2, f32[1024,1024]{1,0:T(8,128)} %k_ref.2, f32[1024,1024]{1,0:T(8,128)} %v_ref.2), custom_call_target="tpu_custom_call" | custom-call | flops 2097152 | bytes 4096 | tf_op jit(solution)/shard_map/local_levels/pallas_call | solution.py:303
  45.4 0.0 collective-permute-done.3.six_ref
  45.4 0.2 collective-permute-done.5.seven_ref
  45.7 1.5 %far_levels.1 = f32[8,72,128]{2,1,0:T(8,128)} custom-call(f32[512,128]{1,0:T(8,128)S(1)} %get-tuple-element.71.o_ref, f32[512,128]{1,0:T(8,128)S(1)} %get-tuple-element.72.lse_ref, f32[240,128]{1,0:T(8,128)S(1)} %get-tuple-element.73.q_ref, f32[2,192,128]{2,1,0:T(8,128)S(1)} %get-tuple-element.59.here_ref, ...), custom_call_target="tpu_custom_call" | custom-call | flops 104857600 | bytes 1048576 | tf_op jit(solution)/shard_map/far_levels/pallas_call | solution.py:444
  47.2 4.8 %all-to-all-start.1 = ((f32[8,72,128]{2,1,0:T(8,128)}), f32[8,72,128]{2,1,0:T(8,128)S(1)}, u32[]{:S(2)}, u32[]{:S(2)}) async-start(f32[8,72,128]{2,1,0:T(8,128)} %far_levels.1), calls=%async_computation.1 | async-start | bytes 589824 | tf_op jit(solution)/shard_map/all_to_all | solution.py:567
  51.9 0.0 collective-permute-done.6.k3_ref
  51.9 4.0 %local_levels.5 = (f32[1024,128]{1,0:T(8,128)}, f32[8,1024]{1,0:T(8,128)}) custom-call(f32[1024,1024]{1,0:T(8,128)} %q_ref.2, f32[1024,1024]{1,0:T(8,128)} %k_ref.2, f32[1024,1024]{1,0:T(8,128)} %v_ref.2), custom_call_target="tpu_custom_call" | custom-call | flops 1073741824 | bytes 2097152 | tf_op jit(solution)/shard_map/local_levels/pallas_call | solution.py:303
  55.9 1.0 %collective-permute-done.7.v3_ref = f32[128,1024]{1,0:T(8,128)S(1)} collective-permute-done((f32[128,1024]{1,0:T(8,128)S(1)}, f32[128,1024]{1,0:T(8,128)S(1)}, u32[]{:S(2)}, u32[]{:S(2)}) %collective-permute-start.7) | collective-permute-done | bytes 524320 | tf_op jit(solution)/shard_map/ppermute | solution.py:563
  56.9 2.6 %near_level.1 = (f32[128,1024]{1,0:T(8,128)}, f32[128,128]{1,0:T(8,128)}) custom-call(f32[128,1024]{1,0:T(8,128)} %get-tuple-element.87.q3_ref, f32[128,1024]{1,0:T(8,128)S(1)} %collective-permute-done.6.k3_ref, f32[128,1024]{1,0:T(8,128)S(1)} %collective-permute-done.7.v3_ref), custom_call_target="tpu_custom_call" | custom-call | flops 209715200 | bytes 2097152 | tf_op jit(solution)/shard_map/near_level/pallas_call | solution.py:466
  59.6 0.8 %all-to-all-done.1.refs_8_ = f32[8,72,128]{2,1,0:T(8,128)S(1)} async-done(((f32[8,72,128]{2,1,0:T(8,128)}), f32[8,72,128]{2,1,0:T(8,128)S(1)}, u32[]{:S(2)}, u32[]{:S(2)}) %all-to-all-start.1) | async-done | bytes 294944 | tf_op jit(solution)/shard_map/all_to_all | solution.py:567
  60.3 5.3 %join_levels.1 = f32[1024,1024]{1,0:T(8,128)} custom-call(f32[1024,640]{1,0:T(8,128)} %get-tuple-element.57.refs_0_, f32[1024,256]{1,0:T(8,128)} %get-tuple-element.70.refs_1_, f32[1024,128]{1,0:T(8,128)} %get-tuple-element.83.refs_2_, f32[8,1024]{1,0:T(8,128)} %get-tuple-element.76.refs_3_, f32[8,1024]{1,0:T(8,128)} %get-tuple-element.84.refs_4_, ...), custom_call_target="tpu_custom_call" | custom-call | flops 16777216 | bytes 9437184 | tf_op jit(solution)/shard_map/join_levels/pallas_call | solution.py:539
  (3 shorter events, 0.0 us)
Async XLA Ops:
  5.0 7.4 %collective-permute-start.2 = (f32[8,4,128]{2,1,0:T(4,128)S(1)}, f32[8,4,128]{2,1,0:T(4,128)S(1)}, u32[]{:S(2)}, u32[]{:S(2)}) collective-permute-start(f32[8,4,128]{2,1,0:T(4,128)S(1)} %get-tuple-element.51), channel_id=1, source_target_pairs={{0,96},{16,112},{32,64},{48,80},{64,32},{80,48},{96,0},{112,16},{1... | collective-permute-start | bytes 49160 | tf_op jit(solution)/shard_map/ppermute | solution.py:563
  7.9 5.2 %collective-permute-start.1 = (f32[8,4,128]{2,1,0:T(4,128)S(1)}, f32[8,4,128]{2,1,0:T(4,128)S(1)}, u32[]{:S(2)}, u32[]{:S(2)}) collective-permute-start(f32[8,4,128]{2,1,0:T(4,128)S(1)} %get-tuple-element.51), channel_id=1, source_target_pairs={{0,64},{16,80},{32,96},{48,112},{64,0},{80,16},{96,32},{112,48},{1... | collective-permute-start | bytes 49160 | tf_op jit(solution)/shard_map/ppermute | solution.py:563
  8.7 4.4 %collective-permute-start = (f32[8,8,128]{2,1,0:T(8,128)S(1)}, f32[8,8,128]{2,1,0:T(8,128)S(1)}, u32[]{:S(2)}, u32[]{:S(2)}) collective-permute-start(f32[8,8,128]{2,1,0:T(8,128)S(1)} %get-tuple-element.50), channel_id=1, source_target_pairs={{0,32},{16,48},{32,0},{48,16},{64,96},{80,112},{96,64},{112,80},{1... | collective-permute-start | bytes 98312 | tf_op jit(solution)/shard_map/ppermute | solution.py:563
  13.8 18.1 %all-to-all-start = ((f32[8,208,128]{2,1,0:T(8,128)}), f32[8,208,128]{2,1,0:T(8,128)S(1)}, u32[]{:S(2)}, u32[]{:S(2)}) async-start(f32[8,208,128]{2,1,0:T(8,128)} %pack_rows.1), calls=%async_computation | async-start | bytes 1703936 | tf_op jit(solution)/shard_map/all_to_all | solution.py:567
  20.2 11.8 %copy-start.1 = (f32[128,1024]{1,0:T(8,128)S(1)}, f32[128,1024]{1,0:T(8,128)}, u32[]{:S(2)}) copy-start(f32[128,1024]{1,0:T(8,128)} %get-tuple-element.79) | copy-start | bytes 1572868
  20.2 13.9 %copy-start = (f32[128,1024]{1,0:T(8,128)S(1)}, f32[128,1024]{1,0:T(8,128)}, u32[]{:S(2)}) copy-start(f32[128,1024]{1,0:T(8,128)} %get-tuple-element.88) | copy-start | bytes 1572868
  31.9 20.0 %collective-permute-start.6 = (f32[128,1024]{1,0:T(8,128)S(1)}, f32[128,1024]{1,0:T(8,128)S(1)}, u32[]{:S(2)}, u32[]{:S(2)}) collective-permute-start(f32[128,1024]{1,0:T(8,128)S(1)} %copy-done.1), channel_id=1, source_target_pairs={{0,1},{1,0},{2,3},{3,2},{4,5},{5,4},{6,7},{7,6},{8,9},{9,8},{10,11... | collective-permute-start | bytes 1572872 | tf_op jit(solution)/shard_map/ppermute | solution.py:563
  34.0 22.9 %collective-permute-start.7 = (f32[128,1024]{1,0:T(8,128)S(1)}, f32[128,1024]{1,0:T(8,128)S(1)}, u32[]{:S(2)}, u32[]{:S(2)}) collective-permute-start(f32[128,1024]{1,0:T(8,128)S(1)} %copy-done), channel_id=1, source_target_pairs={{0,1},{1,0},{2,3},{3,2},{4,5},{5,4},{6,7},{7,6},{8,9},{9,8},{10,11... | collective-permute-start | bytes 1572872 | tf_op jit(solution)/shard_map/ppermute | solution.py:563
  34.2 2.4 %collective-permute-start.4 = (f32[2,128,128]{2,1,0:T(8,128)S(1)}, f32[2,128,128]{2,1,0:T(8,128)S(1)}, u32[]{:S(2)}, u32[]{:S(2)}) collective-permute-start(f32[2,128,128]{2,1,0:T(8,128)S(1)} %get-tuple-element.60), channel_id=1, source_target_pairs={{0,16},{16,0},{32,48},{48,32},{64,80},{80,64},{96,112},{112,96},{1... | collective-permute-start | bytes 393224 | tf_op jit(solution)/shard_map/ppermute | solution.py:563
  34.3 11.1 %collective-permute-start.3 = (f32[2,192,128]{2,1,0:T(8,128)S(1)}, f32[2,192,128]{2,1,0:T(8,128)S(1)}, u32[]{:S(2)}, u32[]{:S(2)}) collective-permute-start(f32[2,192,128]{2,1,0:T(8,128)S(1)} %get-tuple-element.59.here_ref), channel_id=1, source_target_pairs={{0,12},{1,13},{2,14},{3,15},{4,8},{5,9},{6,10},{7,11},{8,4},{9,5},... | collective-permute-start | bytes 589832 | tf_op jit(solution)/shard_map/ppermute | solution.py:563
  36.6 9.1 %collective-permute-start.5 = (f32[2,128,128]{2,1,0:T(8,128)S(1)}, f32[2,128,128]{2,1,0:T(8,128)S(1)}, u32[]{:S(2)}, u32[]{:S(2)}) collective-permute-start(f32[2,128,128]{2,1,0:T(8,128)S(1)} %collective-permute-done.4.core_ref), channel_id=1, source_target_pairs={{0,12},{1,13},{2,14},{3,15},{4,8},{5,9},{6,10},{7,11},{8,4},{9,5},... | collective-permute-start | bytes 393224 | tf_op jit(solution)/shard_map/ppermute | solution.py:563
  47.2 13.2 %all-to-all-start.1 = ((f32[8,72,128]{2,1,0:T(8,128)}), f32[8,72,128]{2,1,0:T(8,128)S(1)}, u32[]{:S(2)}, u32[]{:S(2)}) async-start(f32[8,72,128]{2,1,0:T(8,128)} %far_levels.1), calls=%async_computation.1 | async-start | bytes 589824 | tf_op jit(solution)/shard_map/all_to_all | solution.py:567

commit v5 on v4

--- a/solution.py
+++ b/solution.py
@@ -478,13 +478,20 @@
     o3_hbm, lse3_hbm, far_ref, out_hbm = refs[2 * n : 2 * n + 4]
     own, own_lse, shares, o3, lse3, wide, stage, own_sems, sems, out_sems = refs[2 * n + 4 :]
     place = [(call, i) for call, count in enumerate(CALLS) for i in range(count)]
+    late = range(CALLS[0], HEADS)
 
     def cols(h):
         return slice(WIDTH * h, WIDTH * h + WIDTH)
 
     def fetch(h):
         call, i = place[h]
-        return pltpu.make_async_copy(own_hbm[call].at[:, cols(i)], own.at[h], own_sems.at[h])
+        j = h - CALLS[0]
+        return pltpu.make_async_copy(own_hbm[call].at[:, cols(i)], own.at[j], own_sems.at[j])
+
+    def results(h, part):
+        if h in late:
+            return own[h - CALLS[0], part, :]
+        return own_hbm[0][part, cols(h)]
 
     def send(h):
         return pltpu.make_async_copy(stage.at[h % 4], out_hbm.at[:, cols(h)], out_sems.at[h % 4])
@@ -493,7 +500,7 @@
     others += [pltpu.make_async_copy(own_lse_hbm[call], own_lse.at[call], sems.at[call + 2]) for call in range(n)]
     for copy in others:
         copy.start()
-    for h in range(HEADS):
+    for h in late:
         fetch(h).start()
 
     for h in range(HEADS):
@@ -521,13 +528,14 @@
             wide[2 + h % 2, pl.ds(c, 64, stride=2), :] = far_ref[h, 0:64, :]
         far = wide[2 + h % 2]
         rest = far + (o3[:, cols(h)] - far) * jnp.broadcast_to(near_share[:, h : h + 1], (128, WIDTH))
-        fetch(h).wait()
+        if h in late:
+            fetch(h).wait()
         if h >= 4:
             send(h - 4).wait()
         for k in range(8):
             part = slice(128 * k, 128 * k + 128)
             weight = jnp.broadcast_to(shares[part, h : h + 1], (128, WIDTH))
-            stage[h % 4, pl.ds(k, 128, stride=8), :] = rest + (own[h, part, :] - rest) * weight
+            stage[h % 4, pl.ds(k, 128, stride=8), :] = rest + (results(h, part) - rest) * weight
         send(h).start()
     for h in range(HEADS - 4, HEADS):
         send(h).wait()
@@ -535,28 +543,29 @@
 
 def join_call(own, o3, lse3, far):
     n = len(CALLS)
+    vmem = pl.BlockSpec(memory_space=pltpu.VMEM)
     anywhere = pl.BlockSpec(memory_space=pl.ANY)
     return pl.pallas_call(
         join_body,
         name="join_levels",
-        in_specs=[anywhere] * (2 * n + 2) + [pl.BlockSpec(memory_space=pltpu.VMEM)],
+        in_specs=[vmem] + [anywhere] * (2 * n + 1) + [vmem],
         out_specs=anywhere,
         out_shape=pltpu.HBM((ROWS, HEADS * WIDTH), F32),
         scratch_shapes=[
-            pltpu.VMEM((HEADS, ROWS, WIDTH), F32),
+            pltpu.VMEM((HEADS - CALLS[0], ROWS, WIDTH), F32),
             pltpu.VMEM((n + 1, HEADS, ROWS), F32),
             pltpu.VMEM((ROWS, WIDTH), F32),
             pltpu.VMEM((128, HEADS * WIDTH), F32),
             pltpu.VMEM((128, WIDTH), F32),
             pltpu.VMEM((4, 128, WIDTH), F32),
             pltpu.VMEM((4, ROWS, WIDTH), F32),
-            pltpu.SemaphoreType.DMA((HEADS,)),
+            pltpu.SemaphoreType.DMA((HEADS - CALLS[0],)),
             pltpu.SemaphoreType.DMA((n + 2,)),
             pltpu.SemaphoreType.DMA((4,)),
         ],
-        compiler_params=params(20),
+        compiler_params=params(14),
         cost_estimate=pl.CostEstimate(flops=16 << 20, bytes_accessed=9 << 20, transcendentals=1 << 20),
-    )(*[in_hbm(o) for o, _ in own], *[in_hbm(lse) for _, lse in own], in_hbm(o3), in_hbm(lse3), far)
+    )(own[0][0], *[in_hbm(o) for o, _ in own[1:]], *[in_hbm(lse) for _, lse in own], in_hbm(o3), in_hbm(lse3), far)
 
 
 def hop(x, axis, flip):
@@ -569,6 +578,7 @@
 
 def on_device(queries, keys, values):
     k3, v3, pay, x8, x9 = pool_kv_call(keys, values)
+    sib_k3 = hop(k3, "node", 1)
     first = [sum(CALLS[:i]) for i in range(len(CALLS))]
     local = []
 
@@ -580,11 +590,11 @@
     q3, pay = pool_q_call(queries, pay)
     pay = pack_call(pay, r8, r9a, r9b)
     got = transpose_heads(pay)
-    part = local_part(0, pay, weight=4096)
+    part = local_part(0, pay, weight=1)
     got, part = lax.optimization_barrier((got, part))
     local.append(part)
-    _, k3, v3 = lax.optimization_barrier((part, k3, v3))
-    sib_k3, sib_v3 = hop(k3, "node", 1), hop(v3, "node", 1)
+    v3 = lax.optimization_barrier((part, v3))[1]
+    sib_v3 = hop(v3, "node", 1)
 
     here6, here7 = rise_call(got)
     six = hop(here6, "node", 12)

time: 66.8 us -> 64.2 us (0.961); the launches traced: 65.8 us -> 63.9 us
  waiting for transfers between devices: 2.84 us -> 1.61 us
  Pallas kernels: 41.7 us -> 41 us
    ppermute x8, waiting for transfers between devices: 2.05 us -> 0.99 us  [hop(): lax.ppermute(x, axis, [(i, i ^ flip) for i in range(lax.axis_size(axis))])]
    pallas_call x1, Pallas kernels: 5.33 us -> 4.41 us  [join_call(): pl.pallas_call(join_body, name='join_levels', in_specs=[vmem] + [anywhere...]
  transfers between devices with their start and end apart: 10 -> 10, of which waited for: 4 -> 3; matrix products, arithmetic and copies ran while one was open for 0% -> 0% of each run, Pallas kernels for 47% -> 48%
where the time goes in v5:
time: 64.2 us; the launch traced here: 63.9 us
  Pallas kernels  41 us (64%)
  starting transfers between devices  21.1 us (33%)
  waiting for transfers between devices  1.61 us (3%)
    pallas_call x3, Pallas kernels, local_call(): pl.pallas_call(functools.partial(local_body, count), name='local_levels',...  21.8 us
    all_to_all x2, starting transfers between devices, transpose_heads(): return lax.all_to_all(x, 'node', 0, 0, axis_index_groups=GROUPS, tiled=True)  11.2 us
    ppermute x8, starting transfers between devices, hop(): lax.ppermute(x, axis, [(i, i ^ flip) for i in range(lax.axis_size(axis))])  9.89 us
    pallas_call x1, Pallas kernels, pool_kv_call(): pl.pallas_call(pool_kv_body, name='pool_keys', in_specs=[anywhere] * 2, o...  5 us
    pallas_call x1, Pallas kernels, join_call(): pl.pallas_call(join_body, name='join_levels', in_specs=[vmem] + [anywhere...  4.41 us
    pallas_call x1, Pallas kernels, pool_q_call(): pl.pallas_call(pool_q_body, name='pool_queries', in_specs=[anywhere] * 2,...  3.23 us
    pallas_call x1, Pallas kernels, near_call(): pl.pallas_call(near_body, name='near_level', out_shape=[pltpu.HBM((128, H...  2.8 us
    pallas_call x1, Pallas kernels, middle_call(): pl.pallas_call(middle_body, name='middle_levels', out_shape=[jax.ShapeDty...  1.51 us
  transfers between devices with their start and end apart: 10, of which 3 were waited for; matrix products, arithmetic and copies ran while one was open for 0% of the time, Pallas kernels for 48%

profile of v5, /device:TPU:0, one launch (start us, length us, event | category | flops | bytes accessed | tf_op | source)
XLA Modules:
  0.0 63.9 jit_solution(9011659686310738775)
XLA Ops:
  0.0 5.0 %pool_keys.1 = (f32[128,1024]{1,0:T(8,128)}, f32[128,1024]{1,0:T(8,128)}, f32[8,208,128]{2,1,0:T(8,128)}, f32[8,8,128]{2,1,0:T(8,128)S(1)}, f32[8,4,128]{2,1,0:T(4,128)S(1)}) custom-call(f32[1024,1024]{1,0:T(8,128)} %k_ref.2, f32[1024,1024]{1,0:T(8,128)} %v_ref.2), custom_call_target="tpu_custom_call" | custom-call | flops 2097152 | bytes 10485760 | tf_op jit(solution)/shard_map/pool_keys/pallas_call | solution.py:150
  5.0 2.9 %collective-permute-start.2 = (f32[8,4,128]{2,1,0:T(4,128)S(1)}, f32[8,4,128]{2,1,0:T(4,128)S(1)}, u32[]{:S(2)}, u32[]{:S(2)}) collective-permute-start(f32[8,4,128]{2,1,0:T(4,128)S(1)} %get-tuple-element.50), channel_id=1, source_target_pairs={{0,96},{16,112},{32,64},{48,80},{64,32},{80,48},{96,0},{112,16},{1... | collective-permute-start | bytes 49160 | tf_op jit(solution)/shard_map/ppermute | solution.py:572
  7.9 0.8 %collective-permute-start.1 = (f32[8,4,128]{2,1,0:T(4,128)S(1)}, f32[8,4,128]{2,1,0:T(4,128)S(1)}, u32[]{:S(2)}, u32[]{:S(2)}) collective-permute-start(f32[8,4,128]{2,1,0:T(4,128)S(1)} %get-tuple-element.50), channel_id=1, source_target_pairs={{0,64},{16,80},{32,96},{48,112},{64,0},{80,16},{96,32},{112,48},{1... | collective-permute-start | bytes 49160 | tf_op jit(solution)/shard_map/ppermute | solution.py:572
  8.7 0.5 collective-permute-start
  9.2 3.2 %pool_queries.1 = (f32[128,1024]{1,0:T(8,128)}, f32[8,208,128]{2,1,0:T(8,128)}) custom-call(f32[1024,1024]{1,0:T(8,128)} %q_ref.2, f32[8,208,128]{2,1,0:T(8,128)} %get-tuple-element.47.pay_in), custom_call_target="tpu_custom_call", output_to_operand_aliasing={{1}: (1, {})} | custom-call | flops 2147483648 | bytes 5242880 | tf_op jit(solution)/shard_map/pool_queries/pallas_call | solution.py:204
  12.4 0.0 collective-permute-done.2.r9b_ref
  12.4 0.7 %collective-permute-done.1.r9a_ref = f32[8,4,128]{2,1,0:T(4,128)S(1)} collective-permute-done((f32[8,4,128]{2,1,0:T(4,128)S(1)}, f32[8,4,128]{2,1,0:T(4,128)S(1)}, u32[]{:S(2)}, u32[]{:S(2)}) %collective-permute-start.1) | collective-permute-done | bytes 16416 | tf_op jit(solution)/shard_map/ppermute | solution.py:572
  13.2 0.0 collective-permute-done.r8_ref
  13.2 0.7 %pack_rows.1 = f32[8,208,128]{2,1,0:T(8,128)} custom-call(f32[8,208,128]{2,1,0:T(8,128)} %get-tuple-element.48.pay_hbm, f32[8,8,128]{2,1,0:T(8,128)S(1)} %collective-permute-done.r8_ref, f32[8,4,128]{2,1,0:T(4,128)S(1)} %collective-permute-done.1.r9a_ref, f32[8,4,128]{2,1,0:T(4,128)S(1)} %collective-permute-done.2.r9b_ref), custom_call_target="tpu_custom_call", output_to_operand_aliasing={{}: (0, {})} | custom-call | bytes 131072 | tf_op jit(solution)/shard_map/pack_rows/pallas_call | solution.py:236
  13.8 6.3 %all-to-all-start = ((f32[8,208,128]{2,1,0:T(8,128)}), f32[8,208,128]{2,1,0:T(8,128)S(1)}, u32[]{:S(2)}, u32[]{:S(2)}) async-start(f32[8,208,128]{2,1,0:T(8,128)} %pack_rows.1), calls=%async_computation | async-start | bytes 1703936 | tf_op jit(solution)/shard_map/all_to_all | solution.py:576
  20.2 2.0 %collective-permute-start.6 = (f32[128,1024]{1,0:T(8,128)}, f32[128,1024]{1,0:T(8,128)S(1)}, u32[]{:S(2)}, u32[]{:S(2)}) collective-permute-start(f32[128,1024]{1,0:T(8,128)} %get-tuple-element.75), channel_id=1, source_target_pairs={{0,1},{1,0},{2,3},{3,2},{4,5},{5,4},{6,7},{7,6},{8,9},{9,8},{10,11... | collective-permute-start | bytes 1572872 | tf_op jit(solution)/shard_map/ppermute | solution.py:572
  22.2 11.6 %local_levels.3 = (f32[1024,640]{1,0:T(8,128)}, f32[8,1024]{1,0:T(8,128)}) custom-call(f32[1024,1024]{1,0:T(8,128)} %q_ref.2, f32[1024,1024]{1,0:T(8,128)} %k_ref.2, f32[1024,1024]{1,0:T(8,128)} %v_ref.2), custom_call_target="tpu_custom_call" | custom-call | flops 5242880 | bytes 10240 | tf_op jit(solution)/shard_map/local_levels/pallas_call | solution.py:303
  33.8 0.0 all-to-all-done.got_ref
  33.8 0.1 collective-permute-start.7
  33.9 0.1 rise_rows.1
  34.0 0.1 collective-permute-start.4
  34.1 2.3 %collective-permute-start.3 = (f32[2,192,128]{2,1,0:T(8,128)S(1)}, f32[2,192,128]{2,1,0:T(8,128)S(1)}, u32[]{:S(2)}, u32[]{:S(2)}) collective-permute-start(f32[2,192,128]{2,1,0:T(8,128)S(1)} %get-tuple-element.58.here_ref), channel_id=1, source_target_pairs={{0,12},{1,13},{2,14},{3,15},{4,8},{5,9},{6,10},{7,11},{8,4},{9,5},... | collective-permute-start | bytes 589832 | tf_op jit(solution)/shard_map/ppermute | solution.py:572
  36.3 0.0 collective-permute-done.4.core_ref
  36.4 1.3 %collective-permute-start.5 = (f32[2,128,128]{2,1,0:T(8,128)S(1)}, f32[2,128,128]{2,1,0:T(8,128)S(1)}, u32[]{:S(2)}, u32[]{:S(2)}) collective-permute-start(f32[2,128,128]{2,1,0:T(8,128)S(1)} %collective-permute-done.4.core_ref), channel_id=1, source_target_pairs={{0,12},{1,13},{2,14},{3,15},{4,8},{5,9},{6,10},{7,11},{8,4},{9,5},... | collective-permute-start | bytes 393224 | tf_op jit(solution)/shard_map/ppermute | solution.py:572
  37.6 1.5 %middle_levels.1 = (f32[512,128]{1,0:T(8,128)S(1)}, f32[512,128]{1,0:T(8,128)S(1)}, f32[240,128]{1,0:T(8,128)S(1)}) custom-call(f32[8,208,128]{2,1,0:T(8,128)S(1)} %all-to-all-done.got_ref), custom_call_target="tpu_custom_call" | custom-call | flops 1048576 | bytes 65536 | tf_op jit(solution)/shard_map/middle_levels/pallas_call | solution.py:383
  39.1 6.1 %local_levels.4 = (f32[1024,256]{1,0:T(8,128)}, f32[8,1024]{1,0:T(8,128)}) custom-call(f32[1024,1024]{1,0:T(8,128)} %q_ref.2, f32[1024,1024]{1,0:T(8,128)} %k_ref.2, f32[1024,1024]{1,0:T(8,128)} %v_ref.2), custom_call_target="tpu_custom_call" | custom-call | flops 2097152 | bytes 4096 | tf_op jit(solution)/shard_map/local_levels/pallas_call | solution.py:303
  45.2 0.0 collective-permute-done.3.six_ref
  45.2 0.2 collective-permute-done.5.seven_ref
  45.4 1.5 %far_levels.1 = f32[8,72,128]{2,1,0:T(8,128)} custom-call(f32[512,128]{1,0:T(8,128)S(1)} %get-tuple-element.70.o_ref, f32[512,128]{1,0:T(8,128)S(1)} %get-tuple-element.71.lse_ref, f32[240,128]{1,0:T(8,128)S(1)} %get-tuple-element.72.q_ref, f32[2,192,128]{2,1,0:T(8,128)S(1)} %get-tuple-element.58.here_ref, ...), custom_call_target="tpu_custom_call" | custom-call | flops 104857600 | bytes 1048576 | tf_op jit(solution)/shard_map/far_levels/pallas_call | solution.py:444
  46.9 4.9 %all-to-all-start.1 = ((f32[8,72,128]{2,1,0:T(8,128)}), f32[8,72,128]{2,1,0:T(8,128)S(1)}, u32[]{:S(2)}, u32[]{:S(2)}) async-start(f32[8,72,128]{2,1,0:T(8,128)} %far_levels.1), calls=%async_computation.1 | async-start | bytes 589824 | tf_op jit(solution)/shard_map/all_to_all | solution.py:576
  51.8 0.0 collective-permute-done.6.k3_ref
  51.8 4.1 %local_levels.5 = (f32[1024,128]{1,0:T(8,128)}, f32[8,1024]{1,0:T(8,128)}) custom-call(f32[1024,1024]{1,0:T(8,128)} %q_ref.2, f32[1024,1024]{1,0:T(8,128)} %k_ref.2, f32[1024,1024]{1,0:T(8,128)} %v_ref.2), custom_call_target="tpu_custom_call" | custom-call | flops 1073741824 | bytes 2097152 | tf_op jit(solution)/shard_map/local_levels/pallas_call | solution.py:303
  55.9 0.0 collective-permute-done.7.v3_ref
  55.9 2.8 %near_level.1 = (f32[128,1024]{1,0:T(8,128)}, f32[128,128]{1,0:T(8,128)}) custom-call(f32[128,1024]{1,0:T(8,128)} %get-tuple-element.84.q3_ref, f32[128,1024]{1,0:T(8,128)S(1)} %collective-permute-done.6.k3_ref, f32[128,1024]{1,0:T(8,128)} %collective-permute-done.7.v3_ref), custom_call_target="tpu_custom_call" | custom-call | flops 209715200 | bytes 2097152 | tf_op jit(solution)/shard_map/near_level/pallas_call | solution.py:466
  58.7 0.6 all-to-all-done.1.refs_8_
  59.3 0.0 copy-done
  59.3 4.4 %join_levels.1 = f32[1024,1024]{1,0:T(8,128)} custom-call(f32[1024,640]{1,0:T(8,128)S(1)} %copy-done, f32[1024,256]{1,0:T(8,128)} %get-tuple-element.69.refs_1_, f32[1024,128]{1,0:T(8,128)} %get-tuple-element.79.refs_2_, f32[8,1024]{1,0:T(8,128)} %get-tuple-element.80.refs_3_, f32[8,1024]{1,0:T(8,128)} %get-tuple-element.81.refs_4_, ...), custom_call_target="tpu_custom_call" | custom-call | flops 16777216 | bytes 9437184 | tf_op jit(solution)/shard_map/join_levels/pallas_call | solution.py:548
  (1 shorter events, 0.0 us)
Async XLA Ops:
  5.0 7.4 %collective-permute-start.2 = (f32[8,4,128]{2,1,0:T(4,128)S(1)}, f32[8,4,128]{2,1,0:T(4,128)S(1)}, u32[]{:S(2)}, u32[]{:S(2)}) collective-permute-start(f32[8,4,128]{2,1,0:T(4,128)S(1)} %get-tuple-element.50), channel_id=1, source_target_pairs={{0,96},{16,112},{32,64},{48,80},{64,32},{80,48},{96,0},{112,16},{1... | collective-permute-start | bytes 49160 | tf_op jit(solution)/shard_map/ppermute | solution.py:572
  7.9 5.2 %collective-permute-start.1 = (f32[8,4,128]{2,1,0:T(4,128)S(1)}, f32[8,4,128]{2,1,0:T(4,128)S(1)}, u32[]{:S(2)}, u32[]{:S(2)}) collective-permute-start(f32[8,4,128]{2,1,0:T(4,128)S(1)} %get-tuple-element.50), channel_id=1, source_target_pairs={{0,64},{16,80},{32,96},{48,112},{64,0},{80,16},{96,32},{112,48},{1... | collective-permute-start | bytes 49160 | tf_op jit(solution)/shard_map/ppermute | solution.py:572
  8.7 4.4 %collective-permute-start = (f32[8,8,128]{2,1,0:T(8,128)S(1)}, f32[8,8,128]{2,1,0:T(8,128)S(1)}, u32[]{:S(2)}, u32[]{:S(2)}) collective-permute-start(f32[8,8,128]{2,1,0:T(8,128)S(1)} %get-tuple-element.49), channel_id=1, source_target_pairs={{0,32},{16,48},{32,0},{48,16},{64,96},{80,112},{96,64},{112,80},{1... | collective-permute-start | bytes 98312 | tf_op jit(solution)/shard_map/ppermute | solution.py:572
  13.8 20.0 %all-to-all-start = ((f32[8,208,128]{2,1,0:T(8,128)}), f32[8,208,128]{2,1,0:T(8,128)S(1)}, u32[]{:S(2)}, u32[]{:S(2)}) async-start(f32[8,208,128]{2,1,0:T(8,128)} %pack_rows.1), calls=%async_computation | async-start | bytes 1703936 | tf_op jit(solution)/shard_map/all_to_all | solution.py:576
  20.2 31.6 %collective-permute-start.6 = (f32[128,1024]{1,0:T(8,128)}, f32[128,1024]{1,0:T(8,128)S(1)}, u32[]{:S(2)}, u32[]{:S(2)}) collective-permute-start(f32[128,1024]{1,0:T(8,128)} %get-tuple-element.75), channel_id=1, source_target_pairs={{0,1},{1,0},{2,3},{3,2},{4,5},{5,4},{6,7},{7,6},{8,9},{9,8},{10,11... | collective-permute-start | bytes 1572872 | tf_op jit(solution)/shard_map/ppermute | solution.py:572
  33.8 22.1 %collective-permute-start.7 = (f32[128,1024]{1,0:T(8,128)}, f32[128,1024]{1,0:T(8,128)}, u32[]{:S(2)}, u32[]{:S(2)}) collective-permute-start(f32[128,1024]{1,0:T(8,128)} %get-tuple-element.86), channel_id=1, source_target_pairs={{0,1},{1,0},{2,3},{3,2},{4,5},{5,4},{6,7},{7,6},{8,9},{9,8},{10,11... | collective-permute-start | bytes 1572872 | tf_op jit(solution)/shard_map/ppermute | solution.py:572
  34.0 2.4 %collective-permute-start.4 = (f32[2,128,128]{2,1,0:T(8,128)S(1)}, f32[2,128,128]{2,1,0:T(8,128)S(1)}, u32[]{:S(2)}, u32[]{:S(2)}) collective-permute-start(f32[2,128,128]{2,1,0:T(8,128)S(1)} %get-tuple-element.59), channel_id=1, source_target_pairs={{0,16},{16,0},{32,48},{48,32},{64,80},{80,64},{96,112},{112,96},{1... | collective-permute-start | bytes 393224 | tf_op jit(solution)/shard_map/ppermute | solution.py:572
  34.1 11.1 %collective-permute-start.3 = (f32[2,192,128]{2,1,0:T(8,128)S(1)}, f32[2,192,128]{2,1,0:T(8,128)S(1)}, u32[]{:S(2)}, u32[]{:S(2)}) collective-permute-start(f32[2,192,128]{2,1,0:T(8,128)S(1)} %get-tuple-element.58.here_ref), channel_id=1, source_target_pairs={{0,12},{1,13},{2,14},{3,15},{4,8},{5,9},{6,10},{7,11},{8,4},{9,5},... | collective-permute-start | bytes 589832 | tf_op jit(solution)/shard_map/ppermute | solution.py:572
  36.4 9.1 %collective-permute-start.5 = (f32[2,128,128]{2,1,0:T(8,128)S(1)}, f32[2,128,128]{2,1,0:T(8,128)S(1)}, u32[]{:S(2)}, u32[]{:S(2)}) collective-permute-start(f32[2,128,128]{2,1,0:T(8,128)S(1)} %collective-permute-done.4.core_ref), channel_id=1, source_target_pairs={{0,12},{1,13},{2,14},{3,15},{4,8},{5,9},{6,10},{7,11},{8,4},{9,5},... | collective-permute-start | bytes 393224 | tf_op jit(solution)/shard_map/ppermute | solution.py:572
  46.9 12.4 %all-to-all-start.1 = ((f32[8,72,128]{2,1,0:T(8,128)}), f32[8,72,128]{2,1,0:T(8,128)S(1)}, u32[]{:S(2)}, u32[]{:S(2)}) async-start(f32[8,72,128]{2,1,0:T(8,128)} %far_levels.1), calls=%async_computation.1 | async-start | bytes 589824 | tf_op jit(solution)/shard_map/all_to_all | solution.py:576
  51.8 7.6 %copy-start = (f32[1024,640]{1,0:T(8,128)S(1)}, f32[1024,640]{1,0:T(8,128)}, u32[]{:S(2)}) copy-start(f32[1024,640]{1,0:T(8,128)} %get-tuple-element.56.refs_0_) | copy-start | bytes 7864324

commit v6 on v5

--- a/solution.py
+++ b/solution.py
@@ -263,17 +263,17 @@
     q1, k1, v1 = pool(q0), pool(k0), pool(v0)
     q2, k2, v2 = pool(q1), pool(k1), pool(v1)
     tasks = []
+    for p in range(4):
+        c = 32 * p
+        tasks.append((rows(q0, c, 32), rows(k0, c, 32), rows(v0, c, 32), 0))
+    for p in range(4):
+        c = 32 * (p ^ 1)
+        tasks.append((rows(q1, 32 * p, 32), rows(k1, c, 32), rows(v1, c, 32), 1))
     for b in range(2):
         c = 64 * (b ^ 1)
         tasks.append((rows(q2, 64 * b, 64), rows(k2, c, 64), rows(v2, c, 64), 2))
-    for p in range(4):
-        c = 32 * (p ^ 1)
-        tasks.append((rows(q1, 32 * p, 32), rows(k1, c, 32), rows(v1, c, 32), 1))
-    for p in range(4):
-        c = 32 * p
-        tasks.append((rows(q0, c, 32), rows(k0, c, 32), rows(v0, c, 32), 0))
     done = attend_all(tasks)
-    at2, at1, at0 = done[:2], done[2:6], done[6:]
+    at0, at1, at2 = done[:4], done[4:8], done[8:]
 
     lane = lax.broadcasted_iota(jnp.int32, (128, WIDTH), 1)
     lses = [[None] * 4 for _ in range(8)]

time: 64.2 us -> 63 us (0.981)
  Pallas kernels: 41 us -> 39.4 us
    pallas_call x3, Pallas kernels: 21.8 us -> 20.2 us  [local_call(): pl.pallas_call(functools.partial(local_body, count), name='local_levels',...]
  transfers between devices with their start and end apart: 10 -> 10, of which waited for: 3 -> 3; matrix products, arithmetic and copies ran while one was open for 0% -> 0% of each run, Pallas kernels for 48% -> 47%
where the time goes in v6:
time: 63 us; the launch traced here: 62.6 us
  Pallas kernels  39.4 us (63%)
  starting transfers between devices  21 us (33%)
  waiting for transfers between devices  1.92 us (3%)
    pallas_call x3, Pallas kernels, local_call(): pl.pallas_call(functools.partial(local_body, count), name='local_levels',...  20.2 us
    all_to_all x2, starting transfers between devices, transpose_heads(): return lax.all_to_all(x, 'node', 0, 0, axis_index_groups=GROUPS, tiled=True)  10.6 us
    ppermute x8, starting transfers between devices, hop(): lax.ppermute(x, axis, [(i, i ^ flip) for i in range(lax.axis_size(axis))])  10.4 us
    pallas_call x1, Pallas kernels, pool_kv_call(): pl.pallas_call(pool_kv_body, name='pool_keys', in_specs=[anywhere] * 2, o...  5 us
    pallas_call x1, Pallas kernels, join_call(): pl.pallas_call(join_body, name='join_levels', in_specs=[vmem] + [anywhere...  4.41 us
    pallas_call x1, Pallas kernels, pool_q_call(): pl.pallas_call(pool_q_body, name='pool_queries', in_specs=[anywhere] * 2,...  3.23 us
    pallas_call x1, Pallas kernels, near_call(): pl.pallas_call(near_body, name='near_level', out_shape=[pltpu.HBM((128, H...  2.79 us
    pallas_call x1, Pallas kernels, middle_call(): pl.pallas_call(middle_body, name='middle_levels', out_shape=[jax.ShapeDty...  1.51 us
  transfers between devices with their start and end apart: 10, of which 3 were waited for; matrix products, arithmetic and copies ran while one was open for 0% of the time, Pallas kernels for 47%

profile of v6, /device:TPU:0, one launch (start us, length us, event | category | flops | bytes accessed | tf_op | source)
XLA Modules:
  0.0 62.6 jit_solution(16989486330020214310)
XLA Ops:
  0.0 5.0 %pool_keys.1 = (f32[128,1024]{1,0:T(8,128)}, f32[128,1024]{1,0:T(8,128)}, f32[8,208,128]{2,1,0:T(8,128)}, f32[8,8,128]{2,1,0:T(8,128)S(1)}, f32[8,4,128]{2,1,0:T(4,128)S(1)}) custom-call(f32[1024,1024]{1,0:T(8,128)} %k_ref.2, f32[1024,1024]{1,0:T(8,128)} %v_ref.2), custom_call_target="tpu_custom_call" | custom-call | flops 2097152 | bytes 10485760 | tf_op jit(solution)/shard_map/pool_keys/pallas_call | solution.py:150
  5.0 2.9 %collective-permute-start.2 = (f32[8,4,128]{2,1,0:T(4,128)S(1)}, f32[8,4,128]{2,1,0:T(4,128)S(1)}, u32[]{:S(2)}, u32[]{:S(2)}) collective-permute-start(f32[8,4,128]{2,1,0:T(4,128)S(1)} %get-tuple-element.50), channel_id=1, source_target_pairs={{0,96},{16,112},{32,64},{48,80},{64,32},{80,48},{96,0},{112,16},{1... | collective-permute-start | bytes 49160 | tf_op jit(solution)/shard_map/ppermute | solution.py:572
  7.9 0.8 %collective-permute-start.1 = (f32[8,4,128]{2,1,0:T(4,128)S(1)}, f32[8,4,128]{2,1,0:T(4,128)S(1)}, u32[]{:S(2)}, u32[]{:S(2)}) collective-permute-start(f32[8,4,128]{2,1,0:T(4,128)S(1)} %get-tuple-element.50), channel_id=1, source_target_pairs={{0,64},{16,80},{32,96},{48,112},{64,0},{80,16},{96,32},{112,48},{1... | collective-permute-start | bytes 49160 | tf_op jit(solution)/shard_map/ppermute | solution.py:572
  8.7 0.5 collective-permute-start
  9.2 3.2 %pool_queries.1 = (f32[128,1024]{1,0:T(8,128)}, f32[8,208,128]{2,1,0:T(8,128)}) custom-call(f32[1024,1024]{1,0:T(8,128)} %q_ref.2, f32[8,208,128]{2,1,0:T(8,128)} %get-tuple-element.47.pay_in), custom_call_target="tpu_custom_call", output_to_operand_aliasing={{1}: (1, {})} | custom-call | flops 2147483648 | bytes 5242880 | tf_op jit(solution)/shard_map/pool_queries/pallas_call | solution.py:204
  12.4 0.0 collective-permute-done.2.r9b_ref
  12.4 0.7 %collective-permute-done.1.r9a_ref = f32[8,4,128]{2,1,0:T(4,128)S(1)} collective-permute-done((f32[8,4,128]{2,1,0:T(4,128)S(1)}, f32[8,4,128]{2,1,0:T(4,128)S(1)}, u32[]{:S(2)}, u32[]{:S(2)}) %collective-permute-start.1) | collective-permute-done | bytes 16416 | tf_op jit(solution)/shard_map/ppermute | solution.py:572
  13.2 0.0 collective-permute-done.r8_ref
  13.2 0.7 %pack_rows.1 = f32[8,208,128]{2,1,0:T(8,128)} custom-call(f32[8,208,128]{2,1,0:T(8,128)} %get-tuple-element.48.pay_hbm, f32[8,8,128]{2,1,0:T(8,128)S(1)} %collective-permute-done.r8_ref, f32[8,4,128]{2,1,0:T(4,128)S(1)} %collective-permute-done.1.r9a_ref, f32[8,4,128]{2,1,0:T(4,128)S(1)} %collective-permute-done.2.r9b_ref), custom_call_target="tpu_custom_call", output_to_operand_aliasing={{}: (0, {})} | custom-call | bytes 131072 | tf_op jit(solution)/shard_map/pack_rows/pallas_call | solution.py:236
  13.8 6.3 %all-to-all-start = ((f32[8,208,128]{2,1,0:T(8,128)}), f32[8,208,128]{2,1,0:T(8,128)S(1)}, u32[]{:S(2)}, u32[]{:S(2)}) async-start(f32[8,208,128]{2,1,0:T(8,128)} %pack_rows.1), calls=%async_computation | async-start | bytes 1703936 | tf_op jit(solution)/shard_map/all_to_all | solution.py:576
  20.2 2.0 %collective-permute-start.6 = (f32[128,1024]{1,0:T(8,128)}, f32[128,1024]{1,0:T(8,128)S(1)}, u32[]{:S(2)}, u32[]{:S(2)}) collective-permute-start(f32[128,1024]{1,0:T(8,128)} %get-tuple-element.75), channel_id=1, source_target_pairs={{0,1},{1,0},{2,3},{3,2},{4,5},{5,4},{6,7},{7,6},{8,9},{9,8},{10,11... | collective-permute-start | bytes 1572872 | tf_op jit(solution)/shard_map/ppermute | solution.py:572
  22.2 10.6 %local_levels.3 = (f32[1024,640]{1,0:T(8,128)}, f32[8,1024]{1,0:T(8,128)}) custom-call(f32[1024,1024]{1,0:T(8,128)} %q_ref.2, f32[1024,1024]{1,0:T(8,128)} %k_ref.2, f32[1024,1024]{1,0:T(8,128)} %v_ref.2), custom_call_target="tpu_custom_call" | custom-call | flops 5242880 | bytes 10240 | tf_op jit(solution)/shard_map/local_levels/pallas_call | solution.py:303
  32.8 0.0 all-to-all-done.got_ref
  32.8 0.6 collective-permute-start.7
  33.4 0.1 rise_rows.1
  33.5 0.1 collective-permute-start.4
  33.6 2.3 %collective-permute-start.3 = (f32[2,192,128]{2,1,0:T(8,128)S(1)}, f32[2,192,128]{2,1,0:T(8,128)S(1)}, u32[]{:S(2)}, u32[]{:S(2)}) collective-permute-start(f32[2,192,128]{2,1,0:T(8,128)S(1)} %get-tuple-element.58.here_ref), channel_id=1, source_target_pairs={{0,12},{1,13},{2,14},{3,15},{4,8},{5,9},{6,10},{7,11},{8,4},{9,5},... | collective-permute-start | bytes 589832 | tf_op jit(solution)/shard_map/ppermute | solution.py:572
  35.8 0.0 collective-permute-done.4.core_ref
  35.8 1.3 %collective-permute-start.5 = (f32[2,128,128]{2,1,0:T(8,128)S(1)}, f32[2,128,128]{2,1,0:T(8,128)S(1)}, u32[]{:S(2)}, u32[]{:S(2)}) collective-permute-start(f32[2,128,128]{2,1,0:T(8,128)S(1)} %collective-permute-done.4.core_ref), channel_id=1, source_target_pairs={{0,12},{1,13},{2,14},{3,15},{4,8},{5,9},{6,10},{7,11},{8,4},{9,5},... | collective-permute-start | bytes 393224 | tf_op jit(solution)/shard_map/ppermute | solution.py:572
  37.1 1.5 %middle_levels.1 = (f32[512,128]{1,0:T(8,128)S(1)}, f32[512,128]{1,0:T(8,128)S(1)}, f32[240,128]{1,0:T(8,128)S(1)}) custom-call(f32[8,208,128]{2,1,0:T(8,128)S(1)} %all-to-all-done.got_ref), custom_call_target="tpu_custom_call" | custom-call | flops 1048576 | bytes 65536 | tf_op jit(solution)/shard_map/middle_levels/pallas_call | solution.py:383
  38.6 5.7 %local_levels.4 = (f32[1024,256]{1,0:T(8,128)}, f32[8,1024]{1,0:T(8,128)}) custom-call(f32[1024,1024]{1,0:T(8,128)} %q_ref.2, f32[1024,1024]{1,0:T(8,128)} %k_ref.2, f32[1024,1024]{1,0:T(8,128)} %v_ref.2), custom_call_target="tpu_custom_call" | custom-call | flops 2097152 | bytes 4096 | tf_op jit(solution)/shard_map/local_levels/pallas_call | solution.py:303
  44.3 0.0 collective-permute-done.3.six_ref
  44.3 0.6 collective-permute-done.5.seven_ref
  44.9 1.5 %far_levels.1 = f32[8,72,128]{2,1,0:T(8,128)} custom-call(f32[512,128]{1,0:T(8,128)S(1)} %get-tuple-element.70.o_ref, f32[512,128]{1,0:T(8,128)S(1)} %get-tuple-element.71.lse_ref, f32[240,128]{1,0:T(8,128)S(1)} %get-tuple-element.72.q_ref, f32[2,192,128]{2,1,0:T(8,128)S(1)} %get-tuple-element.58.here_ref, ...), custom_call_target="tpu_custom_call" | custom-call | flops 104857600 | bytes 1048576 | tf_op jit(solution)/shard_map/far_levels/pallas_call | solution.py:444
  46.4 4.3 %all-to-all-start.1 = ((f32[8,72,128]{2,1,0:T(8,128)}), f32[8,72,128]{2,1,0:T(8,128)S(1)}, u32[]{:S(2)}, u32[]{:S(2)}) async-start(f32[8,72,128]{2,1,0:T(8,128)} %far_levels.1), calls=%async_computation.1 | async-start | bytes 589824 | tf_op jit(solution)/shard_map/all_to_all | solution.py:576
  50.7 0.0 collective-permute-done.6.k3_ref
  50.7 4.0 %local_levels.5 = (f32[1024,128]{1,0:T(8,128)}, f32[8,1024]{1,0:T(8,128)}) custom-call(f32[1024,1024]{1,0:T(8,128)} %q_ref.2, f32[1024,1024]{1,0:T(8,128)} %k_ref.2, f32[1024,1024]{1,0:T(8,128)} %v_ref.2), custom_call_target="tpu_custom_call" | custom-call | flops 1073741824 | bytes 2097152 | tf_op jit(solution)/shard_map/local_levels/pallas_call | solution.py:303
  54.7 0.0 collective-permute-done.7.v3_ref
  54.7 2.8 %near_level.1 = (f32[128,1024]{1,0:T(8,128)}, f32[128,128]{1,0:T(8,128)}) custom-call(f32[128,1024]{1,0:T(8,128)} %get-tuple-element.84.q3_ref, f32[128,1024]{1,0:T(8,128)S(1)} %collective-permute-done.6.k3_ref, f32[128,1024]{1,0:T(8,128)} %collective-permute-done.7.v3_ref), custom_call_target="tpu_custom_call" | custom-call | flops 209715200 | bytes 2097152 | tf_op jit(solution)/shard_map/near_level/pallas_call | solution.py:466
  57.5 0.5 all-to-all-done.1.refs_8_
  58.0 0.0 copy-done
  58.0 4.4 %join_levels.1 = f32[1024,1024]{1,0:T(8,128)} custom-call(f32[1024,640]{1,0:T(8,128)S(1)} %copy-done, f32[1024,256]{1,0:T(8,128)} %get-tuple-element.69.refs_1_, f32[1024,128]{1,0:T(8,128)} %get-tuple-element.79.refs_2_, f32[8,1024]{1,0:T(8,128)} %get-tuple-element.80.refs_3_, f32[8,1024]{1,0:T(8,128)} %get-tuple-element.81.refs_4_, ...), custom_call_target="tpu_custom_call" | custom-call | flops 16777216 | bytes 9437184 | tf_op jit(solution)/shard_map/join_levels/pallas_call | solution.py:548
  (1 shorter events, 0.0 us)
Async XLA Ops:
  5.0 7.4 %collective-permute-start.2 = (f32[8,4,128]{2,1,0:T(4,128)S(1)}, f32[8,4,128]{2,1,0:T(4,128)S(1)}, u32[]{:S(2)}, u32[]{:S(2)}) collective-permute-start(f32[8,4,128]{2,1,0:T(4,128)S(1)} %get-tuple-element.50), channel_id=1, source_target_pairs={{0,96},{16,112},{32,64},{48,80},{64,32},{80,48},{96,0},{112,16},{1... | collective-permute-start | bytes 49160 | tf_op jit(solution)/shard_map/ppermute | solution.py:572
  7.9 5.2 %collective-permute-start.1 = (f32[8,4,128]{2,1,0:T(4,128)S(1)}, f32[8,4,128]{2,1,0:T(4,128)S(1)}, u32[]{:S(2)}, u32[]{:S(2)}) collective-permute-start(f32[8,4,128]{2,1,0:T(4,128)S(1)} %get-tuple-element.50), channel_id=1, source_target_pairs={{0,64},{16,80},{32,96},{48,112},{64,0},{80,16},{96,32},{112,48},{1... | collective-permute-start | bytes 49160 | tf_op jit(solution)/shard_map/ppermute | solution.py:572
  8.7 4.4 %collective-permute-start = (f32[8,8,128]{2,1,0:T(8,128)S(1)}, f32[8,8,128]{2,1,0:T(8,128)S(1)}, u32[]{:S(2)}, u32[]{:S(2)}) collective-permute-start(f32[8,8,128]{2,1,0:T(8,128)S(1)} %get-tuple-element.49), channel_id=1, source_target_pairs={{0,32},{16,48},{32,0},{48,16},{64,96},{80,112},{96,64},{112,80},{1... | collective-permute-start | bytes 98312 | tf_op jit(solution)/shard_map/ppermute | solution.py:572
  13.8 18.9 %all-to-all-start = ((f32[8,208,128]{2,1,0:T(8,128)}), f32[8,208,128]{2,1,0:T(8,128)S(1)}, u32[]{:S(2)}, u32[]{:S(2)}) async-start(f32[8,208,128]{2,1,0:T(8,128)} %pack_rows.1), calls=%async_computation | async-start | bytes 1703936 | tf_op jit(solution)/shard_map/all_to_all | solution.py:576
  20.2 30.5 %collective-permute-start.6 = (f32[128,1024]{1,0:T(8,128)}, f32[128,1024]{1,0:T(8,128)S(1)}, u32[]{:S(2)}, u32[]{:S(2)}) collective-permute-start(f32[128,1024]{1,0:T(8,128)} %get-tuple-element.75), channel_id=1, source_target_pairs={{0,1},{1,0},{2,3},{3,2},{4,5},{5,4},{6,7},{7,6},{8,9},{9,8},{10,11... | collective-permute-start | bytes 1572872 | tf_op jit(solution)/shard_map/ppermute | solution.py:572
  32.8 21.9 %collective-permute-start.7 = (f32[128,1024]{1,0:T(8,128)}, f32[128,1024]{1,0:T(8,128)}, u32[]{:S(2)}, u32[]{:S(2)}) collective-permute-start(f32[128,1024]{1,0:T(8,128)} %get-tuple-element.86), channel_id=1, source_target_pairs={{0,1},{1,0},{2,3},{3,2},{4,5},{5,4},{6,7},{7,6},{8,9},{9,8},{10,11... | collective-permute-start | bytes 1572872 | tf_op jit(solution)/shard_map/ppermute | solution.py:572
  33.5 2.4 %collective-permute-start.4 = (f32[2,128,128]{2,1,0:T(8,128)S(1)}, f32[2,128,128]{2,1,0:T(8,128)S(1)}, u32[]{:S(2)}, u32[]{:S(2)}) collective-permute-start(f32[2,128,128]{2,1,0:T(8,128)S(1)} %get-tuple-element.59), channel_id=1, source_target_pairs={{0,16},{16,0},{32,48},{48,32},{64,80},{80,64},{96,112},{112,96},{1... | collective-permute-start | bytes 393224 | tf_op jit(solution)/shard_map/ppermute | solution.py:572
  33.6 10.7 %collective-permute-start.3 = (f32[2,192,128]{2,1,0:T(8,128)S(1)}, f32[2,192,128]{2,1,0:T(8,128)S(1)}, u32[]{:S(2)}, u32[]{:S(2)}) collective-permute-start(f32[2,192,128]{2,1,0:T(8,128)S(1)} %get-tuple-element.58.here_ref), channel_id=1, source_target_pairs={{0,12},{1,13},{2,14},{3,15},{4,8},{5,9},{6,10},{7,11},{8,4},{9,5},... | collective-permute-start | bytes 589832 | tf_op jit(solution)/shard_map/ppermute | solution.py:572
  35.8 9.1 %collective-permute-start.5 = (f32[2,128,128]{2,1,0:T(8,128)S(1)}, f32[2,128,128]{2,1,0:T(8,128)S(1)}, u32[]{:S(2)}, u32[]{:S(2)}) collective-permute-start(f32[2,128,128]{2,1,0:T(8,128)S(1)} %collective-permute-done.4.core_ref), channel_id=1, source_target_pairs={{0,12},{1,13},{2,14},{3,15},{4,8},{5,9},{6,10},{7,11},{8,4},{9,5},... | collective-permute-start | bytes 393224 | tf_op jit(solution)/shard_map/ppermute | solution.py:572
  46.4 11.6 %all-to-all-start.1 = ((f32[8,72,128]{2,1,0:T(8,128)}), f32[8,72,128]{2,1,0:T(8,128)S(1)}, u32[]{:S(2)}, u32[]{:S(2)}) async-start(f32[8,72,128]{2,1,0:T(8,128)} %far_levels.1), calls=%async_computation.1 | async-start | bytes 589824 | tf_op jit(solution)/shard_map/all_to_all | solution.py:576
  50.7 7.4 %copy-start = (f32[1024,640]{1,0:T(8,128)S(1)}, f32[1024,640]{1,0:T(8,128)}, u32[]{:S(2)}) copy-start(f32[1024,640]{1,0:T(8,128)} %get-tuple-element.56.refs_0_) | copy-start | bytes 7864324

commit v7 on v6

--- a/solution.py
+++ b/solution.py
@@ -62,7 +62,7 @@
 
 def weigh(p, side):
     hi, lo = side
-    p_hi, p_lo = split(p)
+    p_hi, p_lo = p
     if hi.shape[0] == 128:
         left = jnp.concatenate([p_hi, p_lo], axis=1)
         right = jnp.concatenate(
@@ -79,7 +79,8 @@
     peaks = [jnp.max(s, axis=1, keepdims=True) for s in grids]
     weights = [jnp.exp2(s - peak) for s, peak in zip(grids, peaks)]
     totals = [jnp.sum(p, axis=1, keepdims=True) for p in weights]
-    numerators = [weigh(p, split(task[2])) for p, task in zip(weights, tasks)]
+    halves = [split(p) for p in weights]
+    numerators = [weigh(p, split(task[2])) for p, task in zip(halves, tasks)]
     return [(peak + float(task[3]), t, n) for peak, t, n, task in zip(peaks, totals, numerators, tasks)]
 
 

time: 63 us -> 63 us (level)
  no operation moved by 1% of the time
where the time goes in v7:
time: 63 us; the launch traced here: 62.6 us
  Pallas kernels  39.4 us (63%)
  starting transfers between devices  21 us (33%)
  waiting for transfers between devices  1.92 us (3%)
    pallas_call x3, Pallas kernels, local_call(): pl.pallas_call(functools.partial(local_body, count), name='local_levels',...  20.2 us
    all_to_all x2, starting transfers between devices, transpose_heads(): return lax.all_to_all(x, 'node', 0, 0, axis_index_groups=GROUPS, tiled=True)  10.6 us
    ppermute x8, starting transfers between devices, hop(): lax.ppermute(x, axis, [(i, i ^ flip) for i in range(lax.axis_size(axis))])  10.4 us
    pallas_call x1, Pallas kernels, pool_kv_call(): pl.pallas_call(pool_kv_body, name='pool_keys', in_specs=[anywhere] * 2, o...  5 us
    pallas_call x1, Pallas kernels, join_call(): pl.pallas_call(join_body, name='join_levels', in_specs=[vmem] + [anywhere...  4.41 us
    pallas_call x1, Pallas kernels, pool_q_call(): pl.pallas_call(pool_q_body, name='pool_queries', in_specs=[anywhere] * 2,...  3.23 us
    pallas_call x1, Pallas kernels, near_call(): pl.pallas_call(near_body, name='near_level', out_shape=[pltpu.HBM((128, H...  2.79 us
    pallas_call x1, Pallas kernels, middle_call(): pl.pallas_call(middle_body, name='middle_levels', out_shape=[jax.ShapeDty...  1.51 us
  transfers between devices with their start and end apart: 10, of which 3 were waited for; matrix products, arithmetic and copies ran while one was open for 0% of the time, Pallas kernels for 47%

profile of v7, /device:TPU:0, one launch (start us, length us, event | category | flops | bytes accessed | tf_op | source)
XLA Modules:
  0.0 62.6 jit_solution(16989486330020214310)
XLA Ops:
  0.0 5.0 %pool_keys.1 = (f32[128,1024]{1,0:T(8,128)}, f32[128,1024]{1,0:T(8,128)}, f32[8,208,128]{2,1,0:T(8,128)}, f32[8,8,128]{2,1,0:T(8,128)S(1)}, f32[8,4,128]{2,1,0:T(4,128)S(1)}) custom-call(f32[1024,1024]{1,0:T(8,128)} %k_ref.2, f32[1024,1024]{1,0:T(8,128)} %v_ref.2), custom_call_target="tpu_custom_call" | custom-call | flops 2097152 | bytes 10485760 | tf_op jit(solution)/shard_map/pool_keys/pallas_call | solution.py:151
  5.0 2.9 %collective-permute-start.2 = (f32[8,4,128]{2,1,0:T(4,128)S(1)}, f32[8,4,128]{2,1,0:T(4,128)S(1)}, u32[]{:S(2)}, u32[]{:S(2)}) collective-permute-start(f32[8,4,128]{2,1,0:T(4,128)S(1)} %get-tuple-element.50), channel_id=1, source_target_pairs={{0,96},{16,112},{32,64},{48,80},{64,32},{80,48},{96,0},{112,16},{1... | collective-permute-start | bytes 49160 | tf_op jit(solution)/shard_map/ppermute | solution.py:573
  7.9 0.8 %collective-permute-start.1 = (f32[8,4,128]{2,1,0:T(4,128)S(1)}, f32[8,4,128]{2,1,0:T(4,128)S(1)}, u32[]{:S(2)}, u32[]{:S(2)}) collective-permute-start(f32[8,4,128]{2,1,0:T(4,128)S(1)} %get-tuple-element.50), channel_id=1, source_target_pairs={{0,64},{16,80},{32,96},{48,112},{64,0},{80,16},{96,32},{112,48},{1... | collective-permute-start | bytes 49160 | tf_op jit(solution)/shard_map/ppermute | solution.py:573
  8.7 0.5 collective-permute-start
  9.2 3.2 %pool_queries.1 = (f32[128,1024]{1,0:T(8,128)}, f32[8,208,128]{2,1,0:T(8,128)}) custom-call(f32[1024,1024]{1,0:T(8,128)} %q_ref.2, f32[8,208,128]{2,1,0:T(8,128)} %get-tuple-element.47.pay_in), custom_call_target="tpu_custom_call", output_to_operand_aliasing={{1}: (1, {})} | custom-call | flops 2147483648 | bytes 5242880 | tf_op jit(solution)/shard_map/pool_queries/pallas_call | solution.py:205
  12.4 0.0 collective-permute-done.2.r9b_ref
  12.4 0.7 %collective-permute-done.1.r9a_ref = f32[8,4,128]{2,1,0:T(4,128)S(1)} collective-permute-done((f32[8,4,128]{2,1,0:T(4,128)S(1)}, f32[8,4,128]{2,1,0:T(4,128)S(1)}, u32[]{:S(2)}, u32[]{:S(2)}) %collective-permute-start.1) | collective-permute-done | bytes 16416 | tf_op jit(solution)/shard_map/ppermute | solution.py:573
  13.2 0.0 collective-permute-done.r8_ref
  13.2 0.7 %pack_rows.1 = f32[8,208,128]{2,1,0:T(8,128)} custom-call(f32[8,208,128]{2,1,0:T(8,128)} %get-tuple-element.48.pay_hbm, f32[8,8,128]{2,1,0:T(8,128)S(1)} %collective-permute-done.r8_ref, f32[8,4,128]{2,1,0:T(4,128)S(1)} %collective-permute-done.1.r9a_ref, f32[8,4,128]{2,1,0:T(4,128)S(1)} %collective-permute-done.2.r9b_ref), custom_call_target="tpu_custom_call", output_to_operand_aliasing={{}: (0, {})} | custom-call | bytes 131072 | tf_op jit(solution)/shard_map/pack_rows/pallas_call | solution.py:237
  13.8 6.3 %all-to-all-start = ((f32[8,208,128]{2,1,0:T(8,128)}), f32[8,208,128]{2,1,0:T(8,128)S(1)}, u32[]{:S(2)}, u32[]{:S(2)}) async-start(f32[8,208,128]{2,1,0:T(8,128)} %pack_rows.1), calls=%async_computation | async-start | bytes 1703936 | tf_op jit(solution)/shard_map/all_to_all | solution.py:577
  20.2 2.0 %collective-permute-start.6 = (f32[128,1024]{1,0:T(8,128)}, f32[128,1024]{1,0:T(8,128)S(1)}, u32[]{:S(2)}, u32[]{:S(2)}) collective-permute-start(f32[128,1024]{1,0:T(8,128)} %get-tuple-element.75), channel_id=1, source_target_pairs={{0,1},{1,0},{2,3},{3,2},{4,5},{5,4},{6,7},{7,6},{8,9},{9,8},{10,11... | collective-permute-start | bytes 1572872 | tf_op jit(solution)/shard_map/ppermute | solution.py:573
  22.2 10.6 %local_levels.3 = (f32[1024,640]{1,0:T(8,128)}, f32[8,1024]{1,0:T(8,128)}) custom-call(f32[1024,1024]{1,0:T(8,128)} %q_ref.2, f32[1024,1024]{1,0:T(8,128)} %k_ref.2, f32[1024,1024]{1,0:T(8,128)} %v_ref.2), custom_call_target="tpu_custom_call" | custom-call | flops 5242880 | bytes 10240 | tf_op jit(solution)/shard_map/local_levels/pallas_call | solution.py:304
  32.8 0.0 all-to-all-done.got_ref
  32.8 0.6 collective-permute-start.7
  33.4 0.1 rise_rows.1
  33.5 0.1 collective-permute-start.4
  33.6 2.3 %collective-permute-start.3 = (f32[2,192,128]{2,1,0:T(8,128)S(1)}, f32[2,192,128]{2,1,0:T(8,128)S(1)}, u32[]{:S(2)}, u32[]{:S(2)}) collective-permute-start(f32[2,192,128]{2,1,0:T(8,128)S(1)} %get-tuple-element.58.here_ref), channel_id=1, source_target_pairs={{0,12},{1,13},{2,14},{3,15},{4,8},{5,9},{6,10},{7,11},{8,4},{9,5},... | collective-permute-start | bytes 589832 | tf_op jit(solution)/shard_map/ppermute | solution.py:573
  35.8 0.0 collective-permute-done.4.core_ref
  35.8 1.3 %collective-permute-start.5 = (f32[2,128,128]{2,1,0:T(8,128)S(1)}, f32[2,128,128]{2,1,0:T(8,128)S(1)}, u32[]{:S(2)}, u32[]{:S(2)}) collective-permute-start(f32[2,128,128]{2,1,0:T(8,128)S(1)} %collective-permute-done.4.core_ref), channel_id=1, source_target_pairs={{0,12},{1,13},{2,14},{3,15},{4,8},{5,9},{6,10},{7,11},{8,4},{9,5},... | collective-permute-start | bytes 393224 | tf_op jit(solution)/shard_map/ppermute | solution.py:573
  37.1 1.5 %middle_levels.1 = (f32[512,128]{1,0:T(8,128)S(1)}, f32[512,128]{1,0:T(8,128)S(1)}, f32[240,128]{1,0:T(8,128)S(1)}) custom-call(f32[8,208,128]{2,1,0:T(8,128)S(1)} %all-to-all-done.got_ref), custom_call_target="tpu_custom_call" | custom-call | flops 1048576 | bytes 65536 | tf_op jit(solution)/shard_map/middle_levels/pallas_call | solution.py:384
  38.6 5.7 %local_levels.4 = (f32[1024,256]{1,0:T(8,128)}, f32[8,1024]{1,0:T(8,128)}) custom-call(f32[1024,1024]{1,0:T(8,128)} %q_ref.2, f32[1024,1024]{1,0:T(8,128)} %k_ref.2, f32[1024,1024]{1,0:T(8,128)} %v_ref.2), custom_call_target="tpu_custom_call" | custom-call | flops 2097152 | bytes 4096 | tf_op jit(solution)/shard_map/local_levels/pallas_call | solution.py:304
  44.3 0.0 collective-permute-done.3.six_ref
  44.3 0.6 collective-permute-done.5.seven_ref
  44.9 1.5 %far_levels.1 = f32[8,72,128]{2,1,0:T(8,128)} custom-call(f32[512,128]{1,0:T(8,128)S(1)} %get-tuple-element.70.o_ref, f32[512,128]{1,0:T(8,128)S(1)} %get-tuple-element.71.lse_ref, f32[240,128]{1,0:T(8,128)S(1)} %get-tuple-element.72.q_ref, f32[2,192,128]{2,1,0:T(8,128)S(1)} %get-tuple-element.58.here_ref, ...), custom_call_target="tpu_custom_call" | custom-call | flops 104857600 | bytes 1048576 | tf_op jit(solution)/shard_map/far_levels/pallas_call | solution.py:445
  46.4 4.3 %all-to-all-start.1 = ((f32[8,72,128]{2,1,0:T(8,128)}), f32[8,72,128]{2,1,0:T(8,128)S(1)}, u32[]{:S(2)}, u32[]{:S(2)}) async-start(f32[8,72,128]{2,1,0:T(8,128)} %far_levels.1), calls=%async_computation.1 | async-start | bytes 589824 | tf_op jit(solution)/shard_map/all_to_all | solution.py:577
  50.7 0.0 collective-permute-done.6.k3_ref
  50.7 4.0 %local_levels.5 = (f32[1024,128]{1,0:T(8,128)}, f32[8,1024]{1,0:T(8,128)}) custom-call(f32[1024,1024]{1,0:T(8,128)} %q_ref.2, f32[1024,1024]{1,0:T(8,128)} %k_ref.2, f32[1024,1024]{1,0:T(8,128)} %v_ref.2), custom_call_target="tpu_custom_call" | custom-call | flops 1073741824 | bytes 2097152 | tf_op jit(solution)/shard_map/local_levels/pallas_call | solution.py:304
  54.7 0.0 collective-permute-done.7.v3_ref
  54.7 2.8 %near_level.1 = (f32[128,1024]{1,0:T(8,128)}, f32[128,128]{1,0:T(8,128)}) custom-call(f32[128,1024]{1,0:T(8,128)} %get-tuple-element.84.q3_ref, f32[128,1024]{1,0:T(8,128)S(1)} %collective-permute-done.6.k3_ref, f32[128,1024]{1,0:T(8,128)} %collective-permute-done.7.v3_ref), custom_call_target="tpu_custom_call" | custom-call | flops 209715200 | bytes 2097152 | tf_op jit(solution)/shard_map/near_level/pallas_call | solution.py:467
  57.5 0.5 all-to-all-done.1.refs_8_
  58.0 0.0 copy-done
  58.0 4.4 %join_levels.1 = f32[1024,1024]{1,0:T(8,128)} custom-call(f32[1024,640]{1,0:T(8,128)S(1)} %copy-done, f32[1024,256]{1,0:T(8,128)} %get-tuple-element.69.refs_1_, f32[1024,128]{1,0:T(8,128)} %get-tuple-element.79.refs_2_, f32[8,1024]{1,0:T(8,128)} %get-tuple-element.80.refs_3_, f32[8,1024]{1,0:T(8,128)} %get-tuple-element.81.refs_4_, ...), custom_call_target="tpu_custom_call" | custom-call | flops 16777216 | bytes 9437184 | tf_op jit(solution)/shard_map/join_levels/pallas_call | solution.py:549
  (1 shorter events, 0.0 us)
Async XLA Ops:
  5.0 7.4 %collective-permute-start.2 = (f32[8,4,128]{2,1,0:T(4,128)S(1)}, f32[8,4,128]{2,1,0:T(4,128)S(1)}, u32[]{:S(2)}, u32[]{:S(2)}) collective-permute-start(f32[8,4,128]{2,1,0:T(4,128)S(1)} %get-tuple-element.50), channel_id=1, source_target_pairs={{0,96},{16,112},{32,64},{48,80},{64,32},{80,48},{96,0},{112,16},{1... | collective-permute-start | bytes 49160 | tf_op jit(solution)/shard_map/ppermute | solution.py:573
  7.9 5.2 %collective-permute-start.1 = (f32[8,4,128]{2,1,0:T(4,128)S(1)}, f32[8,4,128]{2,1,0:T(4,128)S(1)}, u32[]{:S(2)}, u32[]{:S(2)}) collective-permute-start(f32[8,4,128]{2,1,0:T(4,128)S(1)} %get-tuple-element.50), channel_id=1, source_target_pairs={{0,64},{16,80},{32,96},{48,112},{64,0},{80,16},{96,32},{112,48},{1... | collective-permute-start | bytes 49160 | tf_op jit(solution)/shard_map/ppermute | solution.py:573
  8.7 4.4 %collective-permute-start = (f32[8,8,128]{2,1,0:T(8,128)S(1)}, f32[8,8,128]{2,1,0:T(8,128)S(1)}, u32[]{:S(2)}, u32[]{:S(2)}) collective-permute-start(f32[8,8,128]{2,1,0:T(8,128)S(1)} %get-tuple-element.49), channel_id=1, source_target_pairs={{0,32},{16,48},{32,0},{48,16},{64,96},{80,112},{96,64},{112,80},{1... | collective-permute-start | bytes 98312 | tf_op jit(solution)/shard_map/ppermute | solution.py:573
  13.8 18.9 %all-to-all-start = ((f32[8,208,128]{2,1,0:T(8,128)}), f32[8,208,128]{2,1,0:T(8,128)S(1)}, u32[]{:S(2)}, u32[]{:S(2)}) async-start(f32[8,208,128]{2,1,0:T(8,128)} %pack_rows.1), calls=%async_computation | async-start | bytes 1703936 | tf_op jit(solution)/shard_map/all_to_all | solution.py:577
  20.2 30.5 %collective-permute-start.6 = (f32[128,1024]{1,0:T(8,128)}, f32[128,1024]{1,0:T(8,128)S(1)}, u32[]{:S(2)}, u32[]{:S(2)}) collective-permute-start(f32[128,1024]{1,0:T(8,128)} %get-tuple-element.75), channel_id=1, source_target_pairs={{0,1},{1,0},{2,3},{3,2},{4,5},{5,4},{6,7},{7,6},{8,9},{9,8},{10,11... | collective-permute-start | bytes 1572872 | tf_op jit(solution)/shard_map/ppermute | solution.py:573
  32.8 21.9 %collective-permute-start.7 = (f32[128,1024]{1,0:T(8,128)}, f32[128,1024]{1,0:T(8,128)}, u32[]{:S(2)}, u32[]{:S(2)}) collective-permute-start(f32[128,1024]{1,0:T(8,128)} %get-tuple-element.86), channel_id=1, source_target_pairs={{0,1},{1,0},{2,3},{3,2},{4,5},{5,4},{6,7},{7,6},{8,9},{9,8},{10,11... | collective-permute-start | bytes 1572872 | tf_op jit(solution)/shard_map/ppermute | solution.py:573
  33.5 2.4 %collective-permute-start.4 = (f32[2,128,128]{2,1,0:T(8,128)S(1)}, f32[2,128,128]{2,1,0:T(8,128)S(1)}, u32[]{:S(2)}, u32[]{:S(2)}) collective-permute-start(f32[2,128,128]{2,1,0:T(8,128)S(1)} %get-tuple-element.59), channel_id=1, source_target_pairs={{0,16},{16,0},{32,48},{48,32},{64,80},{80,64},{96,112},{112,96},{1... | collective-permute-start | bytes 393224 | tf_op jit(solution)/shard_map/ppermute | solution.py:573
  33.6 10.7 %collective-permute-start.3 = (f32[2,192,128]{2,1,0:T(8,128)S(1)}, f32[2,192,128]{2,1,0:T(8,128)S(1)}, u32[]{:S(2)}, u32[]{:S(2)}) collective-permute-start(f32[2,192,128]{2,1,0:T(8,128)S(1)} %get-tuple-element.58.here_ref), channel_id=1, source_target_pairs={{0,12},{1,13},{2,14},{3,15},{4,8},{5,9},{6,10},{7,11},{8,4},{9,5},... | collective-permute-start | bytes 589832 | tf_op jit(solution)/shard_map/ppermute | solution.py:573
  35.8 9.1 %collective-permute-start.5 = (f32[2,128,128]{2,1,0:T(8,128)S(1)}, f32[2,128,128]{2,1,0:T(8,128)S(1)}, u32[]{:S(2)}, u32[]{:S(2)}) collective-permute-start(f32[2,128,128]{2,1,0:T(8,128)S(1)} %collective-permute-done.4.core_ref), channel_id=1, source_target_pairs={{0,12},{1,13},{2,14},{3,15},{4,8},{5,9},{6,10},{7,11},{8,4},{9,5},... | collective-permute-start | bytes 393224 | tf_op jit(solution)/shard_map/ppermute | solution.py:573
  46.4 11.6 %all-to-all-start.1 = ((f32[8,72,128]{2,1,0:T(8,128)}), f32[8,72,128]{2,1,0:T(8,128)S(1)}, u32[]{:S(2)}, u32[]{:S(2)}) async-start(f32[8,72,128]{2,1,0:T(8,128)} %far_levels.1), calls=%async_computation.1 | async-start | bytes 589824 | tf_op jit(solution)/shard_map/all_to_all | solution.py:577
  50.7 7.4 %copy-start = (f32[1024,640]{1,0:T(8,128)S(1)}, f32[1024,640]{1,0:T(8,128)}, u32[]{:S(2)}) copy-start(f32[1024,640]{1,0:T(8,128)} %get-tuple-element.56.refs_0_) | copy-start | bytes 7864324
